TPU v7x, 512 devices: a whole 4x8x8 slice. The times are simulated.
512 devices in a mesh: lat: 16 (over z_hi, x, core), lon: 32 (over z_lo, y).
Axes of the slice: x: 4, y: 8, z: 8 (z_hi: 2, z_lo: 4; z = z_hi * 4 + z_lo), core: 2. Of those that a mesh axis runs over, the one named last changes fastest.
Arguments:
- warm_start: float32 [32, 512, 2048], P(None, 'lon', 'lat'), may hold values from -2 to 2
- probe_signs: int32 [32, 512, 2048], P(None, 'lon', 'lat'), may hold values from 0 to 1
- ocean_mask: int32 [512, 2048], P('lon', 'lat'), may hold values 0 or 1
- kappa_sq: float32 [512, 2048], P('lon', 'lat'), may hold values from 0.02 to 2
- scale_field: float32 [512, 2048], P('lon', 'lat'), may hold values from 0.03 to 0.3
Outputs:
- solution: float32 [32, 512, 2048], P(None, 'lon', 'lat')
- residual: float32 [32, 512, 2048], P(None, 'lon', 'lat')
- kappa_grad: float32 [512, 2048], P('lon', 'lat')
Inputs may be any that keep to these rules, and one draw needn't show every extreme that they name: `probe_signs`: 1 stands for a sign of +1 and 0 for -1. `ocean_mask`: 1 marks an ocean cell, 0 a land cell.
All inputs are finite; a program needn't handle non-finite values. No bound on the sum of `ocean_mask` on one device may be relied on, other than what follows from the above.
Results may differ from a plain program's by a relative error of at most 0.0003.
Values sent between devices are 32-bit elements; how exact they have to be, the bound alone decides.
No kernel may reach another device: no remote copies, remote signals or barrier semaphores. Data moves between devices by JAX's collectives and lax.ppermute only.
A program may use at most 64 MiB of HBM per device.

v0:
```python
import jax
import jax.numpy as jnp
from jax import lax
from jax.sharding import PartitionSpec as P

ITERS = 3


top_precision = lax.Precision.HIGHEST


def with_halo(array, sides, width, wrap):
    for axis, dim in sides:
        size, length = (lax.axis_size(axis), array.shape[dim])
        up = [(i, (i + 1) % size) for i in range(size if wrap else size - 1)]
        down = [(j, i) for i, j in up]
        last = lax.slice_in_dim(array, length - width, length, axis=dim)
        first = lax.slice_in_dim(array, 0, width, axis=dim)
        before = lax.ppermute(last, axis, up)
        after = lax.ppermute(first, axis, down)
        array = jnp.concatenate([before, array, after], axis=dim)
    return array


def halo_k(values, wet_cells, diag_term):
    masked = values * wet_cells
    edges = jnp.concatenate([masked[:, :1, :], masked[:, -1:, :]], axis=1)
    arrived = with_halo(edges, (("lon", 1),), 1, True)
    wide = jnp.concatenate([arrived[:, :1, :], masked, arrived[:, -1:, :]], axis=1)
    tall = with_halo(masked, (("lat", 2),), 1, False)
    beside = wide[:, :-2, :] + wide[:, 2:, :]
    beside = beside + tall[:, :, 2:] + tall[:, :, :-2]
    return wet_cells * (diag_term * masked - beside)


def shallow_q(values, wet_cells, diag_term, scale_field):
    inner = scale_field * halo_k(values, wet_cells, diag_term)
    return halo_k(inner, wet_cells, diag_term) + (1.0 - wet_cells) * values


def gram(left, right):
    return jnp.einsum("pij,qij->pq", left, right, precision=top_precision)


def combine(base, block, coeffs):
    return base + jnp.einsum("pij,pq->qij", block, coeffs, precision=top_precision)


def solve_spd(matrix, rhs_block):
    factor = jnp.linalg.cholesky(matrix)
    return jax.scipy.linalg.cho_solve((factor, True), rhs_block)


def residual_sum(block):
    return lax.psum(gram(block, block), ("lat", "lon"))


def curvature_sum(block, image):
    return lax.psum(gram(block, image), ("lat", "lon"))


def local(warm_start, probe_signs, ocean_mask, kappa_sq, scale_field):
    wet_cells = ocean_mask.astype(jnp.float32)
    diag_term = kappa_sq + 4.0
    probes = 2.0 * probe_signs.astype(jnp.float32) - 1.0

    def apply_q(values):
        return shallow_q(values, wet_cells, diag_term, scale_field)

    solution = warm_start
    residual = probes - apply_q(solution)
    direction = residual
    norms = residual_sum(residual)
    for iteration in range(ITERS):
        image = apply_q(direction)
        curvature = curvature_sum(direction, image)
        alpha = solve_spd(curvature, norms)
        solution = combine(solution, direction, alpha)
        residual = combine(residual, image, -alpha)
        if iteration + 1 < ITERS:
            fresh = residual_sum(residual)
            beta = solve_spd(norms, fresh)
            direction = combine(residual, direction, beta)
            norms = fresh
    count = probes.shape[0]
    stacked = halo_k(jnp.concatenate([solution, probes], axis=0), wet_cells, diag_term)
    k_solution = stacked[:count]
    k_probes = stacked[count:]
    terms = solution * (scale_field * k_probes) + k_solution * (scale_field * probes)
    kappa_grad = wet_cells * jnp.mean(terms, axis=0)
    return (solution, residual, kappa_grad)


def solution(mesh):
    return jax.shard_map(
        local,
        mesh=mesh,
        in_specs=(
            P(None, "lon", "lat"),
            P(None, "lon", "lat"),
            P("lon", "lat"),
            P("lon", "lat"),
            P("lon", "lat"),
        ),
        out_specs=(P(None, "lon", "lat"), P(None, "lon", "lat"), P("lon", "lat")),
        check_vma=False,
    )
```

profile of v0, /device:TPU:71, one launch (start us, length us, event | category | flops | bytes accessed | tf_op | source)
XLA Modules:
  0.0 739.5 jit_solution(16226930706342658353)
XLA Ops:
  1.3 1.0 copy_multiply_fusion
  2.5 10.2 %collective-permute-start.3 = (f32[32,16,1]{2,0,1:T(8,128)S(1)}, f32[32,16,1]{2,0,1:T(8,128)S(1)}, u32[]{:S(2)}, u32[]{:S(2)}) collective-permute-start(f32[32,16,1]{2,0,1:T(8,128)S(1)} %get-tuple-element.48), channel_id=1, source_target_pairs={{0,32},{32,64},{64,96},{96,128},{128,160},{160,192},{192,224},{224... | collective-permute-start | bytes 6152 | tf_op jit(solution)/shard_map/ppermute | solution.py:19
  12.7 1.9 collective-permute-start.2
  14.7 5.1 collective-permute-start.1
  19.8 1.9 collective-permute-start
  21.7 7.5 %collective-permute-done.2 = f32[32,16,1]{2,0,1:T(8,128)S(1)} collective-permute-done((f32[32,16,1]{2,0,1:T(8,128)S(1)}, f32[32,16,1]{2,0,1:T(8,128)S(1)}, u32[]{:S(2)}, u32[]{:S(2)}) %collective-permute-start.2) | collective-permute-done | bytes 2080 | tf_op jit(solution)/shard_map/ppermute | solution.py:20
  29.7 8.2 %collective-permute-start.7 = (f32[32,16,1]{2,0,1:T(8,128)S(1)}, f32[32,16,1]{2,0,1:T(8,128)S(1)}, u32[]{:S(2)}, u32[]{:S(2)}) collective-permute-start(f32[32,16,1]{2,0,1:T(8,128)S(1)} %get-tuple-element.44), channel_id=1, source_target_pairs={{0,32},{32,64},{64,96},{96,128},{128,160},{160,192},{192,224},{224... | collective-permute-start | bytes 6152 | tf_op jit(solution)/shard_map/ppermute | solution.py:19
  38.0 1.9 collective-permute-start.6
  39.9 1.9 collective-permute-start.5
  41.8 3.4 collective-permute-start.4
  45.2 9.4 %collective-permute-done.6 = f32[32,16,1]{2,0,1:T(8,128)S(1)} collective-permute-done((f32[32,16,1]{2,0,1:T(8,128)S(1)}, f32[32,16,1]{2,0,1:T(8,128)S(1)}, u32[]{:S(2)}, u32[]{:S(2)}) %collective-permute-start.6) | collective-permute-done | bytes 2080 | tf_op jit(solution)/shard_map/ppermute | solution.py:20
  55.1 1.9 collective-permute-start.9
  57.0 3.4 collective-permute-start.8
  60.5 5.1 collective-permute-start.11
  65.6 1.9 collective-permute-start.10
  67.5 4.2 collective-permute-done.11
  71.7 10.4 %collective-permute-done.10 = f32[32,16,1]{2,0,1:T(8,128)S(1)} collective-permute-done((f32[32,16,1]{2,0,1:T(8,128)S(1)}, f32[32,16,1]{2,0,1:T(8,128)S(1)}, u32[]{:S(2)}, u32[]{:S(2)}) %collective-permute-start.10) | collective-permute-done | bytes 2080 | tf_op jit(solution)/shard_map/ppermute | solution.py:20
  82.6 1.9 collective-permute-start.15
  84.5 2.4 collective-permute-start.14
  86.9 1.9 collective-permute-start.13
  88.8 3.4 collective-permute-start.12
  92.6 7.5 %collective-permute-done.14 = f32[32,16,1]{2,0,1:T(8,128)S(1)} collective-permute-done((f32[32,16,1]{2,0,1:T(8,128)S(1)}, f32[32,16,1]{2,0,1:T(8,128)S(1)}, u32[]{:S(2)}, u32[]{:S(2)}) %collective-permute-start.14) | collective-permute-done | bytes 2080 | tf_op jit(solution)/shard_map/ppermute | solution.py:20
  100.7 100.9 %all-reduce = (f32[32,32]{0,1:T(8,128)S(1)}, f32[32,32]{0,1:T(8,128)S(1)}) all-reduce(f32[32,32]{0,1:T(8,128)S(1)} %convolution_bitcast_fusion.6, f32[32,32]{0,1:T(8,128)S(1)} %convolution_bitcast_fusion.7), channel_id=1, replica_groups=mesh['lat'=16,'lon'=32] {'lat','lon'}, use_global_device_ids=true, to_apply=%region_3.5 | all-reduce | flops 2048 | bytes 16384 | tf_op jit(solution)/shard_map/psum | solution.py:55
  201.8 2.9 cholesky.89
  206.0 2.4 custom-call.11
  209.9 94.5 %psum.44 = f32[32,32]{0,1:T(8,128)S(1)} all-reduce(f32[32,32]{0,1:T(8,128)S(1)} %convolution_bitcast_fusion.5), channel_id=1, replica_groups=mesh['lat'=16,'lon'=32] {'lat','lon'}, use_global_device_ids=true, to_apply=%region_4.0 | all-reduce | flops 1024 | bytes 8192 | tf_op jit(solution)/shard_map/psum | solution.py:55
  304.4 2.9 cholesky.100
  308.7 2.4 custom-call.12
  312.1 7.3 collective-permute-start.19
  319.5 1.9 collective-permute-start.18
  321.4 4.3 collective-permute-start.17
  325.7 1.9 collective-permute-start.16
  327.7 2.9 cholesky.122
  331.2 4.6 collective-permute-done.18
  336.3 7.5 %collective-permute-start.23 = (f32[32,16,1]{2,0,1:T(8,128)S(1)}, f32[32,16,1]{2,0,1:T(8,128)S(1)}, u32[]{:S(2)}, u32[]{:S(2)}) collective-permute-start(f32[32,16,1]{2,0,1:T(8,128)S(1)} %get-tuple-element.28), channel_id=1, source_target_pairs={{0,32},{32,64},{64,96},{96,128},{128,160},{160,192},{192,224},{224... | collective-permute-start | bytes 6152 | tf_op jit(solution)/shard_map/ppermute | solution.py:19
  343.8 1.9 collective-permute-start.22
  345.8 3.6 collective-permute-start.21
  349.3 1.9 collective-permute-start.20
  351.9 2.4 custom-call.14
  354.4 5.9 collective-permute-done.22
  360.9 95.0 %psum.45 = f32[32,32]{0,1:T(8,128)S(1)} all-reduce(f32[32,32]{0,1:T(8,128)S(1)} %convolution_bitcast_fusion.4), channel_id=1, replica_groups=mesh['lat'=16,'lon'=32] {'lat','lon'}, use_global_device_ids=true, to_apply=%region_5.0 | all-reduce | flops 1024 | bytes 8192 | tf_op jit(solution)/shard_map/psum | solution.py:59
  456.0 2.9 cholesky.111
  460.2 2.4 custom-call.13
  463.9 94.5 %psum.46 = f32[32,32]{1,0:T(8,128)S(1)} all-reduce(f32[32,32]{1,0:T(8,128)S(1)} %convolution_bitcast_fusion.3), channel_id=1, replica_groups=mesh['lat'=16,'lon'=32] {'lat','lon'}, use_global_device_ids=true, to_apply=%region_6.0 | all-reduce | flops 1024 | bytes 8192 | tf_op jit(solution)/shard_map/psum | solution.py:55
  559.3 7.3 collective-permute-start.27
  566.7 1.9 collective-permute-start.26
  568.6 4.3 collective-permute-start.25
  572.9 1.9 collective-permute-start.24
  575.3 8.0 %collective-permute-done.26 = f32[32,16,1]{2,0,1:T(8,128)S(1)} collective-permute-done((f32[32,16,1]{2,0,1:T(8,128)S(1)}, f32[32,16,1]{2,0,1:T(8,128)S(1)}, u32[]{:S(2)}, u32[]{:S(2)}) %collective-permute-start.26) | collective-permute-done | bytes 2080 | tf_op jit(solution)/shard_map/ppermute | solution.py:20
  583.7 7.3 collective-permute-start.31
  591.0 1.9 collective-permute-start.30
  593.0 1.9 collective-permute-start.29
  594.9 3.4 collective-permute-start.28
  598.7 8.7 %collective-permute-done.30 = f32[32,16,1]{2,0,1:T(8,128)S(1)} collective-permute-done((f32[32,16,1]{2,0,1:T(8,128)S(1)}, f32[32,16,1]{2,0,1:T(8,128)S(1)}, u32[]{:S(2)}, u32[]{:S(2)}) %collective-permute-start.30) | collective-permute-done | bytes 2080 | tf_op jit(solution)/shard_map/ppermute | solution.py:20
  608.1 92.9 %psum.47 = f32[32,32]{0,1:T(8,128)S(1)} all-reduce(f32[32,32]{0,1:T(8,128)S(1)} %convolution_bitcast_fusion.2), channel_id=1, replica_groups=mesh['lat'=16,'lon'=32] {'lat','lon'}, use_global_device_ids=true, to_apply=%region_7.10 | all-reduce | flops 1024 | bytes 8192 | tf_op jit(solution)/shard_map/psum | solution.py:59
  701.1 2.9 cholesky.133
  705.3 2.4 custom-call.15
  708.8 6.5 collective-permute-start.35
  715.3 1.9 collective-permute-start.34
  717.2 4.3 collective-permute-start.33
  721.5 1.9 collective-permute-start.32
  723.9 0.9 copy.28
  725.6 1.8 collective-permute-done.35
  727.4 10.8 %collective-permute-done.34 = f32[64,16,1]{2,0,1:T(8,128)S(1)} collective-permute-done((f32[64,16,1]{2,0,1:T(8,128)S(1)}, f32[64,16,1]{2,0,1:T(8,128)S(1)}, u32[]{:S(2)}, u32[]{:S(2)}) %collective-permute-start.34) | collective-permute-done | bytes 4128 | tf_op jit(solution)/shard_map/ppermute | solution.py:20
  (116 shorter events, 21.2 us)
Async XLA Ops:
  2.5 19.2 %collective-permute-start.3 = (f32[32,16,1]{2,0,1:T(8,128)S(1)}, f32[32,16,1]{2,0,1:T(8,128)S(1)}, u32[]{:S(2)}, u32[]{:S(2)}) collective-permute-start(f32[32,16,1]{2,0,1:T(8,128)S(1)} %get-tuple-element.48), channel_id=1, source_target_pairs={{0,32},{32,64},{64,96},{96,128},{128,160},{160,192},{192,224},{224... | collective-permute-start | bytes 6152 | tf_op jit(solution)/shard_map/ppermute | solution.py:19
  12.7 16.5 %collective-permute-start.2 = (f32[32,16,1]{2,0,1:T(8,128)S(1)}, f32[32,16,1]{2,0,1:T(8,128)S(1)}, u32[]{:S(2)}, u32[]{:S(2)}) collective-permute-start(f32[32,16,1]{2,0,1:T(8,128)S(1)} %get-tuple-element.47), channel_id=1, source_target_pairs={{32,0},{64,32},{96,64},{128,96},{160,128},{192,160},{224,192},{256... | collective-permute-start | bytes 6152 | tf_op jit(solution)/shard_map/ppermute | solution.py:20
  14.7 7.1 copy-start.4
  14.7 14.6 %collective-permute-start.1 = (f32[32,1,128]{2,0,1:T(8,128)S(1)}, f32[32,1,128]{2,0,1:T(8,128)S(1)}, u32[]{:S(2)}, u32[]{:S(2)}) collective-permute-start(f32[32,1,128]{2,0,1:T(8,128)S(1)} %get-tuple-element.46), channel_id=1, source_target_pairs={{1,0},{2,1},{3,2},{4,3},{5,4},{6,5},{7,6},{8,7},{9,8},{10,9},{11,1... | collective-permute-start | bytes 49160 | tf_op jit(solution)/shard_map/ppermute | solution.py:20
  19.8 9.5 %copy-start.2 = (f32[16,128]{1,0:T(8,128)S(1)}, f32[16,128]{1,0:T(8,128)}, u32[]{:S(2)}) copy-start(f32[16,128]{1,0:T(8,128)} %param.12) | copy-start | bytes 24580
  19.8 9.5 %collective-permute-start = (f32[32,1,128]{2,0,1:T(8,128)S(1)}, f32[32,1,128]{2,0,1:T(8,128)S(1)}, u32[]{:S(2)}, u32[]{:S(2)}) collective-permute-start(f32[32,1,128]{2,0,1:T(8,128)S(1)} %get-tuple-element.45), channel_id=1, source_target_pairs={{0,1},{1,2},{2,3},{3,4},{4,5},{5,6},{6,7},{7,8},{8,9},{9,10},{10,1... | collective-permute-start | bytes 49160 | tf_op jit(solution)/shard_map/ppermute | solution.py:19
  29.5 25.1 %copy-start = (f32[32,16,128]{2,1,0:T(8,128)S(1)}, f32[32,16,128]{2,1,0:T(8,128)}, u32[]{:S(2)}) copy-start(f32[32,16,128]{2,1,0:T(8,128)} %param.8) | copy-start | bytes 786436
  29.6 25.1 %copy-start.1 = (s32[32,16,128]{2,1,0:T(8,128)S(1)}, s32[32,16,128]{2,1,0:T(8,128)}, u32[]{:S(2)}) copy-start(s32[32,16,128]{2,1,0:T(8,128)} %param.9) | copy-start | bytes 786436
  29.7 15.5 %copy-start.3 = (s32[16,128]{1,0:T(8,128)S(1)}, s32[16,128]{1,0:T(8,128)}, u32[]{:S(2)}) copy-start(s32[16,128]{1,0:T(8,128)} %param.10) | copy-start | bytes 24580
  29.7 15.5 %collective-permute-start.7 = (f32[32,16,1]{2,0,1:T(8,128)S(1)}, f32[32,16,1]{2,0,1:T(8,128)S(1)}, u32[]{:S(2)}, u32[]{:S(2)}) collective-permute-start(f32[32,16,1]{2,0,1:T(8,128)S(1)} %get-tuple-element.44), channel_id=1, source_target_pairs={{0,32},{32,64},{64,96},{96,128},{128,160},{160,192},{192,224},{224... | collective-permute-start | bytes 6152 | tf_op jit(solution)/shard_map/ppermute | solution.py:19
  38.0 16.7 %collective-permute-start.6 = (f32[32,16,1]{2,0,1:T(8,128)S(1)}, f32[32,16,1]{2,0,1:T(8,128)S(1)}, u32[]{:S(2)}, u32[]{:S(2)}) collective-permute-start(f32[32,16,1]{2,0,1:T(8,128)S(1)} %get-tuple-element.43), channel_id=1, source_target_pairs={{32,0},{64,32},{96,64},{128,96},{160,128},{192,160},{224,192},{256... | collective-permute-start | bytes 6152 | tf_op jit(solution)/shard_map/ppermute | solution.py:20
  39.9 14.8 %collective-permute-start.5 = (f32[32,1,128]{2,0,1:T(8,128)S(1)}, f32[32,1,128]{2,0,1:T(8,128)S(1)}, u32[]{:S(2)}, u32[]{:S(2)}) collective-permute-start(f32[32,1,128]{2,0,1:T(8,128)S(1)} %get-tuple-element.42), channel_id=1, source_target_pairs={{1,0},{2,1},{3,2},{4,3},{5,4},{6,5},{7,6},{8,7},{9,8},{10,9},{11,1... | collective-permute-start | bytes 49160 | tf_op jit(solution)/shard_map/ppermute | solution.py:20
  41.8 12.8 %collective-permute-start.4 = (f32[32,1,128]{2,0,1:T(8,128)S(1)}, f32[32,1,128]{2,0,1:T(8,128)S(1)}, u32[]{:S(2)}, u32[]{:S(2)}) collective-permute-start(f32[32,1,128]{2,0,1:T(8,128)S(1)} %get-tuple-element.41), channel_id=1, source_target_pairs={{0,1},{1,2},{2,3},{3,4},{4,5},{5,6},{6,7},{7,8},{8,9},{9,10},{10,1... | collective-permute-start | bytes 49160 | tf_op jit(solution)/shard_map/ppermute | solution.py:19
  55.1 27.1 %collective-permute-start.9 = (f32[32,1,128]{2,0,1:T(8,128)S(1)}, f32[32,1,128]{2,0,1:T(8,128)S(1)}, u32[]{:S(2)}, u32[]{:S(2)}) collective-permute-start(f32[32,1,128]{2,0,1:T(8,128)S(1)} %get-tuple-element.38), channel_id=1, source_target_pairs={{1,0},{2,1},{3,2},{4,3},{5,4},{6,5},{7,6},{8,7},{9,8},{10,9},{11,1... | collective-permute-start | bytes 49160 | tf_op jit(solution)/shard_map/ppermute | solution.py:20
  57.0 25.1 %collective-permute-start.8 = (f32[32,1,128]{2,0,1:T(8,128)S(1)}, f32[32,1,128]{2,0,1:T(8,128)S(1)}, u32[]{:S(2)}, u32[]{:S(2)}) collective-permute-start(f32[32,1,128]{2,0,1:T(8,128)S(1)} %get-tuple-element.37), channel_id=1, source_target_pairs={{0,1},{1,2},{2,3},{3,4},{4,5},{5,6},{6,7},{7,8},{8,9},{9,10},{10,1... | collective-permute-start | bytes 49160 | tf_op jit(solution)/shard_map/ppermute | solution.py:19
  60.5 11.2 %collective-permute-start.11 = (f32[32,16,1]{2,0,1:T(8,128)S(1)}, f32[32,16,1]{2,0,1:T(8,128)S(1)}, u32[]{:S(2)}, u32[]{:S(2)}) collective-permute-start(f32[32,16,1]{2,0,1:T(8,128)S(1)} %get-tuple-element.40), channel_id=1, source_target_pairs={{0,32},{32,64},{64,96},{96,128},{128,160},{160,192},{192,224},{224... | collective-permute-start | bytes 6152 | tf_op jit(solution)/shard_map/ppermute | solution.py:19
  65.6 16.5 %collective-permute-start.10 = (f32[32,16,1]{2,0,1:T(8,128)S(1)}, f32[32,16,1]{2,0,1:T(8,128)S(1)}, u32[]{:S(2)}, u32[]{:S(2)}) collective-permute-start(f32[32,16,1]{2,0,1:T(8,128)S(1)} %get-tuple-element.39), channel_id=1, source_target_pairs={{32,0},{64,32},{96,64},{128,96},{160,128},{192,160},{224,192},{256... | collective-permute-start | bytes 6152 | tf_op jit(solution)/shard_map/ppermute | solution.py:20
  82.6 10.0 %collective-permute-start.15 = (f32[32,16,1]{2,0,1:T(8,128)S(1)}, f32[32,16,1]{2,0,1:T(8,128)S(1)}, u32[]{:S(2)}, u32[]{:S(2)}) collective-permute-start(f32[32,16,1]{2,0,1:T(8,128)S(1)} %get-tuple-element.36), channel_id=1, source_target_pairs={{0,32},{32,64},{64,96},{96,128},{128,160},{160,192},{192,224},{224... | collective-permute-start | bytes 6152 | tf_op jit(solution)/shard_map/ppermute | solution.py:19
  84.5 15.6 %collective-permute-start.14 = (f32[32,16,1]{2,0,1:T(8,128)S(1)}, f32[32,16,1]{2,0,1:T(8,128)S(1)}, u32[]{:S(2)}, u32[]{:S(2)}) collective-permute-start(f32[32,16,1]{2,0,1:T(8,128)S(1)} %get-tuple-element.35), channel_id=1, source_target_pairs={{32,0},{64,32},{96,64},{128,96},{160,128},{192,160},{224,192},{256... | collective-permute-start | bytes 6152 | tf_op jit(solution)/shard_map/ppermute | solution.py:20
  86.9 13.2 %collective-permute-start.13 = (f32[32,1,128]{2,0,1:T(8,128)S(1)}, f32[32,1,128]{2,0,1:T(8,128)S(1)}, u32[]{:S(2)}, u32[]{:S(2)}) collective-permute-start(f32[32,1,128]{2,0,1:T(8,128)S(1)} %get-tuple-element.34), channel_id=1, source_target_pairs={{1,0},{2,1},{3,2},{4,3},{5,4},{6,5},{7,6},{8,7},{9,8},{10,9},{11,1... | collective-permute-start | bytes 49160 | tf_op jit(solution)/shard_map/ppermute | solution.py:20
  88.8 11.3 %collective-permute-start.12 = (f32[32,1,128]{2,0,1:T(8,128)S(1)}, f32[32,1,128]{2,0,1:T(8,128)S(1)}, u32[]{:S(2)}, u32[]{:S(2)}) collective-permute-start(f32[32,1,128]{2,0,1:T(8,128)S(1)} %get-tuple-element.33), channel_id=1, source_target_pairs={{0,1},{1,2},{2,3},{3,4},{4,5},{5,6},{6,7},{7,8},{8,9},{9,10},{10,1... | collective-permute-start | bytes 49160 | tf_op jit(solution)/shard_map/ppermute | solution.py:19
  312.1 19.1 %collective-permute-start.19 = (f32[32,16,1]{2,0,1:T(8,128)S(1)}, f32[32,16,1]{2,0,1:T(8,128)S(1)}, u32[]{:S(2)}, u32[]{:S(2)}) collective-permute-start(f32[32,16,1]{2,0,1:T(8,128)S(1)} %get-tuple-element.32), channel_id=1, source_target_pairs={{0,32},{32,64},{64,96},{96,128},{128,160},{160,192},{192,224},{224... | collective-permute-start | bytes 6152 | tf_op jit(solution)/shard_map/ppermute | solution.py:19
  319.5 16.4 %collective-permute-start.18 = (f32[32,16,1]{2,0,1:T(8,128)S(1)}, f32[32,16,1]{2,0,1:T(8,128)S(1)}, u32[]{:S(2)}, u32[]{:S(2)}) collective-permute-start(f32[32,16,1]{2,0,1:T(8,128)S(1)} %get-tuple-element.31), channel_id=1, source_target_pairs={{32,0},{64,32},{96,64},{128,96},{160,128},{192,160},{224,192},{256... | collective-permute-start | bytes 6152 | tf_op jit(solution)/shard_map/ppermute | solution.py:20
  321.4 14.5 %collective-permute-start.17 = (f32[32,1,128]{2,0,1:T(8,128)S(1)}, f32[32,1,128]{2,0,1:T(8,128)S(1)}, u32[]{:S(2)}, u32[]{:S(2)}) collective-permute-start(f32[32,1,128]{2,0,1:T(8,128)S(1)} %get-tuple-element.30), channel_id=1, source_target_pairs={{1,0},{2,1},{3,2},{4,3},{5,4},{6,5},{7,6},{8,7},{9,8},{10,9},{11,1... | collective-permute-start | bytes 49160 | tf_op jit(solution)/shard_map/ppermute | solution.py:20
  325.7 10.2 %collective-permute-start.16 = (f32[32,1,128]{2,0,1:T(8,128)S(1)}, f32[32,1,128]{2,0,1:T(8,128)S(1)}, u32[]{:S(2)}, u32[]{:S(2)}) collective-permute-start(f32[32,1,128]{2,0,1:T(8,128)S(1)} %get-tuple-element.29), channel_id=1, source_target_pairs={{0,1},{1,2},{2,3},{3,4},{4,5},{5,6},{6,7},{7,8},{8,9},{9,10},{10,1... | collective-permute-start | bytes 49160 | tf_op jit(solution)/shard_map/ppermute | solution.py:19
  336.3 18.1 %collective-permute-start.23 = (f32[32,16,1]{2,0,1:T(8,128)S(1)}, f32[32,16,1]{2,0,1:T(8,128)S(1)}, u32[]{:S(2)}, u32[]{:S(2)}) collective-permute-start(f32[32,16,1]{2,0,1:T(8,128)S(1)} %get-tuple-element.28), channel_id=1, source_target_pairs={{0,32},{32,64},{64,96},{96,128},{128,160},{160,192},{192,224},{224... | collective-permute-start | bytes 6152 | tf_op jit(solution)/shard_map/ppermute | solution.py:19
  343.8 16.4 %collective-permute-start.22 = (f32[32,16,1]{2,0,1:T(8,128)S(1)}, f32[32,16,1]{2,0,1:T(8,128)S(1)}, u32[]{:S(2)}, u32[]{:S(2)}) collective-permute-start(f32[32,16,1]{2,0,1:T(8,128)S(1)} %get-tuple-element.27), channel_id=1, source_target_pairs={{32,0},{64,32},{96,64},{128,96},{160,128},{192,160},{224,192},{256... | collective-permute-start | bytes 6152 | tf_op jit(solution)/shard_map/ppermute | solution.py:20
  345.8 14.5 %collective-permute-start.21 = (f32[32,1,128]{2,0,1:T(8,128)S(1)}, f32[32,1,128]{2,0,1:T(8,128)S(1)}, u32[]{:S(2)}, u32[]{:S(2)}) collective-permute-start(f32[32,1,128]{2,0,1:T(8,128)S(1)} %get-tuple-element.26), channel_id=1, source_target_pairs={{1,0},{2,1},{3,2},{4,3},{5,4},{6,5},{7,6},{8,7},{9,8},{10,9},{11,1... | collective-permute-start | bytes 49160 | tf_op jit(solution)/shard_map/ppermute | solution.py:20
  349.3 10.9 %collective-permute-start.20 = (f32[32,1,128]{2,0,1:T(8,128)S(1)}, f32[32,1,128]{2,0,1:T(8,128)S(1)}, u32[]{:S(2)}, u32[]{:S(2)}) collective-permute-start(f32[32,1,128]{2,0,1:T(8,128)S(1)} %get-tuple-element.25), channel_id=1, source_target_pairs={{0,1},{1,2},{2,3},{3,4},{4,5},{5,6},{6,7},{7,8},{8,9},{9,10},{10,1... | collective-permute-start | bytes 49160 | tf_op jit(solution)/shard_map/ppermute | solution.py:19
  559.3 16.0 %collective-permute-start.27 = (f32[32,16,1]{2,0,1:T(8,128)S(1)}, f32[32,16,1]{2,0,1:T(8,128)S(1)}, u32[]{:S(2)}, u32[]{:S(2)}) collective-permute-start(f32[32,16,1]{2,0,1:T(8,128)S(1)} %get-tuple-element.24), channel_id=1, source_target_pairs={{0,32},{32,64},{64,96},{96,128},{128,160},{160,192},{192,224},{224... | collective-permute-start | bytes 6152 | tf_op jit(solution)/shard_map/ppermute | solution.py:19
  566.7 16.6 %collective-permute-start.26 = (f32[32,16,1]{2,0,1:T(8,128)S(1)}, f32[32,16,1]{2,0,1:T(8,128)S(1)}, u32[]{:S(2)}, u32[]{:S(2)}) collective-permute-start(f32[32,16,1]{2,0,1:T(8,128)S(1)} %get-tuple-element.23), channel_id=1, source_target_pairs={{32,0},{64,32},{96,64},{128,96},{160,128},{192,160},{224,192},{256... | collective-permute-start | bytes 6152 | tf_op jit(solution)/shard_map/ppermute | solution.py:20
  568.6 14.7 %collective-permute-start.25 = (f32[32,1,128]{2,0,1:T(8,128)S(1)}, f32[32,1,128]{2,0,1:T(8,128)S(1)}, u32[]{:S(2)}, u32[]{:S(2)}) collective-permute-start(f32[32,1,128]{2,0,1:T(8,128)S(1)} %get-tuple-element.22), channel_id=1, source_target_pairs={{1,0},{2,1},{3,2},{4,3},{5,4},{6,5},{7,6},{8,7},{9,8},{10,9},{11,1... | collective-permute-start | bytes 49160 | tf_op jit(solution)/shard_map/ppermute | solution.py:20
  572.9 10.4 %collective-permute-start.24 = (f32[32,1,128]{2,0,1:T(8,128)S(1)}, f32[32,1,128]{2,0,1:T(8,128)S(1)}, u32[]{:S(2)}, u32[]{:S(2)}) collective-permute-start(f32[32,1,128]{2,0,1:T(8,128)S(1)} %get-tuple-element.21), channel_id=1, source_target_pairs={{0,1},{1,2},{2,3},{3,4},{4,5},{5,6},{6,7},{7,8},{8,9},{9,10},{10,1... | collective-permute-start | bytes 49160 | tf_op jit(solution)/shard_map/ppermute | solution.py:19
  583.7 15.0 %collective-permute-start.31 = (f32[32,16,1]{2,0,1:T(8,128)S(1)}, f32[32,16,1]{2,0,1:T(8,128)S(1)}, u32[]{:S(2)}, u32[]{:S(2)}) collective-permute-start(f32[32,16,1]{2,0,1:T(8,128)S(1)} %get-tuple-element.20), channel_id=1, source_target_pairs={{0,32},{32,64},{64,96},{96,128},{128,160},{160,192},{192,224},{224... | collective-permute-start | bytes 6152 | tf_op jit(solution)/shard_map/ppermute | solution.py:19
  591.0 16.4 %collective-permute-start.30 = (f32[32,16,1]{2,0,1:T(8,128)S(1)}, f32[32,16,1]{2,0,1:T(8,128)S(1)}, u32[]{:S(2)}, u32[]{:S(2)}) collective-permute-start(f32[32,16,1]{2,0,1:T(8,128)S(1)} %get-tuple-element.19), channel_id=1, source_target_pairs={{32,0},{64,32},{96,64},{128,96},{160,128},{192,160},{224,192},{256... | collective-permute-start | bytes 6152 | tf_op jit(solution)/shard_map/ppermute | solution.py:20
  593.0 14.5 %collective-permute-start.29 = (f32[32,1,128]{2,0,1:T(8,128)S(1)}, f32[32,1,128]{2,0,1:T(8,128)S(1)}, u32[]{:S(2)}, u32[]{:S(2)}) collective-permute-start(f32[32,1,128]{2,0,1:T(8,128)S(1)} %get-tuple-element.18), channel_id=1, source_target_pairs={{1,0},{2,1},{3,2},{4,3},{5,4},{6,5},{7,6},{8,7},{9,8},{10,9},{11,1... | collective-permute-start | bytes 49160 | tf_op jit(solution)/shard_map/ppermute | solution.py:20
  594.9 12.5 %collective-permute-start.28 = (f32[32,1,128]{2,0,1:T(8,128)S(1)}, f32[32,1,128]{2,0,1:T(8,128)S(1)}, u32[]{:S(2)}, u32[]{:S(2)}) collective-permute-start(f32[32,1,128]{2,0,1:T(8,128)S(1)} %get-tuple-element.17), channel_id=1, source_target_pairs={{0,1},{1,2},{2,3},{3,4},{4,5},{5,6},{6,7},{7,8},{8,9},{9,10},{10,1... | collective-permute-start | bytes 49160 | tf_op jit(solution)/shard_map/ppermute | solution.py:19
  708.8 18.5 %collective-permute-start.35 = (f32[64,16,1]{2,0,1:T(8,128)S(1)}, f32[64,16,1]{2,0,1:T(8,128)S(1)}, u32[]{:S(2)}, u32[]{:S(2)}) collective-permute-start(f32[64,16,1]{2,0,1:T(8,128)S(1)} %get-tuple-element.15), channel_id=1, source_target_pairs={{0,32},{32,64},{64,96},{96,128},{128,160},{160,192},{192,224},{224... | collective-permute-start | bytes 12296 | tf_op jit(solution)/shard_map/ppermute | solution.py:19
  715.3 22.8 %collective-permute-start.34 = (f32[64,16,1]{2,0,1:T(8,128)S(1)}, f32[64,16,1]{2,0,1:T(8,128)S(1)}, u32[]{:S(2)}, u32[]{:S(2)}) collective-permute-start(f32[64,16,1]{2,0,1:T(8,128)S(1)} %get-tuple-element.14), channel_id=1, source_target_pairs={{32,0},{64,32},{96,64},{128,96},{160,128},{192,160},{224,192},{256... | collective-permute-start | bytes 12296 | tf_op jit(solution)/shard_map/ppermute | solution.py:20
  717.2 20.9 %collective-permute-start.33 = (f32[64,1,128]{2,0,1:T(8,128)S(1)}, f32[64,1,128]{2,0,1:T(8,128)S(1)}, u32[]{:S(2)}, u32[]{:S(2)}) collective-permute-start(f32[64,1,128]{2,0,1:T(8,128)S(1)} %get-tuple-element.13), channel_id=1, source_target_pairs={{1,0},{2,1},{3,2},{4,3},{5,4},{6,5},{7,6},{8,7},{9,8},{10,9},{11,1... | collective-permute-start | bytes 98312 | tf_op jit(solution)/shard_map/ppermute | solution.py:20
  721.5 16.6 %collective-permute-start.32 = (f32[64,1,128]{2,0,1:T(8,128)S(1)}, f32[64,1,128]{2,0,1:T(8,128)S(1)}, u32[]{:S(2)}, u32[]{:S(2)}) collective-permute-start(f32[64,1,128]{2,0,1:T(8,128)S(1)} %get-tuple-element.12), channel_id=1, source_target_pairs={{0,1},{1,2},{2,3},{3,4},{4,5},{5,6},{6,7},{7,8},{8,9},{9,10},{10,1... | collective-permute-start | bytes 98312 | tf_op jit(solution)/shard_map/ppermute | solution.py:19
where the time goes:
time: 741 us; the launch traced here: 739 us
  blocking collectives  478 us (65%)
  starting transfers between devices  131 us (18%)
  waiting for transfers between devices  78.8 us (11%)
  other arithmetic  38.6 us (5%)
  matrix products  7.82 us (1%)
    psum x3, blocking collectives, residual_sum(): return lax.psum(gram(block, block), ('lat', 'lon'))  290 us
    psum x2, blocking collectives, curvature_sum(): return lax.psum(gram(block, image), ('lat', 'lon'))  188 us
    ppermute x18, starting transfers between devices, with_halo(): before = lax.ppermute(last, axis, up)  84.5 us
    ppermute x18, waiting for transfers between devices, with_halo(): after = lax.ppermute(first, axis, down)  72.8 us
    ppermute x18, starting transfers between devices, with_halo(): after = lax.ppermute(first, axis, down)  47 us
    another operation x15, other arithmetic, solve_spd(): factor = jnp.linalg.cholesky(matrix)  18 us
    another operation x10, other arithmetic, solve_spd(): return jax.scipy.linalg.cho_solve((factor, True), rhs_block)  15.4 us
  transfers between devices with their start and end apart: 36, of which 11 were waited for; matrix products, arithmetic and copies ran while one was open for 1% of the time, Pallas kernels for 0%

commit v1 on v0

v1 whole, which is shorter than its diff:
```python
import jax
import jax.numpy as jnp
from jax import lax
from jax.experimental import pallas as pl
from jax.experimental.pallas import tpu as pltpu
from jax.sharding import Mesh
from jax.sharding import PartitionSpec as P

PROBES = 32
DEPTH = 8
ROWS = 16
LANES = 128
FIELDS = 72
SHIFT = 4.0
GAIN = 0.25
PARAMS = pltpu.CompilerParams(vmem_limit_bytes=48 * 1024 * 1024)


def pack_kernel(warm, signs, mask, kappa, scale, low, high, left, right):
    wet = mask[...].astype(jnp.float32)
    diag = kappa[...] + 4.0
    scaled = scale[...]
    block = lax.broadcasted_iota(jnp.int32, (FIELDS, LANES), 1) // DEPTH
    left_edge = jnp.zeros((FIELDS, LANES), jnp.float32)
    right_edge = jnp.zeros((FIELDS, LANES), jnp.float32)
    for i in range(ROWS):
        out = low if i < DEPTH else high
        j = i % DEPTH
        out[j, 0:PROBES, :] = warm[:, i, :]
        out[j, PROBES : 2 * PROBES, :] = 2.0 * signs[:, i, :].astype(jnp.float32) - 1.0
        out[j, 2 * PROBES :, :] = jnp.concatenate(
            [wet[i : i + 1], diag[i : i + 1], scaled[i : i + 1], jnp.zeros((5, LANES), jnp.float32)], axis=0
        )
        row = out[j]
        turned = pltpu.roll(row, DEPTH * i, 1) if i else row
        left_edge = jnp.where(block == i, turned, left_edge)
        right_edge = jnp.where(block == (i - 1) % ROWS, turned, right_edge)
    left[...] = left_edge
    right[...] = right_edge


def corner_kernel(from_left, from_right, first, last):
    lane = lax.broadcasted_iota(jnp.int32, (FIELDS, LANES), 1)
    before, after = from_left[...], from_right[...]
    first[...] = jnp.where(lane < 64, after, pltpu.roll(before, 72, 1))
    last[...] = jnp.where(lane < 64, pltpu.roll(after, 64, 1), pltpu.roll(before, 8, 1))


def krylov_kernel(
    low, high, from_left, from_right, from_next, from_prev, corner_next, corner_prev,
    sums, basis, images, probe_image,
    wide, power, inner, coef,
):
    lane = lax.broadcasted_iota(jnp.int32, (FIELDS, LANES), 1)
    for r in range(ROWS + 2 * DEPTH):
        i = r - DEPTH
        if i < 0:
            wide[r, :, 0:LANES] = from_prev[r]
            pair = corner_prev[...]
            after, before = (pltpu.roll(pair, (LANES - 8 * r) % LANES, 1), pltpu.roll(pair, (56 - 8 * r) % LANES, 1))
        elif i < ROWS:
            wide[r, :, 0:LANES] = low[i] if i < DEPTH else high[i - DEPTH]
            turn = (LANES - 8 * i) % LANES
            after, before = (pltpu.roll(from_right[...], turn, 1), pltpu.roll(from_left[...], turn, 1))
        else:
            j = i - ROWS
            wide[r, :, 0:LANES] = from_next[j]
            pair = corner_next[...]
            after, before = (pltpu.roll(pair, (LANES - 8 * j) % LANES, 1), pltpu.roll(pair, (56 - 8 * j) % LANES, 1))
        wide[r, :, LANES:] = jnp.where(lane < 64, after, before)
        wet = wide[r, 64:65, :]
        coef[r, 0:1, :] = wet
        coef[r, 1:2, :] = wide[r, 65:66, :]
        coef[r, 2:3, :] = wet * wide[r, 66:67, :]
        coef[r, 3:4, :] = GAIN * wet
        coef[r, 4:5, :] = GAIN * ((1.0 - wet) - SHIFT)

    def stencil(read, r):
        here = read(r)
        around = read(r - 1) + read(r + 1)
        around = around + (pltpu.roll(here, 1, 1) + pltpu.roll(here, 2 * LANES - 1, 1))
        return coef[r, 1:2, :] * here - around

    def half_image(read, reach):
        @pl.loop(DEPTH - reach, DEPTH + ROWS + reach, unroll=2)
        def _(r):
            inner[r] = coef[r, 2:3, :] * stencil(lambda t: coef[t, 0:1, :] * read(t), r)

    def inner_row(r):
        return inner[r]

    def warm_row(r):
        return wide[r, 0:PROBES, :]

    def probe_row(r):
        return wide[r, PROBES : 2 * PROBES, :]

    half_image(probe_row, 0)
    for i in range(ROWS):
        probe_image[i] = inner[DEPTH + i, :, 0:LANES]
    half_image(warm_row, 7)
    for i in range(ROWS):
        images[i, 0:PROBES, :] = inner[DEPTH + i, :, 0:LANES]

    @pl.loop(DEPTH - 6, DEPTH + ROWS + 6, unroll=2)
    def _(r):
        image = coef[r, 0:1, :] * stencil(inner_row, r) + (1.0 - coef[r, 0:1, :]) * warm_row(r)
        power[0, r] = probe_row(r) - image

    for k in range(3):

        def read(r, k=k):
            return power[k, r]

        half_image(read, 5 - 2 * k)
        for i in range(ROWS):
            images[i, (k + 1) * PROBES : (k + 2) * PROBES, :] = inner[DEPTH + i, :, 0:LANES]

        @pl.loop(DEPTH - (4 - 2 * k), DEPTH + ROWS + (4 - 2 * k), unroll=2)
        def _(r, k=k, read=read):
            power[k + 1, r] = coef[r, 3:4, :] * stencil(inner_row, r) + coef[r, 4:5, :] * read(r)

    for k in range(4):
        for i in range(ROWS):
            basis[i, k * PROBES : (k + 1) * PROBES, :] = power[k, DEPTH + i, :, 0:LANES]

    def add_gram(i, total):
        block = basis[i]
        return total + lax.dot_general(
            block[0 : 3 * PROBES],
            block,
            (((1,), (1,)), ((), ())),
            precision=lax.Precision.HIGHEST,
            preferred_element_type=jnp.float32,
        )

    total = lax.fori_loop(0, ROWS, add_gram, jnp.zeros((3 * PROBES, 4 * PROBES), jnp.float32))
    lane = lax.broadcasted_iota(jnp.int32, (PROBES, LANES), 1)
    row = lax.broadcasted_iota(jnp.int32, (PROBES, LANES), 0)
    packed = jnp.zeros((PROBES, LANES), jnp.float32)
    for b in range(3):
        even = total[b * PROBES : (b + 1) * PROBES]
        odd = pltpu.roll(even, LANES - PROBES, 1)
        column = lane - b * PROBES
        inside = (column >= 0) & (column < PROBES)
        packed = jnp.where(inside, jnp.where(column >= row, even, odd), packed)
        odd_diagonal = jnp.sum(jnp.where(column == row, odd, 0.0), axis=1, keepdims=True)
        packed = jnp.where(lane == 3 * PROBES + b, odd_diagonal, packed)
    sums[...] = packed


def dot(left, right):
    return jnp.dot(left, right, precision=lax.Precision.HIGHEST, preferred_element_type=jnp.float32)


def eliminate(table):
    row = lax.broadcasted_iota(jnp.int32, (PROBES, 1), 0)
    for k in range(PROBES):
        pivot_row = table[k : k + 1, :]
        pivot_row = pivot_row / pivot_row[:, k : k + 1]
        table = jnp.where(row == k, pivot_row, table - table[:, k : k + 1] * pivot_row)
    return table[:, PROBES:]


def finish_kernel(
    sums, low, high, basis, images, probe_image,
    solution_out, residual_out, grad_out,
    coeffs,
):
    packed = sums[...]
    flipped = packed.T
    lane = lax.broadcasted_iota(jnp.int32, (PROBES, PROBES), 1)
    row = lax.broadcasted_iota(jnp.int32, (PROBES, PROBES), 0)
    moments = []
    for b in range(3):
        block = packed[:, b * PROBES : (b + 1) * PROBES]
        mirror = flipped[b * PROBES : (b + 1) * PROBES, :]
        moments.append(jnp.where(lane >= row, block, mirror))
        odd = jnp.where(lane < row, block, mirror)
        moments.append(jnp.where(lane == row, packed[:, 3 * PROBES + b : 3 * PROBES + b + 1], odd))
    power = [moments[k + 1] * (1.0 / GAIN) + moments[k] * SHIFT for k in range(5)]

    first = eliminate(jnp.concatenate([power[0], power[1], power[2], moments[0]], axis=1))
    below = jnp.concatenate([power[1], power[2]], axis=0)
    rest = jnp.concatenate(
        [
            jnp.concatenate([power[2], power[3], moments[1]], axis=1),
            jnp.concatenate([power[3], power[4], moments[2]], axis=1),
        ],
        axis=0,
    )
    rest = rest - dot(below, first)
    second = eliminate(rest[0:PROBES])
    last = rest[PROBES:, PROBES:] - dot(rest[PROBES:, 0:PROBES], second)
    c2 = eliminate(last)
    c1 = second[:, PROBES:] - dot(second[:, 0:PROBES], c2)
    c0 = first[:, 2 * PROBES :] - dot(first[:, 0 : 2 * PROBES], jnp.concatenate([c1, c2], axis=0))

    one = (lane == row).astype(jnp.float32)
    scale = 1.0 / GAIN
    coeffs[0:PROBES, :] = jnp.concatenate([c0.T, c1.T, c2.T, jnp.zeros_like(c0)], axis=1)
    coeffs[PROBES:, :] = jnp.concatenate(
        [(one - SHIFT * c0).T, (-scale * c0 - SHIFT * c1).T, (-scale * c1 - SHIFT * c2).T, (-scale * c2).T], axis=1
    )
    weights = jnp.concatenate([one, c0.T, c1.T, c2.T], axis=1)

    for i in range(ROWS):
        own = low if i < DEPTH else high
        both = dot(coeffs[...], basis[i])
        values = both[0:PROBES] + own[i % DEPTH, 0:PROBES, :]
        solution_out[:, i, :] = values
        residual_out[:, i, :] = both[PROBES:]
        image = dot(weights, images[i])
        terms = values * probe_image[i] + image * own[i % DEPTH, PROBES : 2 * PROBES, :]
        wet = own[i % DEPTH, 64:65, :]
        grad_out[i : i + 1, :] = wet * (jnp.sum(terms, axis=0, keepdims=True) * (1.0 / PROBES))


def f32(*shape):
    return jax.ShapeDtypeStruct(shape, jnp.float32)


def shifted(value, axes, step, wrap):
    size = lax.axis_size(axes)
    if wrap:
        pairs = [(i, (i + step) % size) for i in range(size)]
    else:
        pairs = [(i, i + step) for i in range(size) if 0 <= i + step < size]
    return lax.ppermute(value, axes, pairs)


def spread_sum(value, axes):
    size = lax.axis_size(axes)
    copies = jnp.broadcast_to(value[None], (size,) + value.shape)
    return jnp.sum(lax.all_to_all(copies, axes, 0, 0), axis=0)


def make_local(lat, lon, stages):
    def local(warm_start, probe_signs, ocean_mask, kappa_sq, scale_field):
        low, high, left, right = pl.pallas_call(
            pack_kernel,
            out_shape=(f32(DEPTH, FIELDS, LANES), f32(DEPTH, FIELDS, LANES), f32(FIELDS, LANES), f32(FIELDS, LANES)),
            compiler_params=PARAMS,
            name="pack_edges",
        )(warm_start, probe_signs, ocean_mask, kappa_sq, scale_field)
        from_left = shifted(right, lat, 1, False)
        from_right = shifted(left, lat, -1, False)
        from_prev = shifted(high, lon, 1, True)
        from_next = shifted(low, lon, -1, True)
        first, last = pl.pallas_call(
            corner_kernel,
            out_shape=(f32(FIELDS, LANES), f32(FIELDS, LANES)),
            compiler_params=PARAMS,
            name="pack_corners",
        )(from_left, from_right)
        corner_prev = shifted(last, lon, 1, True)
        corner_next = shifted(first, lon, -1, True)
        tall = ROWS + 2 * DEPTH
        sums, basis, images, probe_image = pl.pallas_call(
            krylov_kernel,
            out_shape=(
                f32(PROBES, LANES),
                f32(ROWS, 4 * PROBES, LANES),
                f32(ROWS, 4 * PROBES, LANES),
                f32(ROWS, PROBES, LANES),
            ),
            scratch_shapes=[
                pltpu.VMEM((tall, FIELDS, 2 * LANES), jnp.float32),
                pltpu.VMEM((4, tall, PROBES, 2 * LANES), jnp.float32),
                pltpu.VMEM((tall, PROBES, 2 * LANES), jnp.float32),
                pltpu.VMEM((tall, 8, 2 * LANES), jnp.float32),
            ],
            compiler_params=PARAMS,
            name="krylov_moments",
        )(low, high, from_left, from_right, from_next, from_prev, corner_next, corner_prev)
        with jax.named_scope("sum_moments"):
            for axes in stages:
                sums = spread_sum(sums, axes)
        return pl.pallas_call(
            finish_kernel,
            out_shape=(
                f32(PROBES, ROWS, LANES),
                f32(PROBES, ROWS, LANES),
                f32(ROWS, LANES),
            ),
            scratch_shapes=[pltpu.VMEM((2 * PROBES, 4 * PROBES), jnp.float32)],
            compiler_params=PARAMS,
            name="solve_and_combine",
        )(sums, low, high, basis, images, probe_image)

    return local


def solution(mesh):
    if mesh.devices.shape == (16, 32):
        grid = Mesh(mesh.devices.reshape(2, 4, 2, 4, 8), ("zh", "x", "c", "zl", "y"))
        lat, lon = (("zh", "x", "c"), ("zl", "y"))
        stages = (("c",), ("x",), ("y",), ("zh", "zl"))
    else:
        grid, lat, lon, stages = (mesh, ("lat",), ("lon",), (("lat",), ("lon",)))
    return jax.shard_map(
        make_local(lat, lon, stages),
        mesh=grid,
        in_specs=(P(None, lon, lat), P(None, lon, lat), P(lon, lat), P(lon, lat), P(lon, lat)),
        out_specs=(P(None, lon, lat), P(None, lon, lat), P(lon, lat)),
        check_vma=False,
    )
```

time: 741 us -> 117 us (0.16)
  the two profiles are of different devices: /device:TPU:71 before, /device:TPU:2 now
where the time goes in v1:
time: 117 us
  blocking collectives  45.5 us (39%)
  Pallas kernels  28.6 us (24%)
  starting transfers between devices  28 us (24%)
  waiting for transfers between devices  9.56 us (8%)
  local copies, waits for them, and re-layouts  4.02 us (3%)
    all_to_all x4, blocking collectives, spread_sum(): return jnp.sum(lax.all_to_all(copies, axes, 0, 0), axis=0)  45.5 us
    ppermute x6, starting transfers between devices, shifted(): return lax.ppermute(value, axes, pairs)  28 us
    pallas_call x1, Pallas kernels, local(): pl.pallas_call(krylov_kernel, out_shape=(f32(PROBES, LANES), f32(ROWS, 4...  15.8 us
    pallas_call x1, Pallas kernels, local(): pl.pallas_call(finish_kernel, out_shape=(f32(PROBES, ROWS, LANES), f32(PR...  12.2 us
    ppermute x6, waiting for transfers between devices, shifted(): return lax.ppermute(value, axes, pairs)  9.56 us
    unnamed x10, local copies, waits for them, and re-layouts  3.98 us
  transfers between devices with their start and end apart: 6, of which 2 were waited for; matrix products, arithmetic and copies ran while one was open for 0% of the time, Pallas kernels for 0%

profile of v1, /device:TPU:2, one launch (start us, length us, event | category | flops | bytes accessed | tf_op | source)
XLA Modules:
  0.0 116.5 jit_solution(5157363604769482486)
XLA Ops:
  0.6 0.0 copy-start
  0.6 0.9 copy-done
  1.6 0.0 copy-start.1
  1.6 0.9 copy-done.1
  2.5 0.0 copy-start.2
  2.5 0.7 copy-done.2
  3.2 0.0 copy-start.3
  3.2 0.7 copy-done.3
  3.9 0.0 copy-start.4
  3.9 0.7 copy-done.4
  4.6 0.5 pack_edges.1
  5.2 10.8 %collective-permute-start.2 = (f32[8,72,128]{2,1,0:T(8,128)S(1)}, f32[8,72,128]{2,1,0:T(8,128)S(1)}, u32[]{:S(2)}, u32[]{:S(2)}) collective-permute-start(f32[8,72,128]{2,1,0:T(8,128)S(1)} %get-tuple-element.13.low), channel_id=1, source_target_pairs={{0,31},{1,0},{2,1},{3,2},{4,3},{5,4},{6,5},{7,6},{8,7},{9,8},{10,9... | collective-permute-start | bytes 884744 | tf_op jit(solution)/shard_map/ppermute | solution.py:229
  16.0 1.9 %collective-permute-start.3 = (f32[8,72,128]{2,1,0:T(8,128)S(1)}, f32[8,72,128]{2,1,0:T(8,128)S(1)}, u32[]{:S(2)}, u32[]{:S(2)}) collective-permute-start(f32[8,72,128]{2,1,0:T(8,128)S(1)} %get-tuple-element.14.high), channel_id=1, source_target_pairs={{0,1},{1,2},{2,3},{3,4},{4,5},{5,6},{6,7},{7,8},{8,9},{9,10},{10,1... | collective-permute-start | bytes 884744 | tf_op jit(solution)/shard_map/ppermute | solution.py:229
  17.9 1.9 %collective-permute-start = (f32[72,128]{1,0:T(8,128)S(1)}, f32[72,128]{1,0:T(8,128)S(1)}, u32[]{:S(2)}, u32[]{:S(2)}) collective-permute-start(f32[72,128]{1,0:T(8,128)S(1)} %get-tuple-element.15), channel_id=1, source_target_pairs={{0,32},{32,64},{64,96},{96,128},{128,160},{160,192},{192,224},{224... | collective-permute-start | bytes 110600 | tf_op jit(solution)/shard_map/ppermute | solution.py:229
  19.8 3.6 %collective-permute-start.1 = (f32[72,128]{1,0:T(8,128)S(1)}, f32[72,128]{1,0:T(8,128)S(1)}, u32[]{:S(2)}, u32[]{:S(2)}) collective-permute-start(f32[72,128]{1,0:T(8,128)S(1)} %get-tuple-element.16), channel_id=1, source_target_pairs={{32,0},{64,32},{96,64},{128,96},{160,128},{192,160},{224,192},{256... | collective-permute-start | bytes 110600 | tf_op jit(solution)/shard_map/ppermute | solution.py:229
  23.5 0.0 collective-permute-done.from_left
  23.5 1.6 %collective-permute-done.1.from_right = f32[72,128]{1,0:T(8,128)S(1)} collective-permute-done((f32[72,128]{1,0:T(8,128)S(1)}, f32[72,128]{1,0:T(8,128)S(1)}, u32[]{:S(2)}, u32[]{:S(2)}) %collective-permute-start.1) | collective-permute-done | bytes 36896 | tf_op jit(solution)/shard_map/ppermute | solution.py:229
  25.1 0.1 pack_corners.1
  25.2 7.8 %collective-permute-start.4 = (f32[72,128]{1,0:T(8,128)S(1)}, f32[72,128]{1,0:T(8,128)S(1)}, u32[]{:S(2)}, u32[]{:S(2)}) collective-permute-start(f32[72,128]{1,0:T(8,128)S(1)} %get-tuple-element.17), channel_id=1, source_target_pairs={{0,31},{1,0},{2,1},{3,2},{4,3},{5,4},{6,5},{7,6},{8,7},{9,8},{10,9... | collective-permute-start | bytes 110600 | tf_op jit(solution)/shard_map/ppermute | solution.py:229
  33.0 1.9 %collective-permute-start.5 = (f32[72,128]{1,0:T(8,128)S(1)}, f32[72,128]{1,0:T(8,128)S(1)}, u32[]{:S(2)}, u32[]{:S(2)}) collective-permute-start(f32[72,128]{1,0:T(8,128)S(1)} %get-tuple-element.18), channel_id=1, source_target_pairs={{0,1},{1,2},{2,3},{3,4},{4,5},{5,6},{6,7},{7,8},{8,9},{9,10},{10,1... | collective-permute-start | bytes 110600 | tf_op jit(solution)/shard_map/ppermute | solution.py:229
  34.9 0.0 collective-permute-done.4.corner_next
  35.0 7.9 %collective-permute-done.5.corner_prev = f32[72,128]{1,0:T(8,128)S(1)} collective-permute-done((f32[72,128]{1,0:T(8,128)S(1)}, f32[72,128]{1,0:T(8,128)S(1)}, u32[]{:S(2)}, u32[]{:S(2)}) %collective-permute-start.5) | collective-permute-done | bytes 36896 | tf_op jit(solution)/shard_map/ppermute | solution.py:229
  42.9 0.0 collective-permute-done.2.from_next
  42.9 0.0 collective-permute-done.3.from_prev
  42.9 15.8 %krylov_moments.1 = (f32[32,128]{1,0:T(8,128)S(1)}, f32[16,128,128]{2,1,0:T(8,128)S(1)}, f32[16,128,128]{2,1,0:T(8,128)S(1)}, f32[16,32,128]{2,1,0:T(8,128)S(1)}) custom-call(f32[8,72,128]{2,1,0:T(8,128)S(1)} %get-tuple-element.13.low, f32[8,72,128]{2,1,0:T(8,128)S(1)} %get-tuple-element.14.high, f32[72,128]{1,0:T(8,128)S(1)} %collective-permute-done.from_left, ...), custom_call_target="tpu_custom_call" | custom-call | tf_op jit(solution)/shard_map/krylov_moments/pallas_call | solution.py:259
  58.7 3.7 %all_to_all.20 = f32[2,32,128]{2,1,0:T(8,128)S(1)} all-to-all(f32[2,32,128]{2,1,0:T(8,128)S(1)} %broadcast_in_dim.8), channel_id=1, replica_groups=mesh['zh'=2,'x'=4,'c'=2,'zl'=4,'y'=8] {'c'}, dimensions={0} | all-to-all | bytes 65536 | tf_op jit(solution)/shard_map/sum_moments/all_to_all | solution.py:235
  62.5 18.8 %all_to_all.21 = f32[4,32,128]{2,1,0:T(8,128)S(1)} all-to-all(f32[4,32,128]{2,1,0:T(8,128)S(1)} %broadcast_in_dim.9), channel_id=1, replica_groups=mesh['zh'=2,'x'=4,'c'=2,'zl'=4,'y'=8] {'x'}, dimensions={0} | all-to-all | bytes 131072 | tf_op jit(solution)/shard_map/sum_moments/all_to_all | solution.py:235
  81.4 11.5 %all_to_all.22 = f32[8,32,128]{2,1,0:T(8,128)S(1)} all-to-all(f32[8,32,128]{2,1,0:T(8,128)S(1)} %broadcast_in_dim.10), channel_id=1, replica_groups=mesh['zh'=2,'x'=4,'c'=2,'zl'=4,'y'=8] {'y'}, dimensions={0} | all-to-all | bytes 262144 | tf_op jit(solution)/shard_map/sum_moments/all_to_all | solution.py:235
  92.9 11.5 %all_to_all.23 = f32[8,32,128]{2,1,0:T(8,128)S(1)} all-to-all(f32[8,32,128]{2,1,0:T(8,128)S(1)} %broadcast_in_dim.11), channel_id=1, replica_groups=mesh['zh'=2,'x'=4,'c'=2,'zl'=4,'y'=8] {'zh','zl'}, dimensions={0} | all-to-all | bytes 262144 | tf_op jit(solution)/shard_map/sum_moments/all_to_all | solution.py:235
  104.3 12.2 %solve_and_combine.1 = (f32[32,16,128]{2,1,0:T(8,128)}, f32[32,16,128]{2,1,0:T(8,128)}, f32[16,128]{1,0:T(8,128)}) custom-call(f32[32,128]{1,0:T(8,128)S(1)} %reduce_sum.39.sums, f32[8,72,128]{2,1,0:T(8,128)S(1)} %get-tuple-element.13.low, f32[8,72,128]{2,1,0:T(8,128)S(1)} %get-tuple-element.14.high, f32[16,128,128]{2,1,0:T(8,128)S(1)} %get-tuple-element.20.basis, ...), custom_call_target="tpu_custom_call" | custom-call | tf_op jit(solution)/shard_map/solve_and_combine/pallas_call | solution.py:279
  (8 shorter events, 0.1 us)
Async XLA Ops:
  0.6 1.0 copy-start
  1.6 0.9 copy-start.1
  2.5 0.7 copy-start.2
  3.2 0.7 copy-start.3
  3.9 0.7 copy-start.4
  5.2 37.7 %collective-permute-start.2 = (f32[8,72,128]{2,1,0:T(8,128)S(1)}, f32[8,72,128]{2,1,0:T(8,128)S(1)}, u32[]{:S(2)}, u32[]{:S(2)}) collective-permute-start(f32[8,72,128]{2,1,0:T(8,128)S(1)} %get-tuple-element.13.low), channel_id=1, source_target_pairs={{0,31},{1,0},{2,1},{3,2},{4,3},{5,4},{6,5},{7,6},{8,7},{9,8},{10,9... | collective-permute-start | bytes 884744 | tf_op jit(solution)/shard_map/ppermute | solution.py:229
  16.0 26.9 %collective-permute-start.3 = (f32[8,72,128]{2,1,0:T(8,128)S(1)}, f32[8,72,128]{2,1,0:T(8,128)S(1)}, u32[]{:S(2)}, u32[]{:S(2)}) collective-permute-start(f32[8,72,128]{2,1,0:T(8,128)S(1)} %get-tuple-element.14.high), channel_id=1, source_target_pairs={{0,1},{1,2},{2,3},{3,4},{4,5},{5,6},{6,7},{7,8},{8,9},{9,10},{10,1... | collective-permute-start | bytes 884744 | tf_op jit(solution)/shard_map/ppermute | solution.py:229
  17.9 5.6 %collective-permute-start = (f32[72,128]{1,0:T(8,128)S(1)}, f32[72,128]{1,0:T(8,128)S(1)}, u32[]{:S(2)}, u32[]{:S(2)}) collective-permute-start(f32[72,128]{1,0:T(8,128)S(1)} %get-tuple-element.15), channel_id=1, source_target_pairs={{0,32},{32,64},{64,96},{96,128},{128,160},{160,192},{192,224},{224... | collective-permute-start | bytes 110600 | tf_op jit(solution)/shard_map/ppermute | solution.py:229
  19.8 5.3 %collective-permute-start.1 = (f32[72,128]{1,0:T(8,128)S(1)}, f32[72,128]{1,0:T(8,128)S(1)}, u32[]{:S(2)}, u32[]{:S(2)}) collective-permute-start(f32[72,128]{1,0:T(8,128)S(1)} %get-tuple-element.16), channel_id=1, source_target_pairs={{32,0},{64,32},{96,64},{128,96},{160,128},{192,160},{224,192},{256... | collective-permute-start | bytes 110600 | tf_op jit(solution)/shard_map/ppermute | solution.py:229
  25.2 9.8 %collective-permute-start.4 = (f32[72,128]{1,0:T(8,128)S(1)}, f32[72,128]{1,0:T(8,128)S(1)}, u32[]{:S(2)}, u32[]{:S(2)}) collective-permute-start(f32[72,128]{1,0:T(8,128)S(1)} %get-tuple-element.17), channel_id=1, source_target_pairs={{0,31},{1,0},{2,1},{3,2},{4,3},{5,4},{6,5},{7,6},{8,7},{9,8},{10,9... | collective-permute-start | bytes 110600 | tf_op jit(solution)/shard_map/ppermute | solution.py:229
  33.0 9.9 %collective-permute-start.5 = (f32[72,128]{1,0:T(8,128)S(1)}, f32[72,128]{1,0:T(8,128)S(1)}, u32[]{:S(2)}, u32[]{:S(2)}) collective-permute-start(f32[72,128]{1,0:T(8,128)S(1)} %get-tuple-element.18), channel_id=1, source_target_pairs={{0,1},{1,2},{2,3},{3,4},{4,5},{5,6},{6,7},{7,8},{8,9},{9,10},{10,1... | collective-permute-start | bytes 110600 | tf_op jit(solution)/shard_map/ppermute | solution.py:229

commit v2 on v1

--- a/solution.py
+++ b/solution.py
@@ -49,7 +49,7 @@
 def krylov_kernel(
     low, high, from_left, from_right, from_next, from_prev, corner_next, corner_prev,
     sums, basis, images, probe_image,
-    wide, power, inner, coef,
+    wide, power, masked, inner, coef,
 ):
     lane = lax.broadcasted_iota(jnp.int32, (FIELDS, LANES), 1)
     for r in range(ROWS + 2 * DEPTH):
@@ -75,66 +75,61 @@
         coef[r, 3:4, :] = GAIN * wet
         coef[r, 4:5, :] = GAIN * ((1.0 - wet) - SHIFT)
 
-    def stencil(read, r):
-        here = read(r)
-        around = read(r - 1) + read(r + 1)
+    def stencil(field, r):
+        here = field[r]
+        around = field[r - 1] + field[r + 1]
         around = around + (pltpu.roll(here, 1, 1) + pltpu.roll(here, 2 * LANES - 1, 1))
         return coef[r, 1:2, :] * here - around
 
-    def half_image(read, reach):
-        @pl.loop(DEPTH - reach, DEPTH + ROWS + reach, unroll=2)
-        def _(r):
-            inner[r] = coef[r, 2:3, :] * stencil(lambda t: coef[t, 0:1, :] * read(t), r)
-
-    def inner_row(r):
-        return inner[r]
-
-    def warm_row(r):
-        return wide[r, 0:PROBES, :]
-
-    def probe_row(r):
-        return wide[r, PROBES : 2 * PROBES, :]
-
-    half_image(probe_row, 0)
+    def half_image(field, reach, keep):
+        for r in range(DEPTH - reach, DEPTH + ROWS + reach):
+            value = coef[r, 2:3, :] * stencil(field, r)
+            inner[r] = value
+            if DEPTH <= r < DEPTH + ROWS:
+                keep(r - DEPTH, value[:, 0:LANES])
+
+    def keep_images(k):
+        def keep(i, value):
+            images[i, k * PROBES : (k + 1) * PROBES, :] = value
+
+        return keep
+
+    def keep_probe_image(i, value):
+        probe_image[i] = value
+
+    for r in range(DEPTH - 1, DEPTH + ROWS + 1):
+        masked[r] = coef[r, 0:1, :] * wide[r, PROBES : 2 * PROBES, :]
+    half_image(masked, 0, keep_probe_image)
+    for r in range(ROWS + 2 * DEPTH):
+        masked[r] = coef[r, 0:1, :] * wide[r, 0:PROBES, :]
+    half_image(masked, 7, keep_images(3))
+
+    for k in range(4):
+        reach = 6 - 2 * k
+        for r in range(DEPTH - reach, DEPTH + ROWS + reach):
+            if k == 0:
+                image = coef[r, 0:1, :] * stencil(inner, r) + (1.0 - coef[r, 0:1, :]) * wide[r, 0:PROBES, :]
+                value = wide[r, PROBES : 2 * PROBES, :] - image
+            else:
+                value = coef[r, 3:4, :] * stencil(inner, r) + coef[r, 4:5, :] * power[r]
+            if k < 3:
+                power[r] = value
+                masked[r] = coef[r, 0:1, :] * value
+            if DEPTH <= r < DEPTH + ROWS:
+                basis[r - DEPTH, k * PROBES : (k + 1) * PROBES, :] = value[:, 0:LANES]
+        if k < 3:
+            half_image(masked, reach - 1, keep_images(k))
+
+    total = jnp.zeros((3 * PROBES, 4 * PROBES), jnp.float32)
     for i in range(ROWS):
-        probe_image[i] = inner[DEPTH + i, :, 0:LANES]
-    half_image(warm_row, 7)
-    for i in range(ROWS):
-        images[i, 0:PROBES, :] = inner[DEPTH + i, :, 0:LANES]
-
-    @pl.loop(DEPTH - 6, DEPTH + ROWS + 6, unroll=2)
-    def _(r):
-        image = coef[r, 0:1, :] * stencil(inner_row, r) + (1.0 - coef[r, 0:1, :]) * warm_row(r)
-        power[0, r] = probe_row(r) - image
-
-    for k in range(3):
-
-        def read(r, k=k):
-            return power[k, r]
-
-        half_image(read, 5 - 2 * k)
-        for i in range(ROWS):
-            images[i, (k + 1) * PROBES : (k + 2) * PROBES, :] = inner[DEPTH + i, :, 0:LANES]
-
-        @pl.loop(DEPTH - (4 - 2 * k), DEPTH + ROWS + (4 - 2 * k), unroll=2)
-        def _(r, k=k, read=read):
-            power[k + 1, r] = coef[r, 3:4, :] * stencil(inner_row, r) + coef[r, 4:5, :] * read(r)
-
-    for k in range(4):
-        for i in range(ROWS):
-            basis[i, k * PROBES : (k + 1) * PROBES, :] = power[k, DEPTH + i, :, 0:LANES]
-
-    def add_gram(i, total):
         block = basis[i]
-        return total + lax.dot_general(
+        total = total + lax.dot_general(
             block[0 : 3 * PROBES],
             block,
             (((1,), (1,)), ((), ())),
-            precision=lax.Precision.HIGHEST,
+            precision=lax.Precision.HIGH,
             preferred_element_type=jnp.float32,
         )
-
-    total = lax.fori_loop(0, ROWS, add_gram, jnp.zeros((3 * PROBES, 4 * PROBES), jnp.float32))
     lane = lax.broadcasted_iota(jnp.int32, (PROBES, LANES), 1)
     row = lax.broadcasted_iota(jnp.int32, (PROBES, LANES), 0)
     packed = jnp.zeros((PROBES, LANES), jnp.float32)
@@ -149,17 +144,45 @@
     sums[...] = packed
 
 
-def dot(left, right):
-    return jnp.dot(left, right, precision=lax.Precision.HIGHEST, preferred_element_type=jnp.float32)
-
-
-def eliminate(table):
-    row = lax.broadcasted_iota(jnp.int32, (PROBES, 1), 0)
-    for k in range(PROBES):
-        pivot_row = table[k : k + 1, :]
-        pivot_row = pivot_row / pivot_row[:, k : k + 1]
-        table = jnp.where(row == k, pivot_row, table - table[:, k : k + 1] * pivot_row)
-    return table[:, PROBES:]
+def dot(left, right, precision=lax.Precision.HIGHEST):
+    return jnp.dot(left, right, precision=precision, preferred_element_type=jnp.float32)
+
+
+def eliminate(table, at):
+    width = table.shape[1]
+    parts = [table[8 * v : 8 * v + 8] for v in range(4)]
+    row = lax.broadcasted_iota(jnp.int32, (8, width), 0)
+
+    def spread(value):
+        return jnp.broadcast_to(value, (8, width))
+
+    for k in range(0, PROBES, 4):
+        home = k // 8
+        r = [spread(parts[home][k % 8 + i : k % 8 + i + 1]) for i in range(4)]
+        p = {(i, j): spread(r[i][:, at + k + j : at + k + j + 1]) for i in range(4) for j in range(i, 4)}
+        columns = [[spread(part[:, at + k + j : at + k + j + 1]) for j in range(4)] for part in parts]
+        first = 1.0 / (p[0, 0] * p[1, 1] - p[0, 1] * p[0, 1])
+        a00, a01, a11 = (p[1, 1] * first, -p[0, 1] * first, p[0, 0] * first)
+        e02, e03 = (a00 * p[0, 2] + a01 * p[1, 2], a00 * p[0, 3] + a01 * p[1, 3])
+        e12, e13 = (a01 * p[0, 2] + a11 * p[1, 2], a01 * p[0, 3] + a11 * p[1, 3])
+        s00 = p[2, 2] - (p[0, 2] * e02 + p[1, 2] * e12)
+        s01 = p[2, 3] - (p[0, 2] * e03 + p[1, 2] * e13)
+        s11 = p[3, 3] - (p[0, 3] * e03 + p[1, 3] * e13)
+        second = 1.0 / (s00 * s11 - s01 * s01)
+        t00, t01, t11 = (s11 * second, -s01 * second, s00 * second)
+        y0, y1 = (a00 * r[0] + a01 * r[1], a01 * r[0] + a11 * r[1])
+        z2 = r[2] - (p[0, 2] * y0 + p[1, 2] * y1)
+        z3 = r[3] - (p[0, 3] * y0 + p[1, 3] * y1)
+        x2, x3 = (t00 * z2 + t01 * z3, t01 * z2 + t11 * z3)
+        x0, x1 = (y0 - (e02 * x2 + e03 * x3), y1 - (e12 * x2 + e13 * x3))
+        solved = (x0, x1, x2, x3)
+        parts = [
+            part - ((column[0] * x0 + column[1] * x1) + (column[2] * x2 + column[3] * x3))
+            for part, column in zip(parts, columns, strict=True)
+        ]
+        for i in range(4):
+            parts[home] = jnp.where(row == k % 8 + i, solved[i], parts[home])
+    return jnp.concatenate(parts, axis=0)
 
 
 def finish_kernel(
@@ -180,37 +203,45 @@
         moments.append(jnp.where(lane == row, packed[:, 3 * PROBES + b : 3 * PROBES + b + 1], odd))
     power = [moments[k + 1] * (1.0 / GAIN) + moments[k] * SHIFT for k in range(5)]
 
-    first = eliminate(jnp.concatenate([power[0], power[1], power[2], moments[0]], axis=1))
-    below = jnp.concatenate([power[1], power[2]], axis=0)
+    zero = jnp.zeros((PROBES, PROBES), jnp.float32)
+    first = eliminate(jnp.concatenate([moments[0], power[2], power[1], power[0]], axis=1), 3 * PROBES)
+    first = first[:, 0 : 3 * PROBES]
     rest = jnp.concatenate(
         [
-            jnp.concatenate([power[2], power[3], moments[1]], axis=1),
-            jnp.concatenate([power[3], power[4], moments[2]], axis=1),
+            jnp.concatenate([moments[1], power[3], power[2]], axis=1),
+            jnp.concatenate([moments[2], power[4], power[3]], axis=1),
         ],
         axis=0,
     )
-    rest = rest - dot(below, first)
-    second = eliminate(rest[0:PROBES])
-    last = rest[PROBES:, PROBES:] - dot(rest[PROBES:, 0:PROBES], second)
-    c2 = eliminate(last)
-    c1 = second[:, PROBES:] - dot(second[:, 0:PROBES], c2)
-    c0 = first[:, 2 * PROBES :] - dot(first[:, 0 : 2 * PROBES], jnp.concatenate([c1, c2], axis=0))
+    rest = rest - dot(jnp.concatenate([power[1], power[2]], axis=0), first)
+    second = eliminate(rest[0:PROBES], 2 * PROBES)[:, 0 : 2 * PROBES]
+    nothing = jnp.zeros((2 * PROBES, 2 * PROBES), jnp.float32)
+    last = rest[PROBES:, 0 : 2 * PROBES] - dot(rest[PROBES:], jnp.concatenate([nothing, second], axis=0))
+    c2 = eliminate(last, PROBES)[:, 0:PROBES]
+    c1 = second[:, 0:PROBES] - dot(second, jnp.concatenate([zero, c2], axis=0))
+    c0 = first[:, 0:PROBES] - dot(first, jnp.concatenate([zero, c2, c1], axis=0))
 
     one = (lane == row).astype(jnp.float32)
     scale = 1.0 / GAIN
-    coeffs[0:PROBES, :] = jnp.concatenate([c0.T, c1.T, c2.T, jnp.zeros_like(c0)], axis=1)
-    coeffs[PROBES:, :] = jnp.concatenate(
-        [(one - SHIFT * c0).T, (-scale * c0 - SHIFT * c1).T, (-scale * c1 - SHIFT * c2).T, (-scale * c2).T], axis=1
+    columns = jnp.concatenate(
+        [
+            jnp.concatenate([c0, one - SHIFT * c0], axis=1),
+            jnp.concatenate([c1, -scale * c0 - SHIFT * c1], axis=1),
+            jnp.concatenate([c2, -scale * c1 - SHIFT * c2], axis=1),
+            jnp.concatenate([zero, -scale * c2], axis=1),
+        ],
+        axis=0,
     )
-    weights = jnp.concatenate([one, c0.T, c1.T, c2.T], axis=1)
+    coeffs[...] = columns.T
+    weights = coeffs[0:PROBES, :] + jnp.concatenate([zero, zero, zero, one], axis=1)
 
     for i in range(ROWS):
         own = low if i < DEPTH else high
-        both = dot(coeffs[...], basis[i])
+        both = dot(coeffs[...], basis[i], lax.Precision.HIGH)
         values = both[0:PROBES] + own[i % DEPTH, 0:PROBES, :]
         solution_out[:, i, :] = values
         residual_out[:, i, :] = both[PROBES:]
-        image = dot(weights, images[i])
+        image = dot(weights, images[i], lax.Precision.HIGH)
         terms = values * probe_image[i] + image * own[i % DEPTH, PROBES : 2 * PROBES, :]
         wet = own[i % DEPTH, 64:65, :]
         grad_out[i : i + 1, :] = wet * (jnp.sum(terms, axis=0, keepdims=True) * (1.0 / PROBES))
@@ -266,7 +297,8 @@
             ),
             scratch_shapes=[
                 pltpu.VMEM((tall, FIELDS, 2 * LANES), jnp.float32),
-                pltpu.VMEM((4, tall, PROBES, 2 * LANES), jnp.float32),
+                pltpu.VMEM((tall, PROBES, 2 * LANES), jnp.float32),
+                pltpu.VMEM((tall, PROBES, 2 * LANES), jnp.float32),
                 pltpu.VMEM((tall, PROBES, 2 * LANES), jnp.float32),
                 pltpu.VMEM((tall, 8, 2 * LANES), jnp.float32),
             ],

time: 117 us -> 101 us (0.86)
  Pallas kernels: 28.6 us -> 12.3 us
    pallas_call x1, Pallas kernels: 15.8 us -> 4.63 us  [local(): pl.pallas_call(krylov_kernel, out_shape=(f32(PROBES, LANES), f32(ROWS, 4...]
    pallas_call x1, Pallas kernels: 12.2 us -> 7.1 us  [local(): pl.pallas_call(finish_kernel, out_shape=(f32(PROBES, ROWS, LANES), f32(PR...]
where the time goes in v2:
time: 101 us; the launch traced here: 100 us
  blocking collectives  45.5 us (45%)
  starting transfers between devices  28 us (28%)
  Pallas kernels  12.3 us (12%)
  waiting for transfers between devices  9.56 us (9%)
  local copies, waits for them, and re-layouts  4.02 us (4%)
    all_to_all x4, blocking collectives, spread_sum(): return jnp.sum(lax.all_to_all(copies, axes, 0, 0), axis=0)  45.5 us
    ppermute x6, starting transfers between devices, shifted(): return lax.ppermute(value, axes, pairs)  28 us
    ppermute x6, waiting for transfers between devices, shifted(): return lax.ppermute(value, axes, pairs)  9.56 us
    pallas_call x1, Pallas kernels, local(): pl.pallas_call(finish_kernel, out_shape=(f32(PROBES, ROWS, LANES), f32(PR...  7.1 us
    pallas_call x1, Pallas kernels, local(): pl.pallas_call(krylov_kernel, out_shape=(f32(PROBES, LANES), f32(ROWS, 4...  4.63 us
    unnamed x10, local copies, waits for them, and re-layouts  3.98 us
  transfers between devices with their start and end apart: 6, of which 2 were waited for; matrix products, arithmetic and copies ran while one was open for 0% of the time, Pallas kernels for 0%

profile of v2, /device:TPU:2, one launch (start us, length us, event | category | flops | bytes accessed | tf_op | source)
XLA Modules:
  0.0 100.2 jit_solution(16691688210440481551)
XLA Ops:
  0.6 0.0 copy-start
  0.6 0.9 copy-done
  1.6 0.0 copy-start.1
  1.6 0.9 copy-done.1
  2.5 0.0 copy-start.2
  2.5 0.7 copy-done.2
  3.2 0.0 copy-start.3
  3.2 0.7 copy-done.3
  3.9 0.0 copy-start.4
  3.9 0.7 copy-done.4
  4.6 0.5 pack_edges.1
  5.2 10.8 %collective-permute-start.2 = (f32[8,72,128]{2,1,0:T(8,128)S(1)}, f32[8,72,128]{2,1,0:T(8,128)S(1)}, u32[]{:S(2)}, u32[]{:S(2)}) collective-permute-start(f32[8,72,128]{2,1,0:T(8,128)S(1)} %get-tuple-element.13.low), channel_id=1, source_target_pairs={{0,31},{1,0},{2,1},{3,2},{4,3},{5,4},{6,5},{7,6},{8,7},{9,8},{10,9... | collective-permute-start | bytes 884744 | tf_op jit(solution)/shard_map/ppermute | solution.py:260
  16.0 1.9 %collective-permute-start.3 = (f32[8,72,128]{2,1,0:T(8,128)S(1)}, f32[8,72,128]{2,1,0:T(8,128)S(1)}, u32[]{:S(2)}, u32[]{:S(2)}) collective-permute-start(f32[8,72,128]{2,1,0:T(8,128)S(1)} %get-tuple-element.14.high), channel_id=1, source_target_pairs={{0,1},{1,2},{2,3},{3,4},{4,5},{5,6},{6,7},{7,8},{8,9},{9,10},{10,1... | collective-permute-start | bytes 884744 | tf_op jit(solution)/shard_map/ppermute | solution.py:260
  17.9 1.9 %collective-permute-start = (f32[72,128]{1,0:T(8,128)S(1)}, f32[72,128]{1,0:T(8,128)S(1)}, u32[]{:S(2)}, u32[]{:S(2)}) collective-permute-start(f32[72,128]{1,0:T(8,128)S(1)} %get-tuple-element.15), channel_id=1, source_target_pairs={{0,32},{32,64},{64,96},{96,128},{128,160},{160,192},{192,224},{224... | collective-permute-start | bytes 110600 | tf_op jit(solution)/shard_map/ppermute | solution.py:260
  19.8 3.6 %collective-permute-start.1 = (f32[72,128]{1,0:T(8,128)S(1)}, f32[72,128]{1,0:T(8,128)S(1)}, u32[]{:S(2)}, u32[]{:S(2)}) collective-permute-start(f32[72,128]{1,0:T(8,128)S(1)} %get-tuple-element.16), channel_id=1, source_target_pairs={{32,0},{64,32},{96,64},{128,96},{160,128},{192,160},{224,192},{256... | collective-permute-start | bytes 110600 | tf_op jit(solution)/shard_map/ppermute | solution.py:260
  23.5 0.0 collective-permute-done.from_left
  23.5 1.6 %collective-permute-done.1.from_right = f32[72,128]{1,0:T(8,128)S(1)} collective-permute-done((f32[72,128]{1,0:T(8,128)S(1)}, f32[72,128]{1,0:T(8,128)S(1)}, u32[]{:S(2)}, u32[]{:S(2)}) %collective-permute-start.1) | collective-permute-done | bytes 36896 | tf_op jit(solution)/shard_map/ppermute | solution.py:260
  25.1 0.1 pack_corners.1
  25.2 7.8 %collective-permute-start.4 = (f32[72,128]{1,0:T(8,128)S(1)}, f32[72,128]{1,0:T(8,128)S(1)}, u32[]{:S(2)}, u32[]{:S(2)}) collective-permute-start(f32[72,128]{1,0:T(8,128)S(1)} %get-tuple-element.17), channel_id=1, source_target_pairs={{0,31},{1,0},{2,1},{3,2},{4,3},{5,4},{6,5},{7,6},{8,7},{9,8},{10,9... | collective-permute-start | bytes 110600 | tf_op jit(solution)/shard_map/ppermute | solution.py:260
  33.0 1.9 %collective-permute-start.5 = (f32[72,128]{1,0:T(8,128)S(1)}, f32[72,128]{1,0:T(8,128)S(1)}, u32[]{:S(2)}, u32[]{:S(2)}) collective-permute-start(f32[72,128]{1,0:T(8,128)S(1)} %get-tuple-element.18), channel_id=1, source_target_pairs={{0,1},{1,2},{2,3},{3,4},{4,5},{5,6},{6,7},{7,8},{8,9},{9,10},{10,1... | collective-permute-start | bytes 110600 | tf_op jit(solution)/shard_map/ppermute | solution.py:260
  34.9 0.0 collective-permute-done.4.corner_next
  35.0 7.9 %collective-permute-done.5.corner_prev = f32[72,128]{1,0:T(8,128)S(1)} collective-permute-done((f32[72,128]{1,0:T(8,128)S(1)}, f32[72,128]{1,0:T(8,128)S(1)}, u32[]{:S(2)}, u32[]{:S(2)}) %collective-permute-start.5) | collective-permute-done | bytes 36896 | tf_op jit(solution)/shard_map/ppermute | solution.py:260
  42.9 0.0 collective-permute-done.2.from_next
  42.9 0.0 collective-permute-done.3.from_prev
  42.9 4.6 %krylov_moments.1 = (f32[32,128]{1,0:T(8,128)S(1)}, f32[16,128,128]{2,1,0:T(8,128)S(1)}, f32[16,128,128]{2,1,0:T(8,128)S(1)}, f32[16,32,128]{2,1,0:T(8,128)S(1)}) custom-call(f32[8,72,128]{2,1,0:T(8,128)S(1)} %get-tuple-element.13.low, f32[8,72,128]{2,1,0:T(8,128)S(1)} %get-tuple-element.14.high, f32[72,128]{1,0:T(8,128)S(1)} %collective-permute-done.from_left, ...), custom_call_target="tpu_custom_call" | custom-call | tf_op jit(solution)/shard_map/krylov_moments/pallas_call | solution.py:290
  47.6 3.7 %all_to_all.20 = f32[2,32,128]{2,1,0:T(8,128)S(1)} all-to-all(f32[2,32,128]{2,1,0:T(8,128)S(1)} %broadcast_in_dim.8), channel_id=1, replica_groups=mesh['zh'=2,'x'=4,'c'=2,'zl'=4,'y'=8] {'c'}, dimensions={0} | all-to-all | bytes 65536 | tf_op jit(solution)/shard_map/sum_moments/all_to_all | solution.py:266
  51.3 18.8 %all_to_all.21 = f32[4,32,128]{2,1,0:T(8,128)S(1)} all-to-all(f32[4,32,128]{2,1,0:T(8,128)S(1)} %broadcast_in_dim.9), channel_id=1, replica_groups=mesh['zh'=2,'x'=4,'c'=2,'zl'=4,'y'=8] {'x'}, dimensions={0} | all-to-all | bytes 131072 | tf_op jit(solution)/shard_map/sum_moments/all_to_all | solution.py:266
  70.2 11.5 %all_to_all.22 = f32[8,32,128]{2,1,0:T(8,128)S(1)} all-to-all(f32[8,32,128]{2,1,0:T(8,128)S(1)} %broadcast_in_dim.10), channel_id=1, replica_groups=mesh['zh'=2,'x'=4,'c'=2,'zl'=4,'y'=8] {'y'}, dimensions={0} | all-to-all | bytes 262144 | tf_op jit(solution)/shard_map/sum_moments/all_to_all | solution.py:266
  81.7 11.5 %all_to_all.23 = f32[8,32,128]{2,1,0:T(8,128)S(1)} all-to-all(f32[8,32,128]{2,1,0:T(8,128)S(1)} %broadcast_in_dim.11), channel_id=1, replica_groups=mesh['zh'=2,'x'=4,'c'=2,'zl'=4,'y'=8] {'zh','zl'}, dimensions={0} | all-to-all | bytes 262144 | tf_op jit(solution)/shard_map/sum_moments/all_to_all | solution.py:266
  93.1 7.1 %solve_and_combine.1 = (f32[32,16,128]{2,1,0:T(8,128)}, f32[32,16,128]{2,1,0:T(8,128)}, f32[16,128]{1,0:T(8,128)}) custom-call(f32[32,128]{1,0:T(8,128)S(1)} %reduce_sum.39.sums, f32[8,72,128]{2,1,0:T(8,128)S(1)} %get-tuple-element.13.low, f32[8,72,128]{2,1,0:T(8,128)S(1)} %get-tuple-element.14.high, f32[16,128,128]{2,1,0:T(8,128)S(1)} %get-tuple-element.20.basis, ...), custom_call_target="tpu_custom_call" | custom-call | tf_op jit(solution)/shard_map/solve_and_combine/pallas_call | solution.py:311
  (8 shorter events, 0.1 us)
Async XLA Ops:
  0.6 1.0 copy-start
  1.6 0.9 copy-start.1
  2.5 0.7 copy-start.2
  3.2 0.7 copy-start.3
  3.9 0.7 copy-start.4
  5.2 37.7 %collective-permute-start.2 = (f32[8,72,128]{2,1,0:T(8,128)S(1)}, f32[8,72,128]{2,1,0:T(8,128)S(1)}, u32[]{:S(2)}, u32[]{:S(2)}) collective-permute-start(f32[8,72,128]{2,1,0:T(8,128)S(1)} %get-tuple-element.13.low), channel_id=1, source_target_pairs={{0,31},{1,0},{2,1},{3,2},{4,3},{5,4},{6,5},{7,6},{8,7},{9,8},{10,9... | collective-permute-start | bytes 884744 | tf_op jit(solution)/shard_map/ppermute | solution.py:260
  16.0 26.9 %collective-permute-start.3 = (f32[8,72,128]{2,1,0:T(8,128)S(1)}, f32[8,72,128]{2,1,0:T(8,128)S(1)}, u32[]{:S(2)}, u32[]{:S(2)}) collective-permute-start(f32[8,72,128]{2,1,0:T(8,128)S(1)} %get-tuple-element.14.high), channel_id=1, source_target_pairs={{0,1},{1,2},{2,3},{3,4},{4,5},{5,6},{6,7},{7,8},{8,9},{9,10},{10,1... | collective-permute-start | bytes 884744 | tf_op jit(solution)/shard_map/ppermute | solution.py:260
  17.9 5.6 %collective-permute-start = (f32[72,128]{1,0:T(8,128)S(1)}, f32[72,128]{1,0:T(8,128)S(1)}, u32[]{:S(2)}, u32[]{:S(2)}) collective-permute-start(f32[72,128]{1,0:T(8,128)S(1)} %get-tuple-element.15), channel_id=1, source_target_pairs={{0,32},{32,64},{64,96},{96,128},{128,160},{160,192},{192,224},{224... | collective-permute-start | bytes 110600 | tf_op jit(solution)/shard_map/ppermute | solution.py:260
  19.8 5.3 %collective-permute-start.1 = (f32[72,128]{1,0:T(8,128)S(1)}, f32[72,128]{1,0:T(8,128)S(1)}, u32[]{:S(2)}, u32[]{:S(2)}) collective-permute-start(f32[72,128]{1,0:T(8,128)S(1)} %get-tuple-element.16), channel_id=1, source_target_pairs={{32,0},{64,32},{96,64},{128,96},{160,128},{192,160},{224,192},{256... | collective-permute-start | bytes 110600 | tf_op jit(solution)/shard_map/ppermute | solution.py:260
  25.2 9.8 %collective-permute-start.4 = (f32[72,128]{1,0:T(8,128)S(1)}, f32[72,128]{1,0:T(8,128)S(1)}, u32[]{:S(2)}, u32[]{:S(2)}) collective-permute-start(f32[72,128]{1,0:T(8,128)S(1)} %get-tuple-element.17), channel_id=1, source_target_pairs={{0,31},{1,0},{2,1},{3,2},{4,3},{5,4},{6,5},{7,6},{8,7},{9,8},{10,9... | collective-permute-start | bytes 110600 | tf_op jit(solution)/shard_map/ppermute | solution.py:260
  33.0 9.9 %collective-permute-start.5 = (f32[72,128]{1,0:T(8,128)S(1)}, f32[72,128]{1,0:T(8,128)S(1)}, u32[]{:S(2)}, u32[]{:S(2)}) collective-permute-start(f32[72,128]{1,0:T(8,128)S(1)} %get-tuple-element.18), channel_id=1, source_target_pairs={{0,1},{1,2},{2,3},{3,4},{4,5},{5,6},{6,7},{7,8},{8,9},{9,10},{10,1... | collective-permute-start | bytes 110600 | tf_op jit(solution)/shard_map/ppermute | solution.py:260

commit v3 on v2

--- a/solution.py
+++ b/solution.py
@@ -1,3 +1,5 @@
+import functools
+
 import jax
 import jax.numpy as jnp
 from jax import lax
@@ -16,58 +18,106 @@
 PARAMS = pltpu.CompilerParams(vmem_limit_bytes=48 * 1024 * 1024)
 
 
-def pack_kernel(warm, signs, mask, kappa, scale, low, high, left, right):
+def parities(axes):
+    return tuple(lax.rem(lax.axis_index(axis), 2) for axis in axes)
+
+
+def pack_kernel(axes, warm_hbm, signs_hbm, mask_hbm, kappa_hbm, scale_hbm, own, fields, to_even, to_odd, *scratch):
+    odd, _ = parities(axes)
+    sems = scratch[-1]
+    copies = [
+        pltpu.make_async_copy(source, target, sems.at[n])
+        for n, (source, target) in enumerate(
+            zip((warm_hbm, signs_hbm, mask_hbm, kappa_hbm, scale_hbm), scratch[:-1], strict=True)
+        )
+    ]
+    for copy in copies:
+        copy.start()
+    for copy in copies:
+        copy.wait()
+    warm, signs, mask, kappa, scale = scratch[:-1]
     wet = mask[...].astype(jnp.float32)
     diag = kappa[...] + 4.0
     scaled = scale[...]
+    fields[0] = wet
+    fields[1] = diag
+    fields[2] = scaled
     block = lax.broadcasted_iota(jnp.int32, (FIELDS, LANES), 1) // DEPTH
     left_edge = jnp.zeros((FIELDS, LANES), jnp.float32)
     right_edge = jnp.zeros((FIELDS, LANES), jnp.float32)
     for i in range(ROWS):
-        out = low if i < DEPTH else high
-        j = i % DEPTH
-        out[j, 0:PROBES, :] = warm[:, i, :]
-        out[j, PROBES : 2 * PROBES, :] = 2.0 * signs[:, i, :].astype(jnp.float32) - 1.0
-        out[j, 2 * PROBES :, :] = jnp.concatenate(
+        own[i, 0:PROBES, :] = warm[:, i, :]
+        own[i, PROBES : 2 * PROBES, :] = 2.0 * signs[:, i, :].astype(jnp.float32) - 1.0
+        own[i, 2 * PROBES :, :] = jnp.concatenate(
             [wet[i : i + 1], diag[i : i + 1], scaled[i : i + 1], jnp.zeros((5, LANES), jnp.float32)], axis=0
         )
-        row = out[j]
+        row = own[i]
         turned = pltpu.roll(row, DEPTH * i, 1) if i else row
         left_edge = jnp.where(block == i, turned, left_edge)
         right_edge = jnp.where(block == (i - 1) % ROWS, turned, right_edge)
-    left[...] = left_edge
-    right[...] = right_edge
-
-
-def corner_kernel(from_left, from_right, first, last):
+    to_even[...] = jnp.where(odd == 0, right_edge, left_edge)
+    to_odd[...] = jnp.where(odd == 0, left_edge, right_edge)
+
+
+def sides(odd, even_side, odd_side):
+    return jnp.where(odd == 0, odd_side, even_side), jnp.where(odd == 0, even_side, odd_side)
+
+
+SEND_PROBES = DEPTH * PROBES
+SEND_FIELDS = SEND_PROBES + (DEPTH - 2) * PROBES
+SEND_CORNER = SEND_FIELDS + 3 * DEPTH
+SEND_ROWS = SEND_CORNER + FIELDS
+
+
+def send_kernel(axes, own, fields, from_even, from_odd, to_even, to_odd):
+    odd_lat, odd_lon = parities(axes)
     lane = lax.broadcasted_iota(jnp.int32, (FIELDS, LANES), 1)
-    before, after = from_left[...], from_right[...]
-    first[...] = jnp.where(lane < 64, after, pltpu.roll(before, 72, 1))
-    last[...] = jnp.where(lane < 64, pltpu.roll(after, 64, 1), pltpu.roll(before, 8, 1))
+    before, after = sides(odd_lat, from_even[...], from_odd[...])
+    first = jnp.where(lane < 64, after, pltpu.roll(before, 72, 1))
+    last = jnp.where(lane < 64, pltpu.roll(after, 64, 1), pltpu.roll(before, 8, 1))
+    for target, is_last in ((to_even, odd_lon == 0), (to_odd, odd_lon != 0)):
+        start = jnp.where(is_last, DEPTH, 0)
+        near = jnp.where(is_last, DEPTH + 2, 0)
+        for j in range(DEPTH):
+            target[j * PROBES : (j + 1) * PROBES, :] = own[start + j, 0:PROBES, :]
+        for j in range(DEPTH - 2):
+            target[SEND_PROBES + j * PROBES : SEND_PROBES + (j + 1) * PROBES, :] = own[near + j, PROBES : 2 * PROBES, :]
+        for f in range(3):
+            target[SEND_FIELDS + f * DEPTH : SEND_FIELDS + (f + 1) * DEPTH, :] = jnp.where(
+                is_last, fields[f, DEPTH:, :], fields[f, 0:DEPTH, :]
+            )
+        target[SEND_CORNER:, :] = jnp.where(is_last, last, first)
 
 
 def krylov_kernel(
-    low, high, from_left, from_right, from_next, from_prev, corner_next, corner_prev,
+    axes,
+    own, from_even_lat, from_odd_lat, from_even_lon, from_odd_lon,
     sums, basis, images, probe_image,
     wide, power, masked, inner, coef,
 ):
+    odd_lat, odd_lon = parities(axes)
     lane = lax.broadcasted_iota(jnp.int32, (FIELDS, LANES), 1)
+    before, after = sides(odd_lat, from_even_lat[...], from_odd_lat[...])
+    for i in range(ROWS):
+        turn = (LANES - 8 * i) % LANES
+        wide[DEPTH + i, :, 0:LANES] = own[i]
+        wide[DEPTH + i, :, LANES:] = jnp.where(lane < 64, pltpu.roll(after, turn, 1), pltpu.roll(before, turn, 1))
+    for side, is_next in ((from_even_lon, odd_lon == 0), (from_odd_lon, odd_lon != 0)):
+        start = jnp.where(is_next, DEPTH + ROWS, 0)
+        near = jnp.where(is_next, DEPTH + ROWS, 2)
+        pair = side[SEND_CORNER:, :]
+        for j in range(DEPTH):
+            wide[start + j, 0:PROBES, 0:LANES] = side[j * PROBES : (j + 1) * PROBES, :]
+            for f in range(3):
+                at = SEND_FIELDS + f * DEPTH + j
+                wide[start + j, 2 * PROBES + f : 2 * PROBES + f + 1, 0:LANES] = side[at : at + 1, :]
+            wide[start + j, :, LANES:] = jnp.where(
+                lane < 64, pltpu.roll(pair, (LANES - 8 * j) % LANES, 1), pltpu.roll(pair, (56 - 8 * j) % LANES, 1)
+            )
+        for j in range(DEPTH - 2):
+            at = SEND_PROBES + j * PROBES
+            wide[near + j, PROBES : 2 * PROBES, 0:LANES] = side[at : at + PROBES, :]
     for r in range(ROWS + 2 * DEPTH):
-        i = r - DEPTH
-        if i < 0:
-            wide[r, :, 0:LANES] = from_prev[r]
-            pair = corner_prev[...]
-            after, before = (pltpu.roll(pair, (LANES - 8 * r) % LANES, 1), pltpu.roll(pair, (56 - 8 * r) % LANES, 1))
-        elif i < ROWS:
-            wide[r, :, 0:LANES] = low[i] if i < DEPTH else high[i - DEPTH]
-            turn = (LANES - 8 * i) % LANES
-            after, before = (pltpu.roll(from_right[...], turn, 1), pltpu.roll(from_left[...], turn, 1))
-        else:
-            j = i - ROWS
-            wide[r, :, 0:LANES] = from_next[j]
-            pair = corner_next[...]
-            after, before = (pltpu.roll(pair, (LANES - 8 * j) % LANES, 1), pltpu.roll(pair, (56 - 8 * j) % LANES, 1))
-        wide[r, :, LANES:] = jnp.where(lane < 64, after, before)
         wet = wide[r, 64:65, :]
         coef[r, 0:1, :] = wet
         coef[r, 1:2, :] = wide[r, 65:66, :]
@@ -186,7 +236,7 @@
 
 
 def finish_kernel(
-    sums, low, high, basis, images, probe_image,
+    sums, own, basis, images, probe_image,
     solution_out, residual_out, grad_out,
     coeffs,
 ):
@@ -236,14 +286,13 @@
     weights = coeffs[0:PROBES, :] + jnp.concatenate([zero, zero, zero, one], axis=1)
 
     for i in range(ROWS):
-        own = low if i < DEPTH else high
         both = dot(coeffs[...], basis[i], lax.Precision.HIGH)
-        values = both[0:PROBES] + own[i % DEPTH, 0:PROBES, :]
+        values = both[0:PROBES] + own[i, 0:PROBES, :]
         solution_out[:, i, :] = values
         residual_out[:, i, :] = both[PROBES:]
         image = dot(weights, images[i], lax.Precision.HIGH)
-        terms = values * probe_image[i] + image * own[i % DEPTH, PROBES : 2 * PROBES, :]
-        wet = own[i % DEPTH, 64:65, :]
+        terms = values * probe_image[i] + image * own[i, PROBES : 2 * PROBES, :]
+        wet = own[i, 64:65, :]
         grad_out[i : i + 1, :] = wet * (jnp.sum(terms, axis=0, keepdims=True) * (1.0 / PROBES))
 
 
@@ -251,12 +300,13 @@
     return jax.ShapeDtypeStruct(shape, jnp.float32)
 
 
-def shifted(value, axes, step, wrap):
+def exchanged(value, axes, odd, wrap):
     size = lax.axis_size(axes)
-    if wrap:
-        pairs = [(i, (i + step) % size) for i in range(size)]
-    else:
-        pairs = [(i, i + step) for i in range(size) if 0 <= i + step < size]
+    pairs = []
+    for i in range(size):
+        other = ((i + odd) ^ 1) - odd
+        if wrap or 0 <= other < size:
+            pairs.append((i, other % size))
     return lax.ppermute(value, axes, pairs)
 
 
@@ -267,28 +317,36 @@
 
 
 def make_local(lat, lon, stages):
+    axes = (lat[-1], lon[-1])
+
     def local(warm_start, probe_signs, ocean_mask, kappa_sq, scale_field):
-        low, high, left, right = pl.pallas_call(
-            pack_kernel,
-            out_shape=(f32(DEPTH, FIELDS, LANES), f32(DEPTH, FIELDS, LANES), f32(FIELDS, LANES), f32(FIELDS, LANES)),
+        args = (warm_start, probe_signs, ocean_mask, kappa_sq, scale_field)
+        own, fields, to_even, to_odd = pl.pallas_call(
+            functools.partial(pack_kernel, axes),
+            out_shape=(
+                f32(ROWS, FIELDS, LANES),
+                f32(3, ROWS, LANES),
+                f32(FIELDS, LANES),
+                f32(FIELDS, LANES),
+            ),
+            in_specs=[pl.BlockSpec(memory_space=pl.ANY)] * 5,
+            scratch_shapes=[pltpu.VMEM(x.shape, x.dtype) for x in args] + [pltpu.SemaphoreType.DMA((5,))],
             compiler_params=PARAMS,
             name="pack_edges",
-        )(warm_start, probe_signs, ocean_mask, kappa_sq, scale_field)
-        from_left = shifted(right, lat, 1, False)
-        from_right = shifted(left, lat, -1, False)
-        from_prev = shifted(high, lon, 1, True)
-        from_next = shifted(low, lon, -1, True)
-        first, last = pl.pallas_call(
-            corner_kernel,
-            out_shape=(f32(FIELDS, LANES), f32(FIELDS, LANES)),
+        )(*args)
+        odd_lat = exchanged(to_odd, lat, 1, False)
+        even_lat = exchanged(to_even, lat, 0, False)
+        to_even, to_odd = pl.pallas_call(
+            functools.partial(send_kernel, axes),
+            out_shape=(f32(SEND_ROWS, LANES), f32(SEND_ROWS, LANES)),
             compiler_params=PARAMS,
-            name="pack_corners",
-        )(from_left, from_right)
-        corner_prev = shifted(last, lon, 1, True)
-        corner_next = shifted(first, lon, -1, True)
+            name="pack_rows",
+        )(own, fields, even_lat, odd_lat)
+        odd_lon = exchanged(to_odd, lon, 1, True)
+        even_lon = exchanged(to_even, lon, 0, True)
         tall = ROWS + 2 * DEPTH
         sums, basis, images, probe_image = pl.pallas_call(
-            krylov_kernel,
+            functools.partial(krylov_kernel, axes),
             out_shape=(
                 f32(PROBES, LANES),
                 f32(ROWS, 4 * PROBES, LANES),
@@ -304,10 +362,10 @@
             ],
             compiler_params=PARAMS,
             name="krylov_moments",
-        )(low, high, from_left, from_right, from_next, from_prev, corner_next, corner_prev)
+        )(own, even_lat, odd_lat, even_lon, odd_lon)
         with jax.named_scope("sum_moments"):
-            for axes in stages:
-                sums = spread_sum(sums, axes)
+            for group in stages:
+                sums = spread_sum(sums, group)
         return pl.pallas_call(
             finish_kernel,
             out_shape=(
@@ -318,7 +376,7 @@
             scratch_shapes=[pltpu.VMEM((2 * PROBES, 4 * PROBES), jnp.float32)],
             compiler_params=PARAMS,
             name="solve_and_combine",
-        )(sums, low, high, basis, images, probe_image)
+        )(sums, own, basis, images, probe_image)
 
     return local
 
@@ -327,7 +385,7 @@
     if mesh.devices.shape == (16, 32):
         grid = Mesh(mesh.devices.reshape(2, 4, 2, 4, 8), ("zh", "x", "c", "zl", "y"))
         lat, lon = (("zh", "x", "c"), ("zl", "y"))
-        stages = (("c",), ("x",), ("y",), ("zh", "zl"))
+        stages = (("x", "c"), ("y",), ("zh", "zl"))
     else:
         grid, lat, lon, stages = (mesh, ("lat",), ("lon",), (("lat",), ("lon",)))
     return jax.shard_map(

time: 101 us -> 87 us (0.86)
  starting transfers between devices: 28 us -> 19.6 us
  blocking collectives: 45.5 us -> 40.9 us
    ppermute x6 -> x4, starting transfers between devices: 28 us -> 19.6 us  [exchanged(): return lax.ppermute(value, axes, pairs)]
    all_to_all x4 -> x3, blocking collectives: 45.5 us -> 40.9 us  [spread_sum(): return jnp.sum(lax.all_to_all(copies, axes, 0, 0), axis=0)]
    ppermute x6 -> x4, waiting for transfers between devices: 9.56 us -> 8.64 us  [exchanged(): return lax.ppermute(value, axes, pairs)]
  transfers between devices with their start and end apart: 6 -> 4, of which waited for: 2 -> 2; matrix products, arithmetic and copies ran while one was open for 0% -> 0% of each run, Pallas kernels for 0% -> 0%
where the time goes in v3:
time: 87 us; the launch traced here: 86.5 us
  blocking collectives  40.9 us (47%)
  starting transfers between devices  19.6 us (23%)
  Pallas kernels  12.5 us (14%)
  waiting for transfers between devices  8.64 us (10%)
  local copies, waits for them, and re-layouts  4.02 us (5%)
    all_to_all x3, blocking collectives, spread_sum(): return jnp.sum(lax.all_to_all(copies, axes, 0, 0), axis=0)  40.9 us
    ppermute x4, starting transfers between devices, exchanged(): return lax.ppermute(value, axes, pairs)  19.6 us
    ppermute x4, waiting for transfers between devices, exchanged(): return lax.ppermute(value, axes, pairs)  8.64 us
    pallas_call x1, Pallas kernels, local(): pl.pallas_call(finish_kernel, out_shape=(f32(PROBES, ROWS, LANES), f32(PR...  7.1 us
    pallas_call x1, Pallas kernels, local(): pl.pallas_call(functools.partial(krylov_kernel, axes), out_shape=(f32(PRO...  4.65 us
    unnamed x10, local copies, waits for them, and re-layouts  3.98 us
  transfers between devices with their start and end apart: 4, of which 2 were waited for; matrix products, arithmetic and copies ran while one was open for 0% of the time, Pallas kernels for 0%

profile of v3, /device:TPU:2, one launch (start us, length us, event | category | flops | bytes accessed | tf_op | source)
XLA Modules:
  0.0 86.5 jit_solution(1616889208913707282)
XLA Ops:
  0.6 0.0 copy-start
  0.6 0.9 %copy-done = f32[32,16,128]{2,1,0:T(8,128)S(1)} copy-done((f32[32,16,128]{2,1,0:T(8,128)S(1)}, f32[32,16,128]{2,1,0:T(8,128)}, u32[]{:S(2)}) %copy-start) | copy-done | bytes 262168
  1.6 0.0 copy-start.1
  1.6 0.9 %copy-done.1 = s32[32,16,128]{2,1,0:T(8,128)S(1)} copy-done((s32[32,16,128]{2,1,0:T(8,128)S(1)}, s32[32,16,128]{2,1,0:T(8,128)}, u32[]{:S(2)}) %copy-start.1) | copy-done | bytes 262168
  2.5 0.0 copy-start.2
  2.5 0.7 copy-done.2
  3.2 0.0 copy-start.3
  3.2 0.7 copy-done.3
  3.9 0.0 copy-start.4
  3.9 0.7 copy-done.4
  4.6 0.7 pack_edges.1
  5.3 1.9 %collective-permute-start = (f32[72,128]{1,0:T(8,128)S(1)}, f32[72,128]{1,0:T(8,128)S(1)}, u32[]{:S(2)}, u32[]{:S(2)}) collective-permute-start(f32[72,128]{1,0:T(8,128)S(1)} %get-tuple-element.14), channel_id=1, source_target_pairs={{0,32},{32,0},{64,96},{96,64},{128,160},{160,128},{192,224},{224,1... | collective-permute-start | bytes 110600 | tf_op jit(solution)/shard_map/ppermute | solution.py:310
  7.2 7.9 %collective-permute-start.1 = (f32[72,128]{1,0:T(8,128)S(1)}, f32[72,128]{1,0:T(8,128)S(1)}, u32[]{:S(2)}, u32[]{:S(2)}) collective-permute-start(f32[72,128]{1,0:T(8,128)S(1)} %get-tuple-element.15), channel_id=1, source_target_pairs={{32,64},{64,32},{96,128},{128,96},{160,192},{192,160},{224,256},{2... | collective-permute-start | bytes 110600 | tf_op jit(solution)/shard_map/ppermute | solution.py:310
  15.1 0.0 collective-permute-done.from_even.from_even_lat
  15.2 1.6 %collective-permute-done.1.from_odd.from_odd_lat = f32[72,128]{1,0:T(8,128)S(1)} collective-permute-done((f32[72,128]{1,0:T(8,128)S(1)}, f32[72,128]{1,0:T(8,128)S(1)}, u32[]{:S(2)}, u32[]{:S(2)}) %collective-permute-start.1) | collective-permute-done | bytes 36896 | tf_op jit(solution)/shard_map/ppermute | solution.py:310
  16.8 0.1 pack_rows.1
  16.9 1.9 %collective-permute-start.2 = (f32[544,128]{1,0:T(8,128)S(1)}, f32[544,128]{1,0:T(8,128)S(1)}, u32[]{:S(2)}, u32[]{:S(2)}) collective-permute-start(f32[544,128]{1,0:T(8,128)S(1)} %get-tuple-element.17), channel_id=1, source_target_pairs={{0,1},{1,0},{2,3},{3,2},{4,5},{5,4},{6,7},{7,6},{8,9},{9,8},{10,11... | collective-permute-start | bytes 835592 | tf_op jit(solution)/shard_map/ppermute | solution.py:310
  18.8 7.9 %collective-permute-start.3 = (f32[544,128]{1,0:T(8,128)S(1)}, f32[544,128]{1,0:T(8,128)S(1)}, u32[]{:S(2)}, u32[]{:S(2)}) collective-permute-start(f32[544,128]{1,0:T(8,128)S(1)} %get-tuple-element.18), channel_id=1, source_target_pairs={{0,31},{1,2},{2,1},{3,4},{4,3},{5,6},{6,5},{7,8},{8,7},{9,10},{10,... | collective-permute-start | bytes 835592 | tf_op jit(solution)/shard_map/ppermute | solution.py:310
  26.7 0.0 collective-permute-done.2.from_even_lon
  26.7 7.0 %collective-permute-done.3.from_odd_lon = f32[544,128]{1,0:T(8,128)S(1)} collective-permute-done((f32[544,128]{1,0:T(8,128)S(1)}, f32[544,128]{1,0:T(8,128)S(1)}, u32[]{:S(2)}, u32[]{:S(2)}) %collective-permute-start.3) | collective-permute-done | bytes 278560 | tf_op jit(solution)/shard_map/ppermute | solution.py:310
  33.7 4.7 %krylov_moments.1 = (f32[32,128]{1,0:T(8,128)S(1)}, f32[16,128,128]{2,1,0:T(8,128)S(1)}, f32[16,128,128]{2,1,0:T(8,128)S(1)}, f32[16,32,128]{2,1,0:T(8,128)S(1)}) custom-call(f32[16,72,128]{2,1,0:T(8,128)S(1)} %get-tuple-element.13.own, f32[72,128]{1,0:T(8,128)S(1)} %collective-permute-done.from_even.from_even_lat, ...), custom_call_target="tpu_custom_call" | custom-call | tf_op jit(solution)/shard_map/krylov_moments/pallas_call | solution.py:348
  38.4 11.5 %all_to_all.15 = f32[8,32,128]{2,1,0:T(8,128)S(1)} all-to-all(f32[8,32,128]{2,1,0:T(8,128)S(1)} %broadcast_in_dim.6), channel_id=1, replica_groups=mesh['zh'=2,'x'=4,'c'=2,'zl'=4,'y'=8] {'x','c'}, dimensions={0} | all-to-all | bytes 262144 | tf_op jit(solution)/shard_map/sum_moments/all_to_all | solution.py:316
  49.9 11.5 %all_to_all.16 = f32[8,32,128]{2,1,0:T(8,128)S(1)} all-to-all(f32[8,32,128]{2,1,0:T(8,128)S(1)} %broadcast_in_dim.7), channel_id=1, replica_groups=mesh['zh'=2,'x'=4,'c'=2,'zl'=4,'y'=8] {'y'}, dimensions={0} | all-to-all | bytes 262144 | tf_op jit(solution)/shard_map/sum_moments/all_to_all | solution.py:316
  61.5 17.9 %all_to_all.17 = f32[8,32,128]{2,1,0:T(8,128)S(1)} all-to-all(f32[8,32,128]{2,1,0:T(8,128)S(1)} %broadcast_in_dim.8), channel_id=1, replica_groups=mesh['zh'=2,'x'=4,'c'=2,'zl'=4,'y'=8] {'zh','zl'}, dimensions={0} | all-to-all | bytes 262144 | tf_op jit(solution)/shard_map/sum_moments/all_to_all | solution.py:316
  79.4 7.1 %solve_and_combine.1 = (f32[32,16,128]{2,1,0:T(8,128)}, f32[32,16,128]{2,1,0:T(8,128)}, f32[16,128]{1,0:T(8,128)}) custom-call(f32[32,128]{1,0:T(8,128)S(1)} %reduce_sum.29.sums, f32[16,72,128]{2,1,0:T(8,128)S(1)} %get-tuple-element.13.own, f32[16,128,128]{2,1,0:T(8,128)S(1)} %get-tuple-element.20.basis, f32[16,128,128]{2,1,0:T(8,128)S(1)} %get-tuple-element.21.images, ...), custom_call_target="tpu_custom_call" | custom-call | tf_op jit(solution)/shard_map/solve_and_combine/pallas_call | solution.py:369
  (6 shorter events, 0.1 us)
Async XLA Ops:
  0.6 1.0 %copy-start = (f32[32,16,128]{2,1,0:T(8,128)S(1)}, f32[32,16,128]{2,1,0:T(8,128)}, u32[]{:S(2)}) copy-start(f32[32,16,128]{2,1,0:T(8,128)} %warm_hbm.1) | copy-start | bytes 786436
  1.6 0.9 %copy-start.1 = (s32[32,16,128]{2,1,0:T(8,128)S(1)}, s32[32,16,128]{2,1,0:T(8,128)}, u32[]{:S(2)}) copy-start(s32[32,16,128]{2,1,0:T(8,128)} %signs_hbm.1) | copy-start | bytes 786436
  2.5 0.7 copy-start.2
  3.2 0.7 copy-start.3
  3.9 0.7 copy-start.4
  5.3 9.9 %collective-permute-start = (f32[72,128]{1,0:T(8,128)S(1)}, f32[72,128]{1,0:T(8,128)S(1)}, u32[]{:S(2)}, u32[]{:S(2)}) collective-permute-start(f32[72,128]{1,0:T(8,128)S(1)} %get-tuple-element.14), channel_id=1, source_target_pairs={{0,32},{32,0},{64,96},{96,64},{128,160},{160,128},{192,224},{224,1... | collective-permute-start | bytes 110600 | tf_op jit(solution)/shard_map/ppermute | solution.py:310
  7.2 9.6 %collective-permute-start.1 = (f32[72,128]{1,0:T(8,128)S(1)}, f32[72,128]{1,0:T(8,128)S(1)}, u32[]{:S(2)}, u32[]{:S(2)}) collective-permute-start(f32[72,128]{1,0:T(8,128)S(1)} %get-tuple-element.15), channel_id=1, source_target_pairs={{32,64},{64,32},{96,128},{128,96},{160,192},{192,160},{224,256},{2... | collective-permute-start | bytes 110600 | tf_op jit(solution)/shard_map/ppermute | solution.py:310
  16.9 9.8 %collective-permute-start.2 = (f32[544,128]{1,0:T(8,128)S(1)}, f32[544,128]{1,0:T(8,128)S(1)}, u32[]{:S(2)}, u32[]{:S(2)}) collective-permute-start(f32[544,128]{1,0:T(8,128)S(1)} %get-tuple-element.17), channel_id=1, source_target_pairs={{0,1},{1,0},{2,3},{3,2},{4,5},{5,4},{6,7},{7,6},{8,9},{9,8},{10,11... | collective-permute-start | bytes 835592 | tf_op jit(solution)/shard_map/ppermute | solution.py:310
  18.8 14.9 %collective-permute-start.3 = (f32[544,128]{1,0:T(8,128)S(1)}, f32[544,128]{1,0:T(8,128)S(1)}, u32[]{:S(2)}, u32[]{:S(2)}) collective-permute-start(f32[544,128]{1,0:T(8,128)S(1)} %get-tuple-element.18), channel_id=1, source_target_pairs={{0,31},{1,2},{2,1},{3,4},{4,3},{5,6},{6,5},{7,8},{8,7},{9,10},{10,... | collective-permute-start | bytes 835592 | tf_op jit(solution)/shard_map/ppermute | solution.py:310

commit v4 on v3

v4 whole, which is shorter than its diff:
```python
import functools

import jax
import jax.numpy as jnp
from jax import lax
from jax.experimental import pallas as pl
from jax.experimental.pallas import tpu as pltpu
from jax.sharding import Mesh
from jax.sharding import PartitionSpec as P

PROBES = 32
DEPTH = 8
ROWS = 16
LANES = 128
FIELDS = 72
SHIFT = 4.0
GAIN = 0.25
PARAMS = pltpu.CompilerParams(vmem_limit_bytes=32 * 1024 * 1024)
ALL_PARAMS = pltpu.CompilerParams(vmem_limit_bytes=60 * 1024 * 1024)


def parities(axes):
    return tuple(lax.rem(lax.axis_index(axis), 2) for axis in axes)


def pack_kernel(axes, warm_hbm, signs_hbm, mask_hbm, kappa_hbm, scale_hbm, own, fields, to_odd, to_even, *scratch):
    odd, _ = parities(axes)
    sems = scratch[-1]
    copies = [
        pltpu.make_async_copy(source, target, sems.at[n])
        for n, (source, target) in enumerate(
            zip((warm_hbm, signs_hbm, mask_hbm, kappa_hbm, scale_hbm), scratch[:-1], strict=True)
        )
    ]
    for copy in copies:
        copy.start()
    for copy in copies:
        copy.wait()
    warm, signs, mask, kappa, scale = scratch[:-1]
    wet = mask[...].astype(jnp.float32)
    diag = kappa[...] + 4.0
    scaled = scale[...]
    fields[0] = wet
    fields[1] = diag
    fields[2] = scaled
    block = lax.broadcasted_iota(jnp.int32, (FIELDS, LANES), 1) // DEPTH
    left_edge = jnp.zeros((FIELDS, LANES), jnp.float32)
    right_edge = jnp.zeros((FIELDS, LANES), jnp.float32)
    for i in range(ROWS):
        own[i, 0:PROBES, :] = warm[:, i, :]
        own[i, PROBES : 2 * PROBES, :] = 2.0 * signs[:, i, :].astype(jnp.float32) - 1.0
        own[i, 2 * PROBES :, :] = jnp.concatenate(
            [wet[i : i + 1], diag[i : i + 1], scaled[i : i + 1], jnp.zeros((5, LANES), jnp.float32)], axis=0
        )
        row = own[i]
        turned = pltpu.roll(row, DEPTH * i, 1) if i else row
        left_edge = jnp.where(block == i, turned, left_edge)
        right_edge = jnp.where(block == (i - 1) % ROWS, turned, right_edge)
    to_even[...] = jnp.where(odd == 0, right_edge, left_edge)
    to_odd[...] = jnp.where(odd == 0, left_edge, right_edge)


def sides(odd, even_side, odd_side):
    return jnp.where(odd == 0, odd_side, even_side), jnp.where(odd == 0, even_side, odd_side)


SEND_PROBES = DEPTH * PROBES
SEND_FIELDS = SEND_PROBES + (DEPTH - 2) * PROBES
SEND_CORNER = SEND_FIELDS + 3 * DEPTH
SEND_ROWS = SEND_CORNER + FIELDS


def send_kernel(axes, own, fields, from_odd, from_even, to_odd, to_even):
    odd_lat, odd_lon = parities(axes)
    lane = lax.broadcasted_iota(jnp.int32, (FIELDS, LANES), 1)
    before, after = sides(odd_lat, from_even[...], from_odd[...])
    first = jnp.where(lane < 64, after, pltpu.roll(before, 72, 1))
    last = jnp.where(lane < 64, pltpu.roll(after, 64, 1), pltpu.roll(before, 8, 1))
    for target, is_last in ((to_even, odd_lon == 0), (to_odd, odd_lon != 0)):
        start = jnp.where(is_last, DEPTH, 0)
        near = jnp.where(is_last, DEPTH + 2, 0)
        for j in range(DEPTH):
            target[j * PROBES : (j + 1) * PROBES, :] = own[start + j, 0:PROBES, :]
        for j in range(DEPTH - 2):
            target[SEND_PROBES + j * PROBES : SEND_PROBES + (j + 1) * PROBES, :] = own[near + j, PROBES : 2 * PROBES, :]
        for f in range(3):
            target[SEND_FIELDS + f * DEPTH : SEND_FIELDS + (f + 1) * DEPTH, :] = jnp.where(
                is_last, fields[f, DEPTH:, :], fields[f, 0:DEPTH, :]
            )
        target[SEND_CORNER:, :] = jnp.where(is_last, last, first)


TALL = ROWS + 2 * DEPTH
INSIDE = dict(mp=(8, 24), up=(9, 23), mw=(8, 24), i0=(9, 23), p0=(10, 22), m0=(10, 22), i1=(11, 21), p1=(12, 20), m1=(12, 20), i2=(13, 19), p2=(14, 18), m2=(14, 18), i3=(15, 17))
NEEDED = dict(mp=(7, 25), up=(8, 24), mw=(0, 32), i0=(1, 31), p0=(2, 30), m0=(2, 30), i1=(3, 29), p1=(4, 28), m1=(4, 28), i2=(5, 27), p2=(6, 26), m2=(6, 26), i3=(7, 25), p3=(8, 24))
HELD = tuple(INSIDE)


def fill_coef(coef, at, wet, diag, scaled):
    coef[at, 0:1, :] = wet
    coef[at, 1:2, :] = diag
    coef[at, 2:3, :] = wet * scaled
    coef[at, 3:4, :] = GAIN * wet
    coef[at, 4:5, :] = GAIN * ((1.0 - wet) - SHIFT)


def march(rows, coef, warm, probe, get, put):
    def stencil(name, r):
        here = get(name, r)
        around = get(name, r - 1) + get(name, r + 1)
        around = around + (pltpu.roll(here, 1, 1) + pltpu.roll(here, 2 * LANES - 1, 1))
        return coef(r, 1) * here - around

    for r in rows("mp"):
        put("mp", r, coef(r, 0) * probe(r))
    for r in rows("mw"):
        put("mw", r, coef(r, 0) * warm(r))
    for r in rows("i0"):
        put("i0", r, coef(r, 2) * stencil("mw", r))
    for r in rows("up"):
        put("up", r, coef(r, 2) * stencil("mp", r))
    for k in range(4):
        power = f"p{k}"
        for r in rows(power):
            if k == 0:
                value = probe(r) - (coef(r, 0) * stencil("i0", r) + (1.0 - coef(r, 0)) * warm(r))
            else:
                value = coef(r, 3) * stencil(f"i{k}", r) + coef(r, 4) * get(f"p{k - 1}", r)
            put(power, r, value)
            if k < 3:
                put(f"m{k}", r, coef(r, 0) * value)
        for r in rows(f"i{k + 1}"):
            put(f"i{k + 1}", r, coef(r, 2) * stencil(f"m{k}", r))


def inside_kernel(axes, own, from_odd, from_even, wide, coefs, *held):
    odd_lat, _ = parities(axes)
    held = dict(zip(HELD, held, strict=True))
    lane = lax.broadcasted_iota(jnp.int32, (FIELDS, LANES), 1)
    before, after = sides(odd_lat, from_even[...], from_odd[...])
    for i in range(ROWS):
        turn = (LANES - 8 * i) % LANES
        wide[i, :, 0:LANES] = own[i]
        wide[i, :, LANES:] = jnp.where(lane < 64, pltpu.roll(after, turn, 1), pltpu.roll(before, turn, 1))
        fill_coef(coefs, i, wide[i, 64:65, :], wide[i, 65:66, :], wide[i, 66:67, :])

    def put(name, r, value):
        held[name][r - DEPTH] = value

    march(
        lambda name: range(*INSIDE.get(name, (0, 0))),
        lambda r, n: coefs[r - DEPTH, n : n + 1, :],
        lambda r: wide[r - DEPTH, 0:PROBES, :],
        lambda r: wide[r - DEPTH, PROBES : 2 * PROBES, :],
        lambda name, r: held[name][r - DEPTH],
        put,
    )


def krylov_kernel(axes, own_wide, own_coefs, *refs):
    held = dict(zip(HELD, refs, strict=False))
    from_odd_lon, from_even_lon, sums, basis, images, probe_image, wide, coefs = refs[len(HELD) : len(HELD) + 8]
    fresh = dict(zip(NEEDED, refs[len(HELD) + 8 :], strict=True))
    _, odd_lon = parities(axes)
    lane = lax.broadcasted_iota(jnp.int32, (FIELDS, LANES), 1)
    for side, is_next in ((from_even_lon, odd_lon == 0), (from_odd_lon, odd_lon != 0)):
        start = jnp.where(is_next, DEPTH + ROWS, 0)
        near = jnp.where(is_next, DEPTH + ROWS, 2)
        pair = side[SEND_CORNER:, :]
        for j in range(DEPTH):
            wide[start + j, 0:PROBES, 0:LANES] = side[j * PROBES : (j + 1) * PROBES, :]
            for f in range(3):
                at = SEND_FIELDS + f * DEPTH + j
                wide[start + j, 2 * PROBES + f : 2 * PROBES + f + 1, 0:LANES] = side[at : at + 1, :]
            wide[start + j, :, LANES:] = jnp.where(
                lane < 64, pltpu.roll(pair, (LANES - 8 * j) % LANES, 1), pltpu.roll(pair, (56 - 8 * j) % LANES, 1)
            )
        for j in range(DEPTH - 2):
            at = SEND_PROBES + j * PROBES
            wide[near + j, PROBES : 2 * PROBES, 0:LANES] = side[at : at + PROBES, :]

    def own(r):
        return DEPTH <= r < DEPTH + ROWS

    for r in range(TALL):
        if not own(r):
            fill_coef(coefs, r, wide[r, 64:65, :], wide[r, 65:66, :], wide[r, 66:67, :])

    def rows(name):
        done = range(*INSIDE.get(name, (0, 0)))
        return [r for r in range(*NEEDED.get(name, (0, 0))) if r not in done]

    def get(name, r):
        return held[name][r - DEPTH] if r in range(*INSIDE.get(name, (0, 0))) else fresh[name][r]

    def put(name, r, value):
        fresh[name][r] = value

    def coef(r, n):
        return own_coefs[r - DEPTH, n : n + 1, :] if own(r) else coefs[r, n : n + 1, :]

    def argument(r, at):
        if own(r):
            return own_wide[r - DEPTH, at : at + PROBES, :]
        return wide[r, at : at + PROBES, :]

    march(rows, coef, lambda r: argument(r, 0), lambda r: argument(r, PROBES), get, put)

    total = jnp.zeros((3 * PROBES, 4 * PROBES), jnp.float32)
    for i in range(ROWS):
        r = DEPTH + i
        for k in range(4):
            at = slice(k * PROBES, (k + 1) * PROBES)
            basis[i, at, :] = get(f"p{k}", r)[:, 0:LANES]
            images[i, at, :] = get(f"i{(k + 1) % 4}", r)[:, 0:LANES]
        probe_image[i] = get("up", r)[:, 0:LANES]
        block = basis[i]
        total = total + lax.dot_general(
            block[0 : 3 * PROBES],
            block,
            (((1,), (1,)), ((), ())),
            precision=lax.Precision.HIGH,
            preferred_element_type=jnp.float32,
        )
    lane = lax.broadcasted_iota(jnp.int32, (PROBES, LANES), 1)
    row = lax.broadcasted_iota(jnp.int32, (PROBES, LANES), 0)
    packed = jnp.zeros((PROBES, LANES), jnp.float32)
    for b in range(3):
        even = total[b * PROBES : (b + 1) * PROBES]
        odd = pltpu.roll(even, LANES - PROBES, 1)
        column = lane - b * PROBES
        inside = (column >= 0) & (column < PROBES)
        packed = jnp.where(inside, jnp.where(column >= row, even, odd), packed)
        odd_diagonal = jnp.sum(jnp.where(column == row, odd, 0.0), axis=1, keepdims=True)
        packed = jnp.where(lane == 3 * PROBES + b, odd_diagonal, packed)
    sums[...] = packed


def dot(left, right):
    return jnp.dot(left, right, precision=lax.Precision.HIGH, preferred_element_type=jnp.float32)


def invert_pair(p):
    scale = 1.0 / (p[0][0] * p[1][1] - p[0][1] * p[0][1])
    return p[1][1] * scale, -p[0][1] * scale, p[0][0] * scale


def prepare(p):
    n = len(p)
    if n == 2:
        a, b, c = invert_pair(p)
        return lambda r: [a * r[0] + b * r[1], b * r[0] + c * r[1]]
    h = n // 2
    top = prepare([row[:h] for row in p[:h]])
    side = [row[h:] for row in p[:h]]
    solved = list(zip(*[top([side[i][j] for i in range(h)]) for j in range(h)], strict=True))

    def product(rows, weights):
        terms = [row * weight for row, weight in zip(rows, weights, strict=True)]
        while len(terms) > 1:
            terms = [sum(terms[i : i + 2][1:], terms[i]) for i in range(0, len(terms), 2)]
        return terms[0]

    rest = [[None] * h for _ in range(h)]
    for i in range(h):
        for j in range(i, h):
            rest[i][j] = p[h + i][h + j] - product([side[t][i] for t in range(h)], [solved[t][j] for t in range(h)])
            rest[j][i] = rest[i][j]
    bottom = prepare(rest)

    def solve(r):
        upper = top(r[:h])
        lower = bottom([r[h + i] - product([side[t][i] for t in range(h)], upper) for i in range(h)])
        return [upper[t] - product(solved[t], lower) for t in range(h)] + lower

    return solve


def eliminate(parts):
    row = lax.broadcasted_iota(jnp.int32, (8, LANES), 0)

    def spread(value):
        return jnp.broadcast_to(value, (8, LANES))

    for home in range(len(parts)):
        at = 8 * home
        columns = [[spread(part[:, at + j : at + j + 1]) for j in range(8)] for part in parts]
        pivot = [[spread(columns[home][j][i : i + 1]) for j in range(8)] for i in range(8)]
        solved = prepare(pivot)([spread(parts[home][i : i + 1]) for i in range(8)])
        for v, column in enumerate(columns):
            if v == home:
                part = solved[0]
                for i in range(1, 8):
                    part = jnp.where(row == i, solved[i], part)
                parts[v] = part
            else:
                terms = [c * x for c, x in zip(column, solved, strict=True)]
                parts[v] = parts[v] - (
                    ((terms[0] + terms[1]) + (terms[2] + terms[3])) + ((terms[4] + terms[5]) + (terms[6] + terms[7]))
                )
    return parts


def finish_kernel(
    sums, own, basis, images, probe_image,
    solution_out, residual_out, grad_out,
    coeffs,
):
    packed = sums[...]
    flipped = packed.T
    lane = lax.broadcasted_iota(jnp.int32, (PROBES, PROBES), 1)
    row = lax.broadcasted_iota(jnp.int32, (PROBES, PROBES), 0)
    moments = []
    for b in range(3):
        block = packed[:, b * PROBES : (b + 1) * PROBES]
        mirror = flipped[b * PROBES : (b + 1) * PROBES, :]
        moments.append(jnp.where(lane >= row, block, mirror))
        odd = jnp.where(lane < row, block, mirror)
        moments.append(jnp.where(lane == row, packed[:, 3 * PROBES + b : 3 * PROBES + b + 1], odd))
    power = [moments[k + 1] * (1.0 / GAIN) + moments[k] * SHIFT for k in range(5)]

    table = jnp.concatenate(
        [jnp.concatenate([power[b], power[b + 1], power[b + 2], moments[b]], axis=1) for b in range(3)], axis=0
    )
    parts = eliminate([table[8 * v : 8 * v + 8] for v in range(12)])
    solved = jnp.concatenate(parts, axis=0)

    nothing = jnp.zeros((PROBES, LANES), jnp.float32)
    wide_lane = lax.broadcasted_iota(jnp.int32, (4 * PROBES, LANES), 1)
    wide_row = lax.broadcasted_iota(jnp.int32, (4 * PROBES, LANES), 0)
    one = (wide_lane == wide_row + 3 * PROBES).astype(jnp.float32)
    kept = jnp.concatenate([solved, nothing], axis=0)
    left = one - SHIFT * kept - (1.0 / GAIN) * jnp.concatenate([nothing, solved], axis=0)
    columns = jnp.where(wide_lane < PROBES, pltpu.roll(kept, PROBES, 1), pltpu.roll(left, 2 * PROBES, 1))
    coeffs[...] = columns.T[0 : 2 * PROBES]
    weights = coeffs[0:PROBES, :] + one[0:PROBES]

    for i in range(ROWS):
        both = dot(coeffs[...], basis[i])
        values = both[0:PROBES] + own[i, 0:PROBES, :]
        solution_out[:, i, :] = values
        residual_out[:, i, :] = both[PROBES:]
        image = dot(weights, images[i])
        terms = values * probe_image[i] + image * own[i, PROBES : 2 * PROBES, :]
        wet = own[i, 64:65, :]
        grad_out[i : i + 1, :] = wet * (jnp.sum(terms, axis=0, keepdims=True) * (1.0 / PROBES))


def f32(*shape):
    return jax.ShapeDtypeStruct(shape, jnp.float32)


def exchanged(value, axes, odd, wrap):
    size = lax.axis_size(axes)
    pairs = []
    for i in range(size):
        other = ((i + odd) ^ 1) - odd
        if wrap or 0 <= other < size:
            pairs.append((i, other % size))
    return lax.ppermute(value, axes, pairs)


def spread_sum(value, axes):
    size = lax.axis_size(axes)
    copies = jnp.broadcast_to(value[None], (size,) + value.shape)
    return jnp.sum(lax.all_to_all(copies, axes, 0, 0), axis=0)


def make_local(lat, lon, stages):
    axes = (lat[-1], lon[-1])

    def local(warm_start, probe_signs, ocean_mask, kappa_sq, scale_field):
        args = (warm_start, probe_signs, ocean_mask, kappa_sq, scale_field)
        own, fields, to_odd, to_even = pl.pallas_call(
            functools.partial(pack_kernel, axes),
            out_shape=(
                f32(ROWS, FIELDS, LANES),
                f32(3, ROWS, LANES),
                f32(FIELDS, LANES),
                f32(FIELDS, LANES),
            ),
            in_specs=[pl.BlockSpec(memory_space=pltpu.HBM)] * 5,
            scratch_shapes=[pltpu.VMEM(x.shape, x.dtype) for x in args] + [pltpu.SemaphoreType.DMA((5,))],
            compiler_params=ALL_PARAMS,
            name="pack_edges",
        )(*args)
        odd_lat = exchanged(to_odd, lat, 1, False)
        even_lat = exchanged(to_even, lat, 0, False)
        to_odd, to_even = pl.pallas_call(
            functools.partial(send_kernel, axes),
            out_shape=(f32(SEND_ROWS, LANES), f32(SEND_ROWS, LANES)),
            compiler_params=PARAMS,
            name="pack_rows",
        )(own, fields, odd_lat, even_lat)
        odd_lon = exchanged(to_odd, lon, 1, True)
        even_lon = exchanged(to_even, lon, 0, True)
        inside = pl.pallas_call(
            functools.partial(inside_kernel, axes),
            out_shape=(f32(ROWS, FIELDS, 2 * LANES), f32(ROWS, 8, 2 * LANES))
            + (f32(ROWS, PROBES, 2 * LANES),) * len(HELD),
            compiler_params=PARAMS,
            cost_estimate=pl.CostEstimate(flops=40_000_000, bytes_accessed=8_000_000, transcendentals=0),
            name="inside_rows",
        )(own, odd_lat, even_lat)
        sums, basis, images, probe_image = pl.pallas_call(
            functools.partial(krylov_kernel, axes),
            out_shape=(
                f32(PROBES, LANES),
                f32(ROWS, 4 * PROBES, LANES),
                f32(ROWS, 4 * PROBES, LANES),
                f32(ROWS, PROBES, LANES),
            ),
            scratch_shapes=[
                pltpu.VMEM((TALL, FIELDS, 2 * LANES), jnp.float32),
                pltpu.VMEM((TALL, 8, 2 * LANES), jnp.float32),
            ]
            + [pltpu.VMEM((TALL, PROBES, 2 * LANES), jnp.float32)] * len(NEEDED),
            compiler_params=PARAMS,
            name="krylov_moments",
        )(*inside, odd_lon, even_lon)
        with jax.named_scope("sum_moments"):
            for group in stages:
                sums = spread_sum(sums, group)
        return pl.pallas_call(
            finish_kernel,
            out_shape=(
                f32(PROBES, ROWS, LANES),
                f32(PROBES, ROWS, LANES),
                f32(ROWS, LANES),
            ),
            scratch_shapes=[pltpu.VMEM((2 * PROBES, 4 * PROBES), jnp.float32)],
            compiler_params=PARAMS,
            name="solve_and_combine",
        )(sums, own, basis, images, probe_image)

    return local


def solution(mesh):
    if mesh.devices.shape == (16, 32):
        grid = Mesh(mesh.devices.reshape(2, 4, 2, 4, 8), ("zh", "x", "c", "zl", "y"))
        lat, lon = (("zh", "x", "c"), ("zl", "y"))
        stages = (("x", "c"), ("y",), ("zh", "zl"))
    else:
        grid, lat, lon, stages = (mesh, ("lat",), ("lon",), (("lat",), ("lon",)))
    return jax.shard_map(
        make_local(lat, lon, stages),
        mesh=grid,
        in_specs=(P(None, lon, lat), P(None, lon, lat), P(lon, lat), P(lon, lat), P(lon, lat)),
        out_specs=(P(None, lon, lat), P(None, lon, lat), P(lon, lat)),
        check_vma=False,
    )
```

time: 87 us -> 81 us (0.931)
  blocking collectives: 40.9 us -> 38.7 us
  local copies, waits for them, and re-layouts: 4.02 us -> 1.84 us
  starting transfers between devices: 19.6 us -> 18.1 us
    all_to_all x3, blocking collectives: 40.9 us -> 38.7 us  [spread_sum(): return jnp.sum(lax.all_to_all(copies, axes, 0, 0), axis=0)]
    unnamed x10 -> x6, local copies, waits for them, and re-layouts: 3.98 us -> 1.8 us
    pallas_call x1, Pallas kernels: 0.66 us -> 2.37 us  [local(): pl.pallas_call(functools.partial(pack_kernel, axes), out_shape=(f32(ROWS,...]
    pallas_call x0 -> x1, Pallas kernels: none -> 1.69 us  [local(): pl.pallas_call(functools.partial(inside_kernel, axes), out_shape=(f32(ROW...]
    pallas_call x1, Pallas kernels: 4.65 us -> 3.16 us  [local(): pl.pallas_call(functools.partial(krylov_kernel, axes), out_shape=(f32(PRO...]
    ppermute x4, starting transfers between devices: 19.6 us -> 18.1 us  [exchanged(): return lax.ppermute(value, axes, pairs)]
    pallas_call x1, Pallas kernels: 7.1 us -> 5.83 us  [local(): pl.pallas_call(finish_kernel, out_shape=(f32(PROBES, ROWS, LANES), f32(PR...]
  transfers between devices with their start and end apart: 4 -> 4, of which waited for: 2 -> 3; matrix products, arithmetic and copies ran while one was open for 0% -> 0% of each run, Pallas kernels for 0% -> 2%
where the time goes in v4:
time: 81 us; the launch traced here: 80.5 us
  blocking collectives  38.7 us (48%)
  starting transfers between devices  18.1 us (22%)
  Pallas kernels  13.1 us (16%)
  waiting for transfers between devices  7.95 us (10%)
  local copies, waits for them, and re-layouts  1.84 us (2%)
    all_to_all x3, blocking collectives, spread_sum(): return jnp.sum(lax.all_to_all(copies, axes, 0, 0), axis=0)  38.7 us
    ppermute x4, starting transfers between devices, exchanged(): return lax.ppermute(value, axes, pairs)  18.1 us
    ppermute x4, waiting for transfers between devices, exchanged(): return lax.ppermute(value, axes, pairs)  7.95 us
    pallas_call x1, Pallas kernels, local(): pl.pallas_call(finish_kernel, out_shape=(f32(PROBES, ROWS, LANES), f32(PR...  5.83 us
    pallas_call x1, Pallas kernels, local(): pl.pallas_call(functools.partial(krylov_kernel, axes), out_shape=(f32(PRO...  3.16 us
    pallas_call x1, Pallas kernels, local(): pl.pallas_call(functools.partial(pack_kernel, axes), out_shape=(f32(ROWS,...  2.37 us
    unnamed x6, local copies, waits for them, and re-layouts  1.8 us
    pallas_call x1, Pallas kernels, local(): pl.pallas_call(functools.partial(inside_kernel, axes), out_shape=(f32(ROW...  1.69 us
  transfers between devices with their start and end apart: 4, of which 3 were waited for; matrix products, arithmetic and copies ran while one was open for 0% of the time, Pallas kernels for 2%

profile of v4, /device:TPU:2, one launch (start us, length us, event | category | flops | bytes accessed | tf_op | source)
XLA Modules:
  0.0 80.5 jit_solution(12463117695844167430)
XLA Ops:
  0.6 2.4 %pack_edges.1 = (f32[16,72,128]{2,1,0:T(8,128)}, f32[3,16,128]{2,1,0:T(8,128)}, f32[72,128]{1,0:T(8,128)}, f32[72,128]{1,0:T(8,128)}) custom-call(f32[32,16,128]{2,1,0:T(8,128)} %warm_hbm.1, s32[32,16,128]{2,1,0:T(8,128)} %signs_hbm.1, s32[16,128]{1,0:T(8,128)} %mask_hbm.1, f32[16,128]{1,0:T(8,128)} %kappa_hbm.1, f32[16,128]{1,0:T(8,128)} %scale_hbm.1), custom_call_target="tpu_custom_call" | custom-call | tf_op jit(solution)/shard_map/pack_edges/pallas_call | solution.py:374
  3.0 1.9 %collective-permute-start = (f32[72,128]{1,0:T(8,128)}, f32[72,128]{1,0:T(8,128)S(1)}, u32[]{:S(2)}, u32[]{:S(2)}) collective-permute-start(f32[72,128]{1,0:T(8,128)} %get-tuple-element.29), channel_id=1, source_target_pairs={{32,64},{64,32},{96,128},{128,96},{160,192},{192,160},{224,256},{2... | collective-permute-start | bytes 110600 | tf_op jit(solution)/shard_map/ppermute | solution.py:360
  4.9 3.5 %collective-permute-start.1 = (f32[72,128]{1,0:T(8,128)}, f32[72,128]{1,0:T(8,128)S(1)}, u32[]{:S(2)}, u32[]{:S(2)}) collective-permute-start(f32[72,128]{1,0:T(8,128)} %get-tuple-element.30), channel_id=1, source_target_pairs={{0,32},{32,0},{64,96},{96,64},{128,160},{160,128},{192,224},{224,1... | collective-permute-start | bytes 110600 | tf_op jit(solution)/shard_map/ppermute | solution.py:360
  8.4 0.0 collective-permute-done.from_odd
  8.5 1.0 %collective-permute-done.1.from_even = f32[72,128]{1,0:T(8,128)S(1)} collective-permute-done((f32[72,128]{1,0:T(8,128)}, f32[72,128]{1,0:T(8,128)S(1)}, u32[]{:S(2)}, u32[]{:S(2)}) %collective-permute-start.1) | collective-permute-done | bytes 36896 | tf_op jit(solution)/shard_map/ppermute | solution.py:360
  9.5 0.0 copy-start
  9.5 1.1 %copy-done = f32[16,72,128]{2,1,0:T(8,128)S(1)} copy-done((f32[16,72,128]{2,1,0:T(8,128)S(1)}, f32[16,72,128]{2,1,0:T(8,128)}, u32[]{:S(2)}) %copy-start) | copy-done | bytes 589848
  10.6 0.0 copy-start.2
  10.6 0.7 copy-done.2
  11.3 0.1 pack_rows.1
  11.4 10.8 %collective-permute-start.2 = (f32[544,128]{1,0:T(8,128)S(1)}, f32[544,128]{1,0:T(8,128)S(1)}, u32[]{:S(2)}, u32[]{:S(2)}) collective-permute-start(f32[544,128]{1,0:T(8,128)S(1)} %get-tuple-element.47), channel_id=1, source_target_pairs={{0,31},{1,2},{2,1},{3,4},{4,3},{5,6},{6,5},{7,8},{8,7},{9,10},{10,... | collective-permute-start | bytes 835592 | tf_op jit(solution)/shard_map/ppermute | solution.py:360
  22.2 1.9 %collective-permute-start.3 = (f32[544,128]{1,0:T(8,128)S(1)}, f32[544,128]{1,0:T(8,128)S(1)}, u32[]{:S(2)}, u32[]{:S(2)}) collective-permute-start(f32[544,128]{1,0:T(8,128)S(1)} %get-tuple-element.48), channel_id=1, source_target_pairs={{0,1},{1,0},{2,3},{3,2},{4,5},{5,4},{6,7},{7,6},{8,9},{9,8},{10,11... | collective-permute-start | bytes 835592 | tf_op jit(solution)/shard_map/ppermute | solution.py:360
  24.1 1.7 %inside_rows.1 = (f32[16,72,256]{2,1,0:T(8,128)S(1)}, f32[16,8,256]{2,1,0:T(8,128)S(1)}, f32[16,32,256]{2,1,0:T(8,128)S(1)}, f32[16,32,256]{2,1,0:T(8,128)S(1)},...) custom-call(f32[16,72,128]{2,1,0:T(8,128)S(1)} %copy-done, ...), custom_call_target="tpu_custom_call" | custom-call | flops 40000000 | bytes 8000000 | tf_op jit(solution)/shard_map/inside_rows/pallas_call | solution.py:397
  25.9 3.5 %collective-permute-done.2.refs_13_ = f32[544,128]{1,0:T(8,128)S(1)} collective-permute-done((f32[544,128]{1,0:T(8,128)S(1)}, f32[544,128]{1,0:T(8,128)S(1)}, u32[]{:S(2)}, u32[]{:S(2)}) %collective-permute-start.2) | collective-permute-done | bytes 278560 | tf_op jit(solution)/shard_map/ppermute | solution.py:360
  29.4 3.4 %collective-permute-done.3.refs_14_ = f32[544,128]{1,0:T(8,128)S(1)} collective-permute-done((f32[544,128]{1,0:T(8,128)S(1)}, f32[544,128]{1,0:T(8,128)S(1)}, u32[]{:S(2)}, u32[]{:S(2)}) %collective-permute-start.3) | collective-permute-done | bytes 278560 | tf_op jit(solution)/shard_map/ppermute | solution.py:360
  32.7 3.2 %krylov_moments.1 = (f32[32,128]{1,0:T(8,128)S(1)}, f32[16,128,128]{2,1,0:T(8,128)S(1)}, f32[16,128,128]{2,1,0:T(8,128)S(1)}, f32[16,32,128]{2,1,0:T(8,128)S(1)}) custom-call(f32[16,72,256]{2,1,0:T(8,128)S(1)} %get-tuple-element.31.own_wide, f32[16,8,256]{2,1,0:T(8,128)S(1)} %get-tuple-element.32.own_coefs, f32[16,32,256]{2,1,0:T(8,128)S(1)} %get-tuple-element.33.refs_0_, ...), custom_call_target="tpu_custom_call" | custom-call | tf_op jit(solution)/shard_map/krylov_moments/pallas_call | solution.py:405
  35.9 0.0 copy-start.1
  35.9 13.9 %all_to_all.15 = f32[8,32,128]{2,1,0:T(8,128)S(1)} all-to-all(f32[8,32,128]{2,1,0:T(8,128)S(1)} %broadcast_in_dim.6), channel_id=1, replica_groups=mesh['zh'=2,'x'=4,'c'=2,'zl'=4,'y'=8] {'x','c'}, dimensions={0} | all-to-all | bytes 262144 | tf_op jit(solution)/shard_map/sum_moments/all_to_all | solution.py:366
  49.9 11.5 %all_to_all.16 = f32[8,32,128]{2,1,0:T(8,128)S(1)} all-to-all(f32[8,32,128]{2,1,0:T(8,128)S(1)} %broadcast_in_dim.7), channel_id=1, replica_groups=mesh['zh'=2,'x'=4,'c'=2,'zl'=4,'y'=8] {'y'}, dimensions={0} | all-to-all | bytes 262144 | tf_op jit(solution)/shard_map/sum_moments/all_to_all | solution.py:366
  61.5 13.2 %all_to_all.17 = f32[8,32,128]{2,1,0:T(8,128)S(1)} all-to-all(f32[8,32,128]{2,1,0:T(8,128)S(1)} %broadcast_in_dim.8), channel_id=1, replica_groups=mesh['zh'=2,'x'=4,'c'=2,'zl'=4,'y'=8] {'zh','zl'}, dimensions={0} | all-to-all | bytes 262144 | tf_op jit(solution)/shard_map/sum_moments/all_to_all | solution.py:366
  74.7 0.0 copy-done.1
  74.7 5.8 %solve_and_combine.1 = (f32[32,16,128]{2,1,0:T(8,128)}, f32[32,16,128]{2,1,0:T(8,128)}, f32[16,128]{1,0:T(8,128)}) custom-call(f32[32,128]{1,0:T(8,128)S(1)} %reduce_sum.29.sums, f32[16,72,128]{2,1,0:T(8,128)S(1)} %copy-done.1, f32[16,128,128]{2,1,0:T(8,128)S(1)} %get-tuple-element.50.basis, f32[16,128,128]{2,1,0:T(8,128)S(1)} %get-tuple-element.51.images, ...), custom_call_target="tpu_custom_call" | custom-call | tf_op jit(solution)/shard_map/solve_and_combine/pallas_call | solution.py:424
  (6 shorter events, 0.1 us)
Async XLA Ops:
  3.0 5.5 %collective-permute-start = (f32[72,128]{1,0:T(8,128)}, f32[72,128]{1,0:T(8,128)S(1)}, u32[]{:S(2)}, u32[]{:S(2)}) collective-permute-start(f32[72,128]{1,0:T(8,128)} %get-tuple-element.29), channel_id=1, source_target_pairs={{32,64},{64,32},{96,128},{128,96},{160,192},{192,160},{224,256},{2... | collective-permute-start | bytes 110600 | tf_op jit(solution)/shard_map/ppermute | solution.py:360
  4.9 4.6 %collective-permute-start.1 = (f32[72,128]{1,0:T(8,128)}, f32[72,128]{1,0:T(8,128)S(1)}, u32[]{:S(2)}, u32[]{:S(2)}) collective-permute-start(f32[72,128]{1,0:T(8,128)} %get-tuple-element.30), channel_id=1, source_target_pairs={{0,32},{32,0},{64,96},{96,64},{128,160},{160,128},{192,224},{224,1... | collective-permute-start | bytes 110600 | tf_op jit(solution)/shard_map/ppermute | solution.py:360
  9.5 1.1 %copy-start = (f32[16,72,128]{2,1,0:T(8,128)S(1)}, f32[16,72,128]{2,1,0:T(8,128)}, u32[]{:S(2)}) copy-start(f32[16,72,128]{2,1,0:T(8,128)} %get-tuple-element.28.own) | copy-start | bytes 1769476
  10.6 0.7 copy-start.2
  11.4 18.0 %collective-permute-start.2 = (f32[544,128]{1,0:T(8,128)S(1)}, f32[544,128]{1,0:T(8,128)S(1)}, u32[]{:S(2)}, u32[]{:S(2)}) collective-permute-start(f32[544,128]{1,0:T(8,128)S(1)} %get-tuple-element.47), channel_id=1, source_target_pairs={{0,31},{1,2},{2,1},{3,4},{4,3},{5,6},{6,5},{7,8},{8,7},{9,10},{10,... | collective-permute-start | bytes 835592 | tf_op jit(solution)/shard_map/ppermute | solution.py:360
  22.2 10.5 %collective-permute-start.3 = (f32[544,128]{1,0:T(8,128)S(1)}, f32[544,128]{1,0:T(8,128)S(1)}, u32[]{:S(2)}, u32[]{:S(2)}) collective-permute-start(f32[544,128]{1,0:T(8,128)S(1)} %get-tuple-element.48), channel_id=1, source_target_pairs={{0,1},{1,0},{2,3},{3,2},{4,5},{5,4},{6,7},{7,6},{8,9},{9,8},{10,11... | collective-permute-start | bytes 835592 | tf_op jit(solution)/shard_map/ppermute | solution.py:360
  35.9 38.8 %copy-start.1 = (f32[16,72,128]{2,1,0:T(8,128)S(1)}, f32[16,72,128]{2,1,0:T(8,128)}, u32[]{:S(2)}) copy-start(f32[16,72,128]{2,1,0:T(8,128)} %get-tuple-element.28.own) | copy-start | bytes 1769476

commit v5 on v4

--- a/solution.py
+++ b/solution.py
@@ -13,10 +13,9 @@
 ROWS = 16
 LANES = 128
 FIELDS = 72
-SHIFT = 4.0
+SHIFT = 1.2
 GAIN = 0.25
 PARAMS = pltpu.CompilerParams(vmem_limit_bytes=32 * 1024 * 1024)
-ALL_PARAMS = pltpu.CompilerParams(vmem_limit_bytes=60 * 1024 * 1024)
 
 
 def parities(axes):
@@ -219,7 +218,7 @@
             block[0 : 3 * PROBES],
             block,
             (((1,), (1,)), ((), ())),
-            precision=lax.Precision.HIGH,
+            precision=lax.Precision.HIGHEST,
             preferred_element_type=jnp.float32,
         )
     lane = lax.broadcasted_iota(jnp.int32, (PROBES, LANES), 1)
@@ -236,8 +235,8 @@
     sums[...] = packed
 
 
-def dot(left, right):
-    return jnp.dot(left, right, precision=lax.Precision.HIGH, preferred_element_type=jnp.float32)
+def dot(left, right, precision):
+    return jnp.dot(left, right, precision=precision, preferred_element_type=jnp.float32)
 
 
 def invert_pair(p):
@@ -336,11 +335,11 @@
     weights = coeffs[0:PROBES, :] + one[0:PROBES]
 
     for i in range(ROWS):
-        both = dot(coeffs[...], basis[i])
+        both = dot(coeffs[...], basis[i], lax.Precision.HIGHEST)
         values = both[0:PROBES] + own[i, 0:PROBES, :]
         solution_out[:, i, :] = values
         residual_out[:, i, :] = both[PROBES:]
-        image = dot(weights, images[i])
+        image = dot(weights, images[i], lax.Precision.HIGH)
         terms = values * probe_image[i] + image * own[i, PROBES : 2 * PROBES, :]
         wet = own[i, 64:65, :]
         grad_out[i : i + 1, :] = wet * (jnp.sum(terms, axis=0, keepdims=True) * (1.0 / PROBES))
@@ -381,9 +380,9 @@
             ),
             in_specs=[pl.BlockSpec(memory_space=pltpu.HBM)] * 5,
             scratch_shapes=[pltpu.VMEM(x.shape, x.dtype) for x in args] + [pltpu.SemaphoreType.DMA((5,))],
-            compiler_params=ALL_PARAMS,
+            compiler_params=PARAMS,
             name="pack_edges",
-        )(*args)
+        )(*(pltpu.with_memory_space_constraint(x, pltpu.HBM) for x in args))
         odd_lat = exchanged(to_odd, lat, 1, False)
         even_lat = exchanged(to_even, lat, 0, False)
         to_odd, to_even = pl.pallas_call(

time: 81 us -> 79.6 us (0.983)
  local copies, waits for them, and re-layouts: 1.84 us -> 0.03 us
  Pallas kernels: 13.1 us -> 14 us
    unnamed x6 -> x0, local copies, waits for them, and re-layouts: 1.8 us -> none
    pallas_call x1, Pallas kernels: 5.83 us -> 6.94 us  [local(): pl.pallas_call(finish_kernel, out_shape=(f32(PROBES, ROWS, LANES), f32(PR...]
where the time goes in v5:
time: 79.6 us; the launch traced here: 79.3 us
  blocking collectives  38.5 us (48%)
  starting transfers between devices  18.1 us (23%)
  Pallas kernels  14 us (18%)
  waiting for transfers between devices  7.73 us (10%)
    all_to_all x3, blocking collectives, spread_sum(): return jnp.sum(lax.all_to_all(copies, axes, 0, 0), axis=0)  38.5 us
    ppermute x4, starting transfers between devices, exchanged(): return lax.ppermute(value, axes, pairs)  18.1 us
    ppermute x4, waiting for transfers between devices, exchanged(): return lax.ppermute(value, axes, pairs)  7.73 us
    pallas_call x1, Pallas kernels, local(): pl.pallas_call(finish_kernel, out_shape=(f32(PROBES, ROWS, LANES), f32(PR...  6.94 us
    pallas_call x1, Pallas kernels, local(): pl.pallas_call(functools.partial(krylov_kernel, axes), out_shape=(f32(PRO...  3.68 us
    pallas_call x1, Pallas kernels, local(): pl.pallas_call(functools.partial(inside_kernel, axes), out_shape=(f32(ROW...  1.69 us
    pallas_call x1, Pallas kernels, local(): pl.pallas_call(functools.partial(pack_kernel, axes), out_shape=(f32(ROWS,...  1.62 us
  transfers between devices with their start and end apart: 4, of which 3 were waited for; matrix products, arithmetic and copies ran while one was open for 0% of the time, Pallas kernels for 2%

profile of v5, /device:TPU:2, one launch (start us, length us, event | category | flops | bytes accessed | tf_op | source)
XLA Modules:
  0.0 79.3 jit_solution(14839177524264472391)
XLA Ops:
  0.6 1.6 %pack_edges.1 = (f32[16,72,128]{2,1,0:T(8,128)S(1)}, f32[3,16,128]{2,1,0:T(8,128)S(1)}, f32[72,128]{1,0:T(8,128)S(1)}, f32[72,128]{1,0:T(8,128)S(1)}) custom-call(f32[32,16,128]{2,1,0:T(8,128)} %warm_hbm.1, s32[32,16,128]{2,1,0:T(8,128)} %signs_hbm.1, s32[16,128]{1,0:T(8,128)} %mask_hbm.1, f32[16,128]{1,0:T(8,128)} %kappa_hbm.1, f32[16,128]{1,0:T(8,128)} %scale_hbm.1), custom_call_target="tpu_custom_call" | custom-call | tf_op jit(solution)/shard_map/pack_edges/pallas_call | solution.py:373
  2.3 1.9 %collective-permute-start = (f32[72,128]{1,0:T(8,128)S(1)}, f32[72,128]{1,0:T(8,128)S(1)}, u32[]{:S(2)}, u32[]{:S(2)}) collective-permute-start(f32[72,128]{1,0:T(8,128)S(1)} %get-tuple-element.29), channel_id=1, source_target_pairs={{32,64},{64,32},{96,128},{128,96},{160,192},{192,160},{224,256},{2... | collective-permute-start | bytes 110600 | tf_op jit(solution)/shard_map/ppermute | solution.py:359
  4.2 3.5 %collective-permute-start.1 = (f32[72,128]{1,0:T(8,128)S(1)}, f32[72,128]{1,0:T(8,128)S(1)}, u32[]{:S(2)}, u32[]{:S(2)}) collective-permute-start(f32[72,128]{1,0:T(8,128)S(1)} %get-tuple-element.30), channel_id=1, source_target_pairs={{0,32},{32,0},{64,96},{96,64},{128,160},{160,128},{192,224},{224,1... | collective-permute-start | bytes 110600 | tf_op jit(solution)/shard_map/ppermute | solution.py:359
  7.7 0.0 collective-permute-done.from_odd
  7.7 0.8 %collective-permute-done.1.from_even = f32[72,128]{1,0:T(8,128)S(1)} collective-permute-done((f32[72,128]{1,0:T(8,128)S(1)}, f32[72,128]{1,0:T(8,128)S(1)}, u32[]{:S(2)}, u32[]{:S(2)}) %collective-permute-start.1) | collective-permute-done | bytes 36896 | tf_op jit(solution)/shard_map/ppermute | solution.py:359
  8.5 0.1 pack_rows.1
  8.6 10.8 %collective-permute-start.2 = (f32[544,128]{1,0:T(8,128)S(1)}, f32[544,128]{1,0:T(8,128)S(1)}, u32[]{:S(2)}, u32[]{:S(2)}) collective-permute-start(f32[544,128]{1,0:T(8,128)S(1)} %get-tuple-element.47), channel_id=1, source_target_pairs={{0,31},{1,2},{2,1},{3,4},{4,3},{5,6},{6,5},{7,8},{8,7},{9,10},{10,... | collective-permute-start | bytes 835592 | tf_op jit(solution)/shard_map/ppermute | solution.py:359
  19.5 1.9 %collective-permute-start.3 = (f32[544,128]{1,0:T(8,128)S(1)}, f32[544,128]{1,0:T(8,128)S(1)}, u32[]{:S(2)}, u32[]{:S(2)}) collective-permute-start(f32[544,128]{1,0:T(8,128)S(1)} %get-tuple-element.48), channel_id=1, source_target_pairs={{0,1},{1,0},{2,3},{3,2},{4,5},{5,4},{6,7},{7,6},{8,9},{9,8},{10,11... | collective-permute-start | bytes 835592 | tf_op jit(solution)/shard_map/ppermute | solution.py:359
  21.4 1.7 %inside_rows.1 = (f32[16,72,256]{2,1,0:T(8,128)S(1)}, f32[16,8,256]{2,1,0:T(8,128)S(1)}, f32[16,32,256]{2,1,0:T(8,128)S(1)}, f32[16,32,256]{2,1,0:T(8,128)S(1)},...) custom-call(f32[16,72,128]{2,1,0:T(8,128)S(1)} %get-tuple-element.28, ...), custom_call_target="tpu_custom_call" | custom-call | flops 40000000 | bytes 8000000 | tf_op jit(solution)/shard_map/inside_rows/pallas_call | solution.py:396
  23.1 3.5 %collective-permute-done.2.refs_13_ = f32[544,128]{1,0:T(8,128)S(1)} collective-permute-done((f32[544,128]{1,0:T(8,128)S(1)}, f32[544,128]{1,0:T(8,128)S(1)}, u32[]{:S(2)}, u32[]{:S(2)}) %collective-permute-start.2) | collective-permute-done | bytes 278560 | tf_op jit(solution)/shard_map/ppermute | solution.py:359
  26.6 3.4 %collective-permute-done.3.refs_14_ = f32[544,128]{1,0:T(8,128)S(1)} collective-permute-done((f32[544,128]{1,0:T(8,128)S(1)}, f32[544,128]{1,0:T(8,128)S(1)}, u32[]{:S(2)}, u32[]{:S(2)}) %collective-permute-start.3) | collective-permute-done | bytes 278560 | tf_op jit(solution)/shard_map/ppermute | solution.py:359
  30.0 3.7 %krylov_moments.1 = (f32[32,128]{1,0:T(8,128)S(1)}, f32[16,128,128]{2,1,0:T(8,128)S(1)}, f32[16,128,128]{2,1,0:T(8,128)S(1)}, f32[16,32,128]{2,1,0:T(8,128)S(1)}) custom-call(f32[16,72,256]{2,1,0:T(8,128)S(1)} %get-tuple-element.31.own_wide, f32[16,8,256]{2,1,0:T(8,128)S(1)} %get-tuple-element.32.own_coefs, f32[16,32,256]{2,1,0:T(8,128)S(1)} %get-tuple-element.33.refs_0_, ...), custom_call_target="tpu_custom_call" | custom-call | tf_op jit(solution)/shard_map/krylov_moments/pallas_call | solution.py:404
  33.7 13.8 %all_to_all.15 = f32[8,32,128]{2,1,0:T(8,128)S(1)} all-to-all(f32[8,32,128]{2,1,0:T(8,128)S(1)} %broadcast_in_dim.6), channel_id=1, replica_groups=mesh['zh'=2,'x'=4,'c'=2,'zl'=4,'y'=8] {'x','c'}, dimensions={0} | all-to-all | bytes 262144 | tf_op jit(solution)/shard_map/sum_moments/all_to_all | solution.py:365
  47.5 11.5 %all_to_all.16 = f32[8,32,128]{2,1,0:T(8,128)S(1)} all-to-all(f32[8,32,128]{2,1,0:T(8,128)S(1)} %broadcast_in_dim.7), channel_id=1, replica_groups=mesh['zh'=2,'x'=4,'c'=2,'zl'=4,'y'=8] {'y'}, dimensions={0} | all-to-all | bytes 262144 | tf_op jit(solution)/shard_map/sum_moments/all_to_all | solution.py:365
  59.1 13.2 %all_to_all.17 = f32[8,32,128]{2,1,0:T(8,128)S(1)} all-to-all(f32[8,32,128]{2,1,0:T(8,128)S(1)} %broadcast_in_dim.8), channel_id=1, replica_groups=mesh['zh'=2,'x'=4,'c'=2,'zl'=4,'y'=8] {'zh','zl'}, dimensions={0} | all-to-all | bytes 262144 | tf_op jit(solution)/shard_map/sum_moments/all_to_all | solution.py:365
  72.3 6.9 %solve_and_combine.1 = (f32[32,16,128]{2,1,0:T(8,128)}, f32[32,16,128]{2,1,0:T(8,128)}, f32[16,128]{1,0:T(8,128)}) custom-call(f32[32,128]{1,0:T(8,128)S(1)} %reduce_sum.29.sums, f32[16,72,128]{2,1,0:T(8,128)S(1)} %get-tuple-element.28.own, f32[16,128,128]{2,1,0:T(8,128)S(1)} %get-tuple-element.50.basis, f32[16,128,128]{2,1,0:T(8,128)S(1)} %get-tuple-element.51.images, ...), custom_call_target="tpu_custom_call" | custom-call | tf_op jit(solution)/shard_map/solve_and_combine/pallas_call | solution.py:423
  (6 shorter events, 0.1 us)
Async XLA Ops:
  2.3 5.4 %collective-permute-start = (f32[72,128]{1,0:T(8,128)S(1)}, f32[72,128]{1,0:T(8,128)S(1)}, u32[]{:S(2)}, u32[]{:S(2)}) collective-permute-start(f32[72,128]{1,0:T(8,128)S(1)} %get-tuple-element.29), channel_id=1, source_target_pairs={{32,64},{64,32},{96,128},{128,96},{160,192},{192,160},{224,256},{2... | collective-permute-start | bytes 110600 | tf_op jit(solution)/shard_map/ppermute | solution.py:359
  4.2 4.4 %collective-permute-start.1 = (f32[72,128]{1,0:T(8,128)S(1)}, f32[72,128]{1,0:T(8,128)S(1)}, u32[]{:S(2)}, u32[]{:S(2)}) collective-permute-start(f32[72,128]{1,0:T(8,128)S(1)} %get-tuple-element.30), channel_id=1, source_target_pairs={{0,32},{32,0},{64,96},{96,64},{128,160},{160,128},{192,224},{224,1... | collective-permute-start | bytes 110600 | tf_op jit(solution)/shard_map/ppermute | solution.py:359
  8.6 18.0 %collective-permute-start.2 = (f32[544,128]{1,0:T(8,128)S(1)}, f32[544,128]{1,0:T(8,128)S(1)}, u32[]{:S(2)}, u32[]{:S(2)}) collective-permute-start(f32[544,128]{1,0:T(8,128)S(1)} %get-tuple-element.47), channel_id=1, source_target_pairs={{0,31},{1,2},{2,1},{3,4},{4,3},{5,6},{6,5},{7,8},{8,7},{9,10},{10,... | collective-permute-start | bytes 835592 | tf_op jit(solution)/shard_map/ppermute | solution.py:359
  19.5 10.5 %collective-permute-start.3 = (f32[544,128]{1,0:T(8,128)S(1)}, f32[544,128]{1,0:T(8,128)S(1)}, u32[]{:S(2)}, u32[]{:S(2)}) collective-permute-start(f32[544,128]{1,0:T(8,128)S(1)} %get-tuple-element.48), channel_id=1, source_target_pairs={{0,1},{1,0},{2,3},{3,2},{4,5},{5,4},{6,7},{7,6},{8,9},{9,8},{10,11... | collective-permute-start | bytes 835592 | tf_op jit(solution)/shard_map/ppermute | solution.py:359

commit v6 on v5

--- a/solution.py
+++ b/solution.py
@@ -23,7 +23,7 @@
 
 
 def pack_kernel(axes, warm_hbm, signs_hbm, mask_hbm, kappa_hbm, scale_hbm, own, fields, to_odd, to_even, *scratch):
-    odd, _ = parities(axes)
+    odd, odd_lon = parities(axes)
     sems = scratch[-1]
     copies = [
         pltpu.make_async_copy(source, target, sems.at[n])
@@ -39,19 +39,20 @@
     wet = mask[...].astype(jnp.float32)
     diag = kappa[...] + 4.0
     scaled = scale[...]
-    fields[0] = wet
-    fields[1] = diag
-    fields[2] = scaled
+    for p in range(ROWS):
+        row = own.at[jnp.where(odd_lon == 0, p, ROWS - 1 - p)]
+        row[0:PROBES, :] = warm[:, p, :]
+        row[PROBES : 2 * PROBES, :] = 2.0 * signs[:, p, :].astype(jnp.float32) - 1.0
+        row[2 * PROBES :, :] = jnp.concatenate(
+            [wet[p : p + 1], diag[p : p + 1], scaled[p : p + 1], jnp.zeros((5, LANES), jnp.float32)], axis=0
+        )
     block = lax.broadcasted_iota(jnp.int32, (FIELDS, LANES), 1) // DEPTH
     left_edge = jnp.zeros((FIELDS, LANES), jnp.float32)
     right_edge = jnp.zeros((FIELDS, LANES), jnp.float32)
     for i in range(ROWS):
-        own[i, 0:PROBES, :] = warm[:, i, :]
-        own[i, PROBES : 2 * PROBES, :] = 2.0 * signs[:, i, :].astype(jnp.float32) - 1.0
-        own[i, 2 * PROBES :, :] = jnp.concatenate(
-            [wet[i : i + 1], diag[i : i + 1], scaled[i : i + 1], jnp.zeros((5, LANES), jnp.float32)], axis=0
-        )
         row = own[i]
+        for f in range(3):
+            fields[f, i : i + 1, :] = row[2 * PROBES + f : 2 * PROBES + f + 1]
         turned = pltpu.roll(row, DEPTH * i, 1) if i else row
         left_edge = jnp.where(block == i, turned, left_edge)
         right_edge = jnp.where(block == (i - 1) % ROWS, turned, right_edge)
@@ -70,29 +71,29 @@
 
 
 def send_kernel(axes, own, fields, from_odd, from_even, to_odd, to_even):
-    odd_lat, odd_lon = parities(axes)
+    odd_lat, _ = parities(axes)
     lane = lax.broadcasted_iota(jnp.int32, (FIELDS, LANES), 1)
     before, after = sides(odd_lat, from_even[...], from_odd[...])
     first = jnp.where(lane < 64, after, pltpu.roll(before, 72, 1))
     last = jnp.where(lane < 64, pltpu.roll(after, 64, 1), pltpu.roll(before, 8, 1))
-    for target, is_last in ((to_even, odd_lon == 0), (to_odd, odd_lon != 0)):
-        start = jnp.where(is_last, DEPTH, 0)
-        near = jnp.where(is_last, DEPTH + 2, 0)
+    for target, corner, low, row in (
+        (to_odd, first, 0, lambda j: j),
+        (to_even, last, DEPTH, lambda j: ROWS - 1 - j),
+    ):
         for j in range(DEPTH):
-            target[j * PROBES : (j + 1) * PROBES, :] = own[start + j, 0:PROBES, :]
+            target[j * PROBES : (j + 1) * PROBES, :] = own[row(j), 0:PROBES, :]
         for j in range(DEPTH - 2):
-            target[SEND_PROBES + j * PROBES : SEND_PROBES + (j + 1) * PROBES, :] = own[near + j, PROBES : 2 * PROBES, :]
+            target[SEND_PROBES + j * PROBES : SEND_PROBES + (j + 1) * PROBES, :] = own[row(j), PROBES : 2 * PROBES, :]
         for f in range(3):
-            target[SEND_FIELDS + f * DEPTH : SEND_FIELDS + (f + 1) * DEPTH, :] = jnp.where(
-                is_last, fields[f, DEPTH:, :], fields[f, 0:DEPTH, :]
-            )
-        target[SEND_CORNER:, :] = jnp.where(is_last, last, first)
+            target[SEND_FIELDS + f * DEPTH : SEND_FIELDS + (f + 1) * DEPTH, :] = fields[f, low : low + DEPTH, :]
+        target[SEND_CORNER:, :] = corner
 
 
 TALL = ROWS + 2 * DEPTH
-INSIDE = dict(mp=(8, 24), up=(9, 23), mw=(8, 24), i0=(9, 23), p0=(10, 22), m0=(10, 22), i1=(11, 21), p1=(12, 20), m1=(12, 20), i2=(13, 19), p2=(14, 18), m2=(14, 18), i3=(15, 17))
+INSIDE = dict(mp=(8, 24), up=(9, 23), mw=(8, 24), i0=(9, 23), p0=(10, 22), m0=(10, 22), i1=(11, 21), p1=(12, 20), m1=(12, 20), i2=(13, 19), p2=(14, 18), m2=(14, 18), i3=(15, 17), p3=(16, 16))
 NEEDED = dict(mp=(7, 25), up=(8, 24), mw=(0, 32), i0=(1, 31), p0=(2, 30), m0=(2, 30), i1=(3, 29), p1=(4, 28), m1=(4, 28), i2=(5, 27), p2=(6, 26), m2=(6, 26), i3=(7, 25), p3=(8, 24))
-HELD = tuple(INSIDE)
+HELD = tuple(name for name in INSIDE if name != "p3")
+HALF = ROWS // 2
 
 
 def fill_coef(coef, at, wet, diag, scaled):
@@ -156,58 +157,60 @@
     )
 
 
-def krylov_kernel(axes, own_wide, own_coefs, *refs):
+def half_kernel(behind, own_wide, own_coefs, *refs):
     held = dict(zip(HELD, refs, strict=False))
-    from_odd_lon, from_even_lon, sums, basis, images, probe_image, wide, coefs = refs[len(HELD) : len(HELD) + 8]
-    fresh = dict(zip(NEEDED, refs[len(HELD) + 8 :], strict=True))
-    _, odd_lon = parities(axes)
+    refs = refs[len(HELD) :]
+    if behind:
+        other, message, sums, basis, images, probe_image, wide, coefs, *fresh = refs
+    else:
+        message, sums, basis, images, probe_image, wide, coefs, *fresh = refs
+    fresh = dict(zip(NEEDED, fresh, strict=True))
     lane = lax.broadcasted_iota(jnp.int32, (FIELDS, LANES), 1)
-    for side, is_next in ((from_even_lon, odd_lon == 0), (from_odd_lon, odd_lon != 0)):
-        start = jnp.where(is_next, DEPTH + ROWS, 0)
-        near = jnp.where(is_next, DEPTH + ROWS, 2)
-        pair = side[SEND_CORNER:, :]
-        for j in range(DEPTH):
-            wide[start + j, 0:PROBES, 0:LANES] = side[j * PROBES : (j + 1) * PROBES, :]
-            for f in range(3):
-                at = SEND_FIELDS + f * DEPTH + j
-                wide[start + j, 2 * PROBES + f : 2 * PROBES + f + 1, 0:LANES] = side[at : at + 1, :]
-            wide[start + j, :, LANES:] = jnp.where(
-                lane < 64, pltpu.roll(pair, (LANES - 8 * j) % LANES, 1), pltpu.roll(pair, (56 - 8 * j) % LANES, 1)
-            )
-        for j in range(DEPTH - 2):
+    pair = message[SEND_CORNER:, :]
+    for j in range(DEPTH):
+        place = DEPTH - 1 - j if behind else j
+        wide[j, 0:PROBES, 0:LANES] = message[j * PROBES : (j + 1) * PROBES, :]
+        if j < DEPTH - 2:
             at = SEND_PROBES + j * PROBES
-            wide[near + j, PROBES : 2 * PROBES, 0:LANES] = side[at : at + PROBES, :]
+            wide[j, PROBES : 2 * PROBES, 0:LANES] = message[at : at + PROBES, :]
+        for f in range(3):
+            at = SEND_FIELDS + f * DEPTH + place
+            wide[j, 2 * PROBES + f : 2 * PROBES + f + 1, 0:LANES] = message[at : at + 1, :]
+        after = pltpu.roll(pair, (LANES - 8 * place) % LANES, 1)
+        before = pltpu.roll(pair, (56 - 8 * place) % LANES, 1)
+        wide[j, :, LANES:] = jnp.where(lane < 64, after, before)
+        fill_coef(coefs, j, wide[j, 64:65, :], wide[j, 65:66, :], wide[j, 66:67, :])
+
+    base = TALL // 2 if behind else 0
 
     def own(r):
         return DEPTH <= r < DEPTH + ROWS
 
-    for r in range(TALL):
-        if not own(r):
-            fill_coef(coefs, r, wide[r, 64:65, :], wide[r, 65:66, :], wide[r, 66:67, :])
+    def halo(r):
+        return r - (DEPTH + ROWS) if behind else DEPTH - 1 - r
 
     def rows(name):
-        done = range(*INSIDE.get(name, (0, 0)))
-        return [r for r in range(*NEEDED.get(name, (0, 0))) if r not in done]
+        if name not in NEEDED:
+            return range(0)
+        return range(INSIDE[name][1], NEEDED[name][1]) if behind else range(NEEDED[name][0], INSIDE[name][0])
 
     def get(name, r):
-        return held[name][r - DEPTH] if r in range(*INSIDE.get(name, (0, 0))) else fresh[name][r]
+        return fresh[name][r - base] if r in rows(name) else held[name][r - DEPTH]
 
     def put(name, r, value):
-        fresh[name][r] = value
+        fresh[name][r - base] = value
 
     def coef(r, n):
-        return own_coefs[r - DEPTH, n : n + 1, :] if own(r) else coefs[r, n : n + 1, :]
+        return own_coefs[r - DEPTH, n : n + 1, :] if own(r) else coefs[halo(r), n : n + 1, :]
 
     def argument(r, at):
-        if own(r):
-            return own_wide[r - DEPTH, at : at + PROBES, :]
-        return wide[r, at : at + PROBES, :]
+        return own_wide[r - DEPTH, at : at + PROBES, :] if own(r) else wide[halo(r), at : at + PROBES, :]
 
     march(rows, coef, lambda r: argument(r, 0), lambda r: argument(r, PROBES), get, put)
 
-    total = jnp.zeros((3 * PROBES, 4 * PROBES), jnp.float32)
-    for i in range(ROWS):
-        r = DEPTH + i
+    total = other[...] if behind else jnp.zeros((3 * PROBES, 4 * PROBES), jnp.float32)
+    for i in range(HALF):
+        r = DEPTH + i + (HALF if behind else 0)
         for k in range(4):
             at = slice(k * PROBES, (k + 1) * PROBES)
             basis[i, at, :] = get(f"p{k}", r)[:, 0:LANES]
@@ -221,6 +224,9 @@
             precision=lax.Precision.HIGHEST,
             preferred_element_type=jnp.float32,
         )
+    if not behind:
+        sums[...] = total
+        return
     lane = lax.broadcasted_iota(jnp.int32, (PROBES, LANES), 1)
     row = lax.broadcasted_iota(jnp.int32, (PROBES, LANES), 0)
     packed = jnp.zeros((PROBES, LANES), jnp.float32)
@@ -281,19 +287,22 @@
     def spread(value):
         return jnp.broadcast_to(value, (8, LANES))
 
+    def take(part, lane):
+        return jnp.take_along_axis(part, jnp.full((8, LANES), lane, jnp.int32), axis=1)
+
     for home in range(len(parts)):
         at = 8 * home
-        columns = [[spread(part[:, at + j : at + j + 1]) for j in range(8)] for part in parts]
-        pivot = [[spread(columns[home][j][i : i + 1]) for j in range(8)] for i in range(8)]
+        column = [take(parts[home], at + j) for j in range(8)]
+        pivot = [[spread(column[j][i : i + 1]) for j in range(8)] for i in range(8)]
         solved = prepare(pivot)([spread(parts[home][i : i + 1]) for i in range(8)])
-        for v, column in enumerate(columns):
+        for v in [*range(home, len(parts)), *range(home)]:
             if v == home:
                 part = solved[0]
                 for i in range(1, 8):
                     part = jnp.where(row == i, solved[i], part)
                 parts[v] = part
             else:
-                terms = [c * x for c, x in zip(column, solved, strict=True)]
+                terms = [take(parts[v], at + j) * solved[j] for j in range(8)]
                 parts[v] = parts[v] - (
                     ((terms[0] + terms[1]) + (terms[2] + terms[3])) + ((terms[4] + terms[5]) + (terms[6] + terms[7]))
                 )
@@ -301,10 +310,12 @@
 
 
 def finish_kernel(
-    sums, own, basis, images, probe_image,
+    axes,
+    sums, own, basis_first, basis_last, images_first, images_last, probe_first, probe_last,
     solution_out, residual_out, grad_out,
-    coeffs,
+    coeffs, rows,
 ):
+    _, odd_lon = parities(axes)
     packed = sums[...]
     flipped = packed.T
     lane = lax.broadcasted_iota(jnp.int32, (PROBES, PROBES), 1)
@@ -324,25 +335,58 @@
     parts = eliminate([table[8 * v : 8 * v + 8] for v in range(12)])
     solved = jnp.concatenate(parts, axis=0)
 
+    t = [jnp.sum(jnp.where(lane == row, m, 0.0), axis=(0, 1), keepdims=True) for m in moments]
+    a = t[1] / t[0]
+    n1 = t[2] - a * t[1]
+    b0, b1 = (t[2] / t[0], (t[3] - a * t[2]) / n1)
+    b2 = b1 * a - b0
+    c0, c1 = (t[3] / t[0], (t[4] - a * t[3]) / n1)
+    c2 = (t[5] - b1 * t[4] + b2 * t[3]) / (t[4] - b1 * t[3] + b2 * t[2])
+
     nothing = jnp.zeros((PROBES, LANES), jnp.float32)
     wide_lane = lax.broadcasted_iota(jnp.int32, (4 * PROBES, LANES), 1)
     wide_row = lax.broadcasted_iota(jnp.int32, (4 * PROBES, LANES), 0)
     one = (wide_lane == wide_row + 3 * PROBES).astype(jnp.float32)
     kept = jnp.concatenate([solved, nothing], axis=0)
     left = one - SHIFT * kept - (1.0 / GAIN) * jnp.concatenate([nothing, solved], axis=0)
-    columns = jnp.where(wide_lane < PROBES, pltpu.roll(kept, PROBES, 1), pltpu.roll(left, 2 * PROBES, 1))
-    coeffs[...] = columns.T[0 : 2 * PROBES]
-    weights = coeffs[0:PROBES, :] + one[0:PROBES]
+
+    def for_polynomials(v):
+        v = [v[k * PROBES : (k + 1) * PROBES] for k in range(4)]
+        return jnp.concatenate(
+            [v[0] + a * v[1] + b0 * v[2] + c0 * v[3], v[1] + b1 * v[2] + c1 * v[3], v[2] + c2 * v[3], v[3]], axis=0
+        )
+
+    columns = jnp.where(
+        wide_lane < PROBES,
+        pltpu.roll(for_polynomials(kept), PROBES, 1),
+        jnp.where(wide_lane < 2 * PROBES, pltpu.roll(for_polynomials(left), 2 * PROBES, 1), pltpu.roll(kept, 3 * PROBES, 1)),
+    )
+    coeffs[...] = columns.T[0 : 3 * PROBES]
+    weights = coeffs[2 * PROBES :, :] + one[0:PROBES]
+    a, b0, b1, c0, c1, c2 = (jnp.broadcast_to(x, (PROBES, LANES)) for x in (a, b0, b1, c0, c1, c2))
 
     for i in range(ROWS):
-        both = dot(coeffs[...], basis[i], lax.Precision.HIGHEST)
+        j = i % HALF
+        basis, images, probe_image = (
+            (basis_first, images_first, probe_first) if i < HALF else (basis_last, images_last, probe_last)
+        )
+        v0 = basis[j, 0:PROBES, :]
+        w1 = basis[j, PROBES : 2 * PROBES, :] - a * v0
+        w2 = basis[j, 2 * PROBES : 3 * PROBES, :] - b1 * w1 - b0 * v0
+        w3 = basis[j, 3 * PROBES :, :] - c2 * w2 - c1 * w1 - c0 * v0
+        both = dot(coeffs[0 : 2 * PROBES, :], jnp.concatenate([v0, w1, w2, w3], axis=0), lax.Precision.HIGH)
         values = both[0:PROBES] + own[i, 0:PROBES, :]
-        solution_out[:, i, :] = values
-        residual_out[:, i, :] = both[PROBES:]
-        image = dot(weights, images[i], lax.Precision.HIGH)
-        terms = values * probe_image[i] + image * own[i, PROBES : 2 * PROBES, :]
+        image = dot(weights, images[j], lax.Precision.HIGH)
+        terms = values * probe_image[j] + image * own[i, PROBES : 2 * PROBES, :]
         wet = own[i, 64:65, :]
-        grad_out[i : i + 1, :] = wet * (jnp.sum(terms, axis=0, keepdims=True) * (1.0 / PROBES))
+        out = rows.at[jnp.where(odd_lon == 0, i, ROWS - 1 - i)]
+        out[0:PROBES, :] = values
+        out[PROBES : 2 * PROBES, :] = both[PROBES:]
+        out[2 * PROBES : 2 * PROBES + 1, :] = wet * (jnp.sum(terms, axis=0, keepdims=True) * (1.0 / PROBES))
+    for p in range(ROWS):
+        solution_out[:, p, :] = rows[p, 0:PROBES, :]
+        residual_out[:, p, :] = rows[p, PROBES : 2 * PROBES, :]
+        grad_out[p : p + 1, :] = rows[p, 2 * PROBES : 2 * PROBES + 1, :]
 
 
 def f32(*shape):
@@ -401,36 +445,45 @@
             cost_estimate=pl.CostEstimate(flops=40_000_000, bytes_accessed=8_000_000, transcendentals=0),
             name="inside_rows",
         )(own, odd_lat, even_lat)
-        sums, basis, images, probe_image = pl.pallas_call(
-            functools.partial(krylov_kernel, axes),
-            out_shape=(
-                f32(PROBES, LANES),
-                f32(ROWS, 4 * PROBES, LANES),
-                f32(ROWS, 4 * PROBES, LANES),
-                f32(ROWS, PROBES, LANES),
-            ),
+        half = dict(
             scratch_shapes=[
-                pltpu.VMEM((TALL, FIELDS, 2 * LANES), jnp.float32),
-                pltpu.VMEM((TALL, 8, 2 * LANES), jnp.float32),
+                pltpu.VMEM((DEPTH, FIELDS, 2 * LANES), jnp.float32),
+                pltpu.VMEM((DEPTH, 8, 2 * LANES), jnp.float32),
             ]
-            + [pltpu.VMEM((TALL, PROBES, 2 * LANES), jnp.float32)] * len(NEEDED),
+            + [pltpu.VMEM((TALL // 2, PROBES, 2 * LANES), jnp.float32)] * len(NEEDED),
             compiler_params=PARAMS,
-            name="krylov_moments",
-        )(*inside, odd_lon, even_lon)
+            cost_estimate=pl.CostEstimate(flops=40_000_000, bytes_accessed=8_000_000, transcendentals=0),
+        )
+        filled = (f32(HALF, 4 * PROBES, LANES), f32(HALF, 4 * PROBES, LANES), f32(HALF, PROBES, LANES))
+        part, *first = pl.pallas_call(
+            functools.partial(half_kernel, False),
+            out_shape=(f32(3 * PROBES, LANES), *filled),
+            name="first_rows",
+            **half,
+        )(*inside, odd_lon)
+        sums, *last = pl.pallas_call(
+            functools.partial(half_kernel, True),
+            out_shape=(f32(PROBES, LANES), *filled),
+            name="last_rows",
+            **half,
+        )(*inside, part, even_lon)
         with jax.named_scope("sum_moments"):
             for group in stages:
                 sums = spread_sum(sums, group)
         return pl.pallas_call(
-            finish_kernel,
+            functools.partial(finish_kernel, axes),
             out_shape=(
                 f32(PROBES, ROWS, LANES),
                 f32(PROBES, ROWS, LANES),
                 f32(ROWS, LANES),
             ),
-            scratch_shapes=[pltpu.VMEM((2 * PROBES, 4 * PROBES), jnp.float32)],
+            scratch_shapes=[
+                pltpu.VMEM((3 * PROBES, 4 * PROBES), jnp.float32),
+                pltpu.VMEM((ROWS, FIELDS, LANES), jnp.float32),
+            ],
             compiler_params=PARAMS,
             name="solve_and_combine",
-        )(sums, own, basis, images, probe_image)
+        )(sums, own, *(x for pair in zip(first, last, strict=True) for x in pair))
 
     return local
 

time: 79.6 us -> 76.3 us (0.959)
  waiting for transfers between devices: 7.73 us -> 5.59 us
  Pallas kernels: 14 us -> 12.3 us
    ppermute x4, waiting for transfers between devices: 7.73 us -> 5.59 us  [exchanged(): return lax.ppermute(value, axes, pairs)]
    pallas_call x2 -> x3, Pallas kernels: 10.6 us -> 8.8 us  [the longest x1 4.67 us: local(): pl.pallas_call(functools.partial(finish_kernel, axes), out_shape=(f32(PRO...]
  transfers between devices with their start and end apart: 4 -> 4, of which waited for: 3 -> 3; matrix products, arithmetic and copies ran while one was open for 0% -> 0% of each run, Pallas kernels for 2% -> 5%
where the time goes in v6:
time: 76.3 us; the launch traced here: 76 us
  blocking collectives  39.1 us (51%)
  starting transfers between devices  18.2 us (24%)
  Pallas kernels  12.3 us (16%)
  waiting for transfers between devices  5.59 us (7%)
    all_to_all x3, blocking collectives, spread_sum(): return jnp.sum(lax.all_to_all(copies, axes, 0, 0), axis=0)  39.1 us
    ppermute x4, starting transfers between devices, exchanged(): return lax.ppermute(value, axes, pairs)  18.2 us
    ppermute x4, waiting for transfers between devices, exchanged(): return lax.ppermute(value, axes, pairs)  5.59 us
    pallas_call x1, Pallas kernels, local(): pl.pallas_call(functools.partial(finish_kernel, axes), out_shape=(f32(PRO...  4.67 us
    pallas_call x1, Pallas kernels, local(): pl.pallas_call(functools.partial(half_kernel, False), out_shape=(f32(3 *...  2.15 us
    pallas_call x1, Pallas kernels, local(): pl.pallas_call(functools.partial(half_kernel, True), out_shape=(f32(PROBE...  1.98 us
    pallas_call x1, Pallas kernels, local(): pl.pallas_call(functools.partial(inside_kernel, axes), out_shape=(f32(ROW...  1.68 us
    pallas_call x1, Pallas kernels, local(): pl.pallas_call(functools.partial(pack_kernel, axes), out_shape=(f32(ROWS,...  1.68 us
  transfers between devices with their start and end apart: 4, of which 3 were waited for; matrix products, arithmetic and copies ran while one was open for 0% of the time, Pallas kernels for 5%

profile of v6, /device:TPU:2, one launch (start us, length us, event | category | flops | bytes accessed | tf_op | source)
XLA Modules:
  0.0 76.0 jit_solution(2653679434954648953)
XLA Ops:
  0.6 1.7 %pack_edges.1 = (f32[16,72,128]{2,1,0:T(8,128)S(1)}, f32[3,16,128]{2,1,0:T(8,128)S(1)}, f32[72,128]{1,0:T(8,128)S(1)}, f32[72,128]{1,0:T(8,128)S(1)}) custom-call(f32[32,16,128]{2,1,0:T(8,128)} %warm_hbm.1, s32[32,16,128]{2,1,0:T(8,128)} %signs_hbm.1, s32[16,128]{1,0:T(8,128)} %mask_hbm.1, f32[16,128]{1,0:T(8,128)} %kappa_hbm.1, f32[16,128]{1,0:T(8,128)} %scale_hbm.1), custom_call_target="tpu_custom_call" | custom-call | tf_op jit(solution)/shard_map/pack_edges/pallas_call | solution.py:417
  2.3 1.9 %collective-permute-start = (f32[72,128]{1,0:T(8,128)S(1)}, f32[72,128]{1,0:T(8,128)S(1)}, u32[]{:S(2)}, u32[]{:S(2)}) collective-permute-start(f32[72,128]{1,0:T(8,128)S(1)} %get-tuple-element.33), channel_id=1, source_target_pairs={{32,64},{64,32},{96,128},{128,96},{160,192},{192,160},{224,256},{2... | collective-permute-start | bytes 110600 | tf_op jit(solution)/shard_map/ppermute | solution.py:403
  4.2 3.5 %collective-permute-start.1 = (f32[72,128]{1,0:T(8,128)S(1)}, f32[72,128]{1,0:T(8,128)S(1)}, u32[]{:S(2)}, u32[]{:S(2)}) collective-permute-start(f32[72,128]{1,0:T(8,128)S(1)} %get-tuple-element.34), channel_id=1, source_target_pairs={{0,32},{32,0},{64,96},{96,64},{128,160},{160,128},{192,224},{224,1... | collective-permute-start | bytes 110600 | tf_op jit(solution)/shard_map/ppermute | solution.py:403
  7.8 0.0 collective-permute-done.from_odd
  7.8 0.8 %collective-permute-done.1.from_even = f32[72,128]{1,0:T(8,128)S(1)} collective-permute-done((f32[72,128]{1,0:T(8,128)S(1)}, f32[72,128]{1,0:T(8,128)S(1)}, u32[]{:S(2)}, u32[]{:S(2)}) %collective-permute-start.1) | collective-permute-done | bytes 36896 | tf_op jit(solution)/shard_map/ppermute | solution.py:403
  8.6 0.1 pack_rows.1
  8.7 10.9 %collective-permute-start.2 = (f32[544,128]{1,0:T(8,128)S(1)}, f32[544,128]{1,0:T(8,128)S(1)}, u32[]{:S(2)}, u32[]{:S(2)}) collective-permute-start(f32[544,128]{1,0:T(8,128)S(1)} %get-tuple-element.51), channel_id=1, source_target_pairs={{0,31},{1,2},{2,1},{3,4},{4,3},{5,6},{6,5},{7,8},{8,7},{9,10},{10,... | collective-permute-start | bytes 835592 | tf_op jit(solution)/shard_map/ppermute | solution.py:403
  19.6 1.9 %collective-permute-start.3 = (f32[544,128]{1,0:T(8,128)S(1)}, f32[544,128]{1,0:T(8,128)S(1)}, u32[]{:S(2)}, u32[]{:S(2)}) collective-permute-start(f32[544,128]{1,0:T(8,128)S(1)} %get-tuple-element.53), channel_id=1, source_target_pairs={{0,1},{1,0},{2,3},{3,2},{4,5},{5,4},{6,7},{7,6},{8,9},{9,8},{10,11... | collective-permute-start | bytes 835592 | tf_op jit(solution)/shard_map/ppermute | solution.py:403
  21.5 1.7 %inside_rows.1 = (f32[16,72,256]{2,1,0:T(8,128)S(1)}, f32[16,8,256]{2,1,0:T(8,128)S(1)}, f32[16,32,256]{2,1,0:T(8,128)S(1)}, f32[16,32,256]{2,1,0:T(8,128)S(1)},...) custom-call(f32[16,72,128]{2,1,0:T(8,128)S(1)} %get-tuple-element.32, ...), custom_call_target="tpu_custom_call" | custom-call | flops 40000000 | bytes 8000000 | tf_op jit(solution)/shard_map/inside_rows/pallas_call | solution.py:440
  23.2 3.5 %collective-permute-done.2.refs_13_ = f32[544,128]{1,0:T(8,128)S(1)} collective-permute-done((f32[544,128]{1,0:T(8,128)S(1)}, f32[544,128]{1,0:T(8,128)S(1)}, u32[]{:S(2)}, u32[]{:S(2)}) %collective-permute-start.2) | collective-permute-done | bytes 278560 | tf_op jit(solution)/shard_map/ppermute | solution.py:403
  26.7 2.1 %first_rows.1 = (f32[96,128]{1,0:T(8,128)S(1)}, f32[8,128,128]{2,1,0:T(8,128)S(1)}, f32[8,128,128]{2,1,0:T(8,128)S(1)}, f32[8,32,128]{2,1,0:T(8,128)S(1)}) custom-call(f32[16,72,256]{2,1,0:T(8,128)S(1)} %get-tuple-element.35.own_wide, f32[16,8,256]{2,1,0:T(8,128)S(1)} %get-tuple-element.36.own_coefs, f32[16,32,256]{2,1,0:T(8,128)S(1)} %get-tuple-element.37.refs_0_, ...), custom_call_target="tpu_custom_call" | custom-call | flops 40000000 | bytes 8000000 | tf_op jit(solution)/shard_map/first_rows/pallas_call | solution.py:458
  28.9 1.2 %collective-permute-done.3.refs_14_ = f32[544,128]{1,0:T(8,128)S(1)} collective-permute-done((f32[544,128]{1,0:T(8,128)S(1)}, f32[544,128]{1,0:T(8,128)S(1)}, u32[]{:S(2)}, u32[]{:S(2)}) %collective-permute-start.3) | collective-permute-done | bytes 278560 | tf_op jit(solution)/shard_map/ppermute | solution.py:403
  30.1 2.0 %last_rows.1 = (f32[32,128]{1,0:T(8,128)S(1)}, f32[8,128,128]{2,1,0:T(8,128)S(1)}, f32[8,128,128]{2,1,0:T(8,128)S(1)}, f32[8,32,128]{2,1,0:T(8,128)S(1)}) custom-call(f32[16,72,256]{2,1,0:T(8,128)S(1)} %get-tuple-element.35.own_wide, f32[16,8,256]{2,1,0:T(8,128)S(1)} %get-tuple-element.36.own_coefs, f32[16,32,256]{2,1,0:T(8,128)S(1)} %get-tuple-element.37.refs_0_, ...), custom_call_target="tpu_custom_call" | custom-call | flops 40000000 | bytes 8000000 | tf_op jit(solution)/shard_map/last_rows/pallas_call | solution.py:464
  32.1 13.8 %all_to_all.15 = f32[8,32,128]{2,1,0:T(8,128)S(1)} all-to-all(f32[8,32,128]{2,1,0:T(8,128)S(1)} %broadcast_in_dim.6), channel_id=1, replica_groups=mesh['zh'=2,'x'=4,'c'=2,'zl'=4,'y'=8] {'x','c'}, dimensions={0} | all-to-all | bytes 262144 | tf_op jit(solution)/shard_map/sum_moments/all_to_all | solution.py:409
  45.9 11.6 %all_to_all.16 = f32[8,32,128]{2,1,0:T(8,128)S(1)} all-to-all(f32[8,32,128]{2,1,0:T(8,128)S(1)} %broadcast_in_dim.7), channel_id=1, replica_groups=mesh['zh'=2,'x'=4,'c'=2,'zl'=4,'y'=8] {'y'}, dimensions={0} | all-to-all | bytes 262144 | tf_op jit(solution)/shard_map/sum_moments/all_to_all | solution.py:409
  57.5 13.8 %all_to_all.17 = f32[8,32,128]{2,1,0:T(8,128)S(1)} all-to-all(f32[8,32,128]{2,1,0:T(8,128)S(1)} %broadcast_in_dim.8), channel_id=1, replica_groups=mesh['zh'=2,'x'=4,'c'=2,'zl'=4,'y'=8] {'zh','zl'}, dimensions={0} | all-to-all | bytes 262144 | tf_op jit(solution)/shard_map/sum_moments/all_to_all | solution.py:409
  71.3 4.7 %solve_and_combine.1 = (f32[32,16,128]{2,1,0:T(8,128)}, f32[32,16,128]{2,1,0:T(8,128)}, f32[16,128]{1,0:T(8,128)}) custom-call(f32[32,128]{1,0:T(8,128)S(1)} %reduce_sum.29.sums, f32[16,72,128]{2,1,0:T(8,128)S(1)} %get-tuple-element.32.own, f32[8,128,128]{2,1,0:T(8,128)S(1)} %get-tuple-element.55.basis_first, ...), custom_call_target="tpu_custom_call" | custom-call | tf_op jit(solution)/shard_map/solve_and_combine/pallas_call | solution.py:473
  (6 shorter events, 0.1 us)
Async XLA Ops:
  2.3 5.4 %collective-permute-start = (f32[72,128]{1,0:T(8,128)S(1)}, f32[72,128]{1,0:T(8,128)S(1)}, u32[]{:S(2)}, u32[]{:S(2)}) collective-permute-start(f32[72,128]{1,0:T(8,128)S(1)} %get-tuple-element.33), channel_id=1, source_target_pairs={{32,64},{64,32},{96,128},{128,96},{160,192},{192,160},{224,256},{2... | collective-permute-start | bytes 110600 | tf_op jit(solution)/shard_map/ppermute | solution.py:403
  4.2 4.4 %collective-permute-start.1 = (f32[72,128]{1,0:T(8,128)S(1)}, f32[72,128]{1,0:T(8,128)S(1)}, u32[]{:S(2)}, u32[]{:S(2)}) collective-permute-start(f32[72,128]{1,0:T(8,128)S(1)} %get-tuple-element.34), channel_id=1, source_target_pairs={{0,32},{32,0},{64,96},{96,64},{128,160},{160,128},{192,224},{224,1... | collective-permute-start | bytes 110600 | tf_op jit(solution)/shard_map/ppermute | solution.py:403
  8.7 18.0 %collective-permute-start.2 = (f32[544,128]{1,0:T(8,128)S(1)}, f32[544,128]{1,0:T(8,128)S(1)}, u32[]{:S(2)}, u32[]{:S(2)}) collective-permute-start(f32[544,128]{1,0:T(8,128)S(1)} %get-tuple-element.51), channel_id=1, source_target_pairs={{0,31},{1,2},{2,1},{3,4},{4,3},{5,6},{6,5},{7,8},{8,7},{9,10},{10,... | collective-permute-start | bytes 835592 | tf_op jit(solution)/shard_map/ppermute | solution.py:403
  19.6 10.5 %collective-permute-start.3 = (f32[544,128]{1,0:T(8,128)S(1)}, f32[544,128]{1,0:T(8,128)S(1)}, u32[]{:S(2)}, u32[]{:S(2)}) collective-permute-start(f32[544,128]{1,0:T(8,128)S(1)} %get-tuple-element.53), channel_id=1, source_target_pairs={{0,1},{1,0},{2,3},{3,2},{4,5},{5,4},{6,7},{7,6},{8,9},{9,8},{10,11... | collective-permute-start | bytes 835592 | tf_op jit(solution)/shard_map/ppermute | solution.py:403

commit v7 on v6

--- a/solution.py
+++ b/solution.py
@@ -216,7 +216,9 @@
             basis[i, at, :] = get(f"p{k}", r)[:, 0:LANES]
             images[i, at, :] = get(f"i{(k + 1) % 4}", r)[:, 0:LANES]
         probe_image[i] = get("up", r)[:, 0:LANES]
-        block = basis[i]
+        if i % 2 == 0:
+            continue
+        block = jnp.concatenate([basis[i - 1], basis[i]], axis=1)
         total = total + lax.dot_general(
             block[0 : 3 * PROBES],
             block,
@@ -365,24 +367,29 @@
     weights = coeffs[2 * PROBES :, :] + one[0:PROBES]
     a, b0, b1, c0, c1, c2 = (jnp.broadcast_to(x, (PROBES, LANES)) for x in (a, b0, b1, c0, c1, c2))
 
-    for i in range(ROWS):
+    for i in range(0, ROWS, 2):
         j = i % HALF
         basis, images, probe_image = (
             (basis_first, images_first, probe_first) if i < HALF else (basis_last, images_last, probe_last)
         )
-        v0 = basis[j, 0:PROBES, :]
-        w1 = basis[j, PROBES : 2 * PROBES, :] - a * v0
-        w2 = basis[j, 2 * PROBES : 3 * PROBES, :] - b1 * w1 - b0 * v0
-        w3 = basis[j, 3 * PROBES :, :] - c2 * w2 - c1 * w1 - c0 * v0
-        both = dot(coeffs[0 : 2 * PROBES, :], jnp.concatenate([v0, w1, w2, w3], axis=0), lax.Precision.HIGH)
-        values = both[0:PROBES] + own[i, 0:PROBES, :]
-        image = dot(weights, images[j], lax.Precision.HIGH)
-        terms = values * probe_image[j] + image * own[i, PROBES : 2 * PROBES, :]
-        wet = own[i, 64:65, :]
-        out = rows.at[jnp.where(odd_lon == 0, i, ROWS - 1 - i)]
-        out[0:PROBES, :] = values
-        out[PROBES : 2 * PROBES, :] = both[PROBES:]
-        out[2 * PROBES : 2 * PROBES + 1, :] = wet * (jnp.sum(terms, axis=0, keepdims=True) * (1.0 / PROBES))
+        polynomials = []
+        for n in (j, j + 1):
+            v0 = basis[n, 0:PROBES, :]
+            w1 = basis[n, PROBES : 2 * PROBES, :] - a * v0
+            w2 = basis[n, 2 * PROBES : 3 * PROBES, :] - b1 * w1 - b0 * v0
+            w3 = basis[n, 3 * PROBES :, :] - c2 * w2 - c1 * w1 - c0 * v0
+            polynomials.append(jnp.concatenate([v0, w1, w2, w3], axis=0))
+        both = dot(coeffs[0 : 2 * PROBES, :], jnp.concatenate(polynomials, axis=1), lax.Precision.HIGH)
+        image = dot(weights, jnp.concatenate([images[j], images[j + 1]], axis=1), lax.Precision.HIGH)
+        for n in range(2):
+            lanes = slice(n * LANES, (n + 1) * LANES)
+            values = both[0:PROBES, lanes] + own[i + n, 0:PROBES, :]
+            terms = values * probe_image[j + n] + image[:, lanes] * own[i + n, PROBES : 2 * PROBES, :]
+            wet = own[i + n, 64:65, :]
+            out = rows.at[jnp.where(odd_lon == 0, i + n, ROWS - 1 - i - n)]
+            out[0:PROBES, :] = values
+            out[PROBES : 2 * PROBES, :] = both[PROBES:, lanes]
+            out[2 * PROBES : 2 * PROBES + 1, :] = wet * (jnp.sum(terms, axis=0, keepdims=True) * (1.0 / PROBES))
     for p in range(ROWS):
         solution_out[:, p, :] = rows[p, 0:PROBES, :]
         residual_out[:, p, :] = rows[p, PROBES : 2 * PROBES, :]

time: 76.3 us -> 75.5 us (0.990)
  Pallas kernels: 12.3 us -> 11.4 us
where the time goes in v7:
time: 75.5 us; the launch traced here: 75.1 us
  blocking collectives  38.8 us (51%)
  starting transfers between devices  18.2 us (24%)
  Pallas kernels  11.4 us (15%)
  waiting for transfers between devices  5.91 us (8%)
    all_to_all x3, blocking collectives, spread_sum(): return jnp.sum(lax.all_to_all(copies, axes, 0, 0), axis=0)  38.8 us
    ppermute x4, starting transfers between devices, exchanged(): return lax.ppermute(value, axes, pairs)  18.2 us
    ppermute x4, waiting for transfers between devices, exchanged(): return lax.ppermute(value, axes, pairs)  5.91 us
    pallas_call x1, Pallas kernels, local(): pl.pallas_call(functools.partial(finish_kernel, axes), out_shape=(f32(PRO...  4.28 us
    pallas_call x1, Pallas kernels, local(): pl.pallas_call(functools.partial(half_kernel, True), out_shape=(f32(PROBE...  1.89 us
    pallas_call x1, Pallas kernels, local(): pl.pallas_call(functools.partial(half_kernel, False), out_shape=(f32(3 *...  1.82 us
    pallas_call x1, Pallas kernels, local(): pl.pallas_call(functools.partial(inside_kernel, axes), out_shape=(f32(ROW...  1.68 us
    pallas_call x1, Pallas kernels, local(): pl.pallas_call(functools.partial(pack_kernel, axes), out_shape=(f32(ROWS,...  1.68 us
  transfers between devices with their start and end apart: 4, of which 3 were waited for; matrix products, arithmetic and copies ran while one was open for 0% of the time, Pallas kernels for 5%

profile of v7, /device:TPU:2, one launch (start us, length us, event | category | flops | bytes accessed | tf_op | source)
XLA Modules:
  0.0 75.1 jit_solution(14357461097581897874)
XLA Ops:
  0.6 1.7 %pack_edges.1 = (f32[16,72,128]{2,1,0:T(8,128)S(1)}, f32[3,16,128]{2,1,0:T(8,128)S(1)}, f32[72,128]{1,0:T(8,128)S(1)}, f32[72,128]{1,0:T(8,128)S(1)}) custom-call(f32[32,16,128]{2,1,0:T(8,128)} %warm_hbm.1, s32[32,16,128]{2,1,0:T(8,128)} %signs_hbm.1, s32[16,128]{1,0:T(8,128)} %mask_hbm.1, f32[16,128]{1,0:T(8,128)} %kappa_hbm.1, f32[16,128]{1,0:T(8,128)} %scale_hbm.1), custom_call_target="tpu_custom_call" | custom-call | tf_op jit(solution)/shard_map/pack_edges/pallas_call | solution.py:424
  2.3 1.9 %collective-permute-start = (f32[72,128]{1,0:T(8,128)S(1)}, f32[72,128]{1,0:T(8,128)S(1)}, u32[]{:S(2)}, u32[]{:S(2)}) collective-permute-start(f32[72,128]{1,0:T(8,128)S(1)} %get-tuple-element.33), channel_id=1, source_target_pairs={{32,64},{64,32},{96,128},{128,96},{160,192},{192,160},{224,256},{2... | collective-permute-start | bytes 110600 | tf_op jit(solution)/shard_map/ppermute | solution.py:410
  4.2 3.5 %collective-permute-start.1 = (f32[72,128]{1,0:T(8,128)S(1)}, f32[72,128]{1,0:T(8,128)S(1)}, u32[]{:S(2)}, u32[]{:S(2)}) collective-permute-start(f32[72,128]{1,0:T(8,128)S(1)} %get-tuple-element.34), channel_id=1, source_target_pairs={{0,32},{32,0},{64,96},{96,64},{128,160},{160,128},{192,224},{224,1... | collective-permute-start | bytes 110600 | tf_op jit(solution)/shard_map/ppermute | solution.py:410
  7.8 0.0 collective-permute-done.from_odd
  7.8 0.8 %collective-permute-done.1.from_even = f32[72,128]{1,0:T(8,128)S(1)} collective-permute-done((f32[72,128]{1,0:T(8,128)S(1)}, f32[72,128]{1,0:T(8,128)S(1)}, u32[]{:S(2)}, u32[]{:S(2)}) %collective-permute-start.1) | collective-permute-done | bytes 36896 | tf_op jit(solution)/shard_map/ppermute | solution.py:410
  8.6 0.1 pack_rows.1
  8.7 10.9 %collective-permute-start.2 = (f32[544,128]{1,0:T(8,128)S(1)}, f32[544,128]{1,0:T(8,128)S(1)}, u32[]{:S(2)}, u32[]{:S(2)}) collective-permute-start(f32[544,128]{1,0:T(8,128)S(1)} %get-tuple-element.51), channel_id=1, source_target_pairs={{0,31},{1,2},{2,1},{3,4},{4,3},{5,6},{6,5},{7,8},{8,7},{9,10},{10,... | collective-permute-start | bytes 835592 | tf_op jit(solution)/shard_map/ppermute | solution.py:410
  19.6 1.9 %collective-permute-start.3 = (f32[544,128]{1,0:T(8,128)S(1)}, f32[544,128]{1,0:T(8,128)S(1)}, u32[]{:S(2)}, u32[]{:S(2)}) collective-permute-start(f32[544,128]{1,0:T(8,128)S(1)} %get-tuple-element.53), channel_id=1, source_target_pairs={{0,1},{1,0},{2,3},{3,2},{4,5},{5,4},{6,7},{7,6},{8,9},{9,8},{10,11... | collective-permute-start | bytes 835592 | tf_op jit(solution)/shard_map/ppermute | solution.py:410
  21.5 1.7 %inside_rows.1 = (f32[16,72,256]{2,1,0:T(8,128)S(1)}, f32[16,8,256]{2,1,0:T(8,128)S(1)}, f32[16,32,256]{2,1,0:T(8,128)S(1)}, f32[16,32,256]{2,1,0:T(8,128)S(1)},...) custom-call(f32[16,72,128]{2,1,0:T(8,128)S(1)} %get-tuple-element.32, ...), custom_call_target="tpu_custom_call" | custom-call | flops 40000000 | bytes 8000000 | tf_op jit(solution)/shard_map/inside_rows/pallas_call | solution.py:447
  23.2 3.5 %collective-permute-done.2.refs_13_ = f32[544,128]{1,0:T(8,128)S(1)} collective-permute-done((f32[544,128]{1,0:T(8,128)S(1)}, f32[544,128]{1,0:T(8,128)S(1)}, u32[]{:S(2)}, u32[]{:S(2)}) %collective-permute-start.2) | collective-permute-done | bytes 278560 | tf_op jit(solution)/shard_map/ppermute | solution.py:410
  26.7 1.8 %first_rows.1 = (f32[96,128]{1,0:T(8,128)S(1)}, f32[8,128,128]{2,1,0:T(8,128)S(1)}, f32[8,128,128]{2,1,0:T(8,128)S(1)}, f32[8,32,128]{2,1,0:T(8,128)S(1)}) custom-call(f32[16,72,256]{2,1,0:T(8,128)S(1)} %get-tuple-element.35.own_wide, f32[16,8,256]{2,1,0:T(8,128)S(1)} %get-tuple-element.36.own_coefs, f32[16,32,256]{2,1,0:T(8,128)S(1)} %get-tuple-element.37.refs_0_, ...), custom_call_target="tpu_custom_call" | custom-call | flops 40000000 | bytes 8000000 | tf_op jit(solution)/shard_map/first_rows/pallas_call | solution.py:465
  28.6 1.5 %collective-permute-done.3.refs_14_ = f32[544,128]{1,0:T(8,128)S(1)} collective-permute-done((f32[544,128]{1,0:T(8,128)S(1)}, f32[544,128]{1,0:T(8,128)S(1)}, u32[]{:S(2)}, u32[]{:S(2)}) %collective-permute-start.3) | collective-permute-done | bytes 278560 | tf_op jit(solution)/shard_map/ppermute | solution.py:410
  30.1 1.9 %last_rows.1 = (f32[32,128]{1,0:T(8,128)S(1)}, f32[8,128,128]{2,1,0:T(8,128)S(1)}, f32[8,128,128]{2,1,0:T(8,128)S(1)}, f32[8,32,128]{2,1,0:T(8,128)S(1)}) custom-call(f32[16,72,256]{2,1,0:T(8,128)S(1)} %get-tuple-element.35.own_wide, f32[16,8,256]{2,1,0:T(8,128)S(1)} %get-tuple-element.36.own_coefs, f32[16,32,256]{2,1,0:T(8,128)S(1)} %get-tuple-element.37.refs_0_, ...), custom_call_target="tpu_custom_call" | custom-call | flops 40000000 | bytes 8000000 | tf_op jit(solution)/shard_map/last_rows/pallas_call | solution.py:471
  32.0 13.8 %all_to_all.15 = f32[8,32,128]{2,1,0:T(8,128)S(1)} all-to-all(f32[8,32,128]{2,1,0:T(8,128)S(1)} %broadcast_in_dim.6), channel_id=1, replica_groups=mesh['zh'=2,'x'=4,'c'=2,'zl'=4,'y'=8] {'x','c'}, dimensions={0} | all-to-all | bytes 262144 | tf_op jit(solution)/shard_map/sum_moments/all_to_all | solution.py:416
  45.8 11.5 %all_to_all.16 = f32[8,32,128]{2,1,0:T(8,128)S(1)} all-to-all(f32[8,32,128]{2,1,0:T(8,128)S(1)} %broadcast_in_dim.7), channel_id=1, replica_groups=mesh['zh'=2,'x'=4,'c'=2,'zl'=4,'y'=8] {'y'}, dimensions={0} | all-to-all | bytes 262144 | tf_op jit(solution)/shard_map/sum_moments/all_to_all | solution.py:416
  57.4 13.4 %all_to_all.17 = f32[8,32,128]{2,1,0:T(8,128)S(1)} all-to-all(f32[8,32,128]{2,1,0:T(8,128)S(1)} %broadcast_in_dim.8), channel_id=1, replica_groups=mesh['zh'=2,'x'=4,'c'=2,'zl'=4,'y'=8] {'zh','zl'}, dimensions={0} | all-to-all | bytes 262144 | tf_op jit(solution)/shard_map/sum_moments/all_to_all | solution.py:416
  70.9 4.3 %solve_and_combine.1 = (f32[32,16,128]{2,1,0:T(8,128)}, f32[32,16,128]{2,1,0:T(8,128)}, f32[16,128]{1,0:T(8,128)}) custom-call(f32[32,128]{1,0:T(8,128)S(1)} %reduce_sum.29.sums, f32[16,72,128]{2,1,0:T(8,128)S(1)} %get-tuple-element.32.own, f32[8,128,128]{2,1,0:T(8,128)S(1)} %get-tuple-element.55.basis_first, ...), custom_call_target="tpu_custom_call" | custom-call | tf_op jit(solution)/shard_map/solve_and_combine/pallas_call | solution.py:480
  (6 shorter events, 0.1 us)
Async XLA Ops:
  2.3 5.4 %collective-permute-start = (f32[72,128]{1,0:T(8,128)S(1)}, f32[72,128]{1,0:T(8,128)S(1)}, u32[]{:S(2)}, u32[]{:S(2)}) collective-permute-start(f32[72,128]{1,0:T(8,128)S(1)} %get-tuple-element.33), channel_id=1, source_target_pairs={{32,64},{64,32},{96,128},{128,96},{160,192},{192,160},{224,256},{2... | collective-permute-start | bytes 110600 | tf_op jit(solution)/shard_map/ppermute | solution.py:410
  4.2 4.4 %collective-permute-start.1 = (f32[72,128]{1,0:T(8,128)S(1)}, f32[72,128]{1,0:T(8,128)S(1)}, u32[]{:S(2)}, u32[]{:S(2)}) collective-permute-start(f32[72,128]{1,0:T(8,128)S(1)} %get-tuple-element.34), channel_id=1, source_target_pairs={{0,32},{32,0},{64,96},{96,64},{128,160},{160,128},{192,224},{224,1... | collective-permute-start | bytes 110600 | tf_op jit(solution)/shard_map/ppermute | solution.py:410
  8.7 18.0 %collective-permute-start.2 = (f32[544,128]{1,0:T(8,128)S(1)}, f32[544,128]{1,0:T(8,128)S(1)}, u32[]{:S(2)}, u32[]{:S(2)}) collective-permute-start(f32[544,128]{1,0:T(8,128)S(1)} %get-tuple-element.51), channel_id=1, source_target_pairs={{0,31},{1,2},{2,1},{3,4},{4,3},{5,6},{6,5},{7,8},{8,7},{9,10},{10,... | collective-permute-start | bytes 835592 | tf_op jit(solution)/shard_map/ppermute | solution.py:410
  19.6 10.5 %collective-permute-start.3 = (f32[544,128]{1,0:T(8,128)S(1)}, f32[544,128]{1,0:T(8,128)S(1)}, u32[]{:S(2)}, u32[]{:S(2)}) collective-permute-start(f32[544,128]{1,0:T(8,128)S(1)} %get-tuple-element.53), channel_id=1, source_target_pairs={{0,1},{1,0},{2,3},{3,2},{4,5},{5,4},{6,7},{7,6},{8,9},{9,8},{10,11... | collective-permute-start | bytes 835592 | tf_op jit(solution)/shard_map/ppermute | solution.py:410

commit v8 on v7

--- a/solution.py
+++ b/solution.py
@@ -33,16 +33,20 @@
     ]
     for copy in copies:
         copy.start()
-    for copy in copies:
+    warm, signs, mask, kappa, scale = scratch[:-1]
+    rows = [own.at[jnp.where(odd_lon == 0, p, ROWS - 1 - p)] for p in range(ROWS)]
+    copies[0].wait()
+    for p, row in enumerate(rows):
+        row[0:PROBES, :] = warm[:, p, :]
+    copies[1].wait()
+    for p, row in enumerate(rows):
+        row[PROBES : 2 * PROBES, :] = 2.0 * signs[:, p, :].astype(jnp.float32) - 1.0
+    for copy in copies[2:]:
         copy.wait()
-    warm, signs, mask, kappa, scale = scratch[:-1]
     wet = mask[...].astype(jnp.float32)
     diag = kappa[...] + 4.0
     scaled = scale[...]
-    for p in range(ROWS):
-        row = own.at[jnp.where(odd_lon == 0, p, ROWS - 1 - p)]
-        row[0:PROBES, :] = warm[:, p, :]
-        row[PROBES : 2 * PROBES, :] = 2.0 * signs[:, p, :].astype(jnp.float32) - 1.0
+    for p, row in enumerate(rows):
         row[2 * PROBES :, :] = jnp.concatenate(
             [wet[p : p + 1], diag[p : p + 1], scaled[p : p + 1], jnp.zeros((5, LANES), jnp.float32)], axis=0
         )
@@ -194,11 +198,14 @@
             return range(0)
         return range(INSIDE[name][1], NEEDED[name][1]) if behind else range(NEEDED[name][0], INSIDE[name][0])
 
-    def get(name, r):
-        return fresh[name][r - base] if r in rows(name) else held[name][r - DEPTH]
+    def get(name, r, lanes=2 * LANES):
+        return fresh[name][r - base, :, 0:lanes] if r in rows(name) else held[name][r - DEPTH, :, 0:lanes]
 
     def put(name, r, value):
-        fresh[name][r - base] = value
+        if name in ("p3", "up"):
+            fresh[name][r - base, :, 0:LANES] = value[:, 0:LANES]
+        else:
+            fresh[name][r - base] = value
 
     def coef(r, n):
         return own_coefs[r - DEPTH, n : n + 1, :] if own(r) else coefs[halo(r), n : n + 1, :]
@@ -213,9 +220,9 @@
         r = DEPTH + i + (HALF if behind else 0)
         for k in range(4):
             at = slice(k * PROBES, (k + 1) * PROBES)
-            basis[i, at, :] = get(f"p{k}", r)[:, 0:LANES]
-            images[i, at, :] = get(f"i{(k + 1) % 4}", r)[:, 0:LANES]
-        probe_image[i] = get("up", r)[:, 0:LANES]
+            basis[i, at, :] = get(f"p{k}", r, LANES)
+            images[i, at, :] = get(f"i{(k + 1) % 4}", r, LANES)
+        probe_image[i] = get("up", r, LANES)
         if i % 2 == 0:
             continue
         block = jnp.concatenate([basis[i - 1], basis[i]], axis=1)
@@ -499,7 +506,7 @@
     if mesh.devices.shape == (16, 32):
         grid = Mesh(mesh.devices.reshape(2, 4, 2, 4, 8), ("zh", "x", "c", "zl", "y"))
         lat, lon = (("zh", "x", "c"), ("zl", "y"))
-        stages = (("x", "c"), ("y",), ("zh", "zl"))
+        stages = (("x", "c"), ("zh", "zl"), ("y",))
     else:
         grid, lat, lon, stages = (mesh, ("lat",), ("lon",), (("lat",), ("lon",)))
     return jax.shard_map(

time: 75.5 us -> 75.4 us (level)
  no operation moved by 1% of the time
where the time goes in v8:
time: 75.4 us; the launch traced here: 75.1 us
  blocking collectives  38.8 us (51%)
  starting transfers between devices  18.1 us (24%)
  Pallas kernels  11.5 us (15%)
  waiting for transfers between devices  5.91 us (8%)
    all_to_all x3, blocking collectives, spread_sum(): return jnp.sum(lax.all_to_all(copies, axes, 0, 0), axis=0)  38.8 us
    ppermute x4, starting transfers between devices, exchanged(): return lax.ppermute(value, axes, pairs)  18.1 us
    ppermute x4, waiting for transfers between devices, exchanged(): return lax.ppermute(value, axes, pairs)  5.91 us
    pallas_call x1, Pallas kernels, local(): pl.pallas_call(functools.partial(finish_kernel, axes), out_shape=(f32(PRO...  4.28 us
    pallas_call x1, Pallas kernels, local(): pl.pallas_call(functools.partial(half_kernel, True), out_shape=(f32(PROBE...  1.89 us
    pallas_call x1, Pallas kernels, local(): pl.pallas_call(functools.partial(half_kernel, False), out_shape=(f32(3 *...  1.82 us
    pallas_call x1, Pallas kernels, local(): pl.pallas_call(functools.partial(pack_kernel, axes), out_shape=(f32(ROWS,...  1.71 us
    pallas_call x1, Pallas kernels, local(): pl.pallas_call(functools.partial(inside_kernel, axes), out_shape=(f32(ROW...  1.68 us
  transfers between devices with their start and end apart: 4, of which 3 were waited for; matrix products, arithmetic and copies ran while one was open for 0% of the time, Pallas kernels for 5%

profile of v8, /device:TPU:2, one launch (start us, length us, event | category | flops | bytes accessed | tf_op | source)
XLA Modules:
  0.0 75.1 jit_solution(2792031786511028937)
XLA Ops:
  0.6 1.7 %pack_edges.1 = (f32[16,72,128]{2,1,0:T(8,128)S(1)}, f32[3,16,128]{2,1,0:T(8,128)S(1)}, f32[72,128]{1,0:T(8,128)S(1)}, f32[72,128]{1,0:T(8,128)S(1)}) custom-call(f32[32,16,128]{2,1,0:T(8,128)} %warm_hbm.1, s32[32,16,128]{2,1,0:T(8,128)} %signs_hbm.1, s32[16,128]{1,0:T(8,128)} %mask_hbm.1, f32[16,128]{1,0:T(8,128)} %kappa_hbm.1, f32[16,128]{1,0:T(8,128)} %scale_hbm.1), custom_call_target="tpu_custom_call" | custom-call | tf_op jit(solution)/shard_map/pack_edges/pallas_call | solution.py:431
  2.4 1.9 %collective-permute-start = (f32[72,128]{1,0:T(8,128)S(1)}, f32[72,128]{1,0:T(8,128)S(1)}, u32[]{:S(2)}, u32[]{:S(2)}) collective-permute-start(f32[72,128]{1,0:T(8,128)S(1)} %get-tuple-element.33), channel_id=1, source_target_pairs={{32,64},{64,32},{96,128},{128,96},{160,192},{192,160},{224,256},{2... | collective-permute-start | bytes 110600 | tf_op jit(solution)/shard_map/ppermute | solution.py:417
  4.3 3.5 %collective-permute-start.1 = (f32[72,128]{1,0:T(8,128)S(1)}, f32[72,128]{1,0:T(8,128)S(1)}, u32[]{:S(2)}, u32[]{:S(2)}) collective-permute-start(f32[72,128]{1,0:T(8,128)S(1)} %get-tuple-element.34), channel_id=1, source_target_pairs={{0,32},{32,0},{64,96},{96,64},{128,160},{160,128},{192,224},{224,1... | collective-permute-start | bytes 110600 | tf_op jit(solution)/shard_map/ppermute | solution.py:417
  7.8 0.0 collective-permute-done.from_odd
  7.8 0.8 %collective-permute-done.1.from_even = f32[72,128]{1,0:T(8,128)S(1)} collective-permute-done((f32[72,128]{1,0:T(8,128)S(1)}, f32[72,128]{1,0:T(8,128)S(1)}, u32[]{:S(2)}, u32[]{:S(2)}) %collective-permute-start.1) | collective-permute-done | bytes 36896 | tf_op jit(solution)/shard_map/ppermute | solution.py:417
  8.6 0.1 pack_rows.1
  8.7 10.8 %collective-permute-start.2 = (f32[544,128]{1,0:T(8,128)S(1)}, f32[544,128]{1,0:T(8,128)S(1)}, u32[]{:S(2)}, u32[]{:S(2)}) collective-permute-start(f32[544,128]{1,0:T(8,128)S(1)} %get-tuple-element.51), channel_id=1, source_target_pairs={{0,31},{1,2},{2,1},{3,4},{4,3},{5,6},{6,5},{7,8},{8,7},{9,10},{10,... | collective-permute-start | bytes 835592 | tf_op jit(solution)/shard_map/ppermute | solution.py:417
  19.6 1.9 %collective-permute-start.3 = (f32[544,128]{1,0:T(8,128)S(1)}, f32[544,128]{1,0:T(8,128)S(1)}, u32[]{:S(2)}, u32[]{:S(2)}) collective-permute-start(f32[544,128]{1,0:T(8,128)S(1)} %get-tuple-element.53), channel_id=1, source_target_pairs={{0,1},{1,0},{2,3},{3,2},{4,5},{5,4},{6,7},{7,6},{8,9},{9,8},{10,11... | collective-permute-start | bytes 835592 | tf_op jit(solution)/shard_map/ppermute | solution.py:417
  21.5 1.7 %inside_rows.1 = (f32[16,72,256]{2,1,0:T(8,128)S(1)}, f32[16,8,256]{2,1,0:T(8,128)S(1)}, f32[16,32,256]{2,1,0:T(8,128)S(1)}, f32[16,32,256]{2,1,0:T(8,128)S(1)},...) custom-call(f32[16,72,128]{2,1,0:T(8,128)S(1)} %get-tuple-element.32, ...), custom_call_target="tpu_custom_call" | custom-call | flops 40000000 | bytes 8000000 | tf_op jit(solution)/shard_map/inside_rows/pallas_call | solution.py:454
  23.2 3.5 %collective-permute-done.2.refs_13_ = f32[544,128]{1,0:T(8,128)S(1)} collective-permute-done((f32[544,128]{1,0:T(8,128)S(1)}, f32[544,128]{1,0:T(8,128)S(1)}, u32[]{:S(2)}, u32[]{:S(2)}) %collective-permute-start.2) | collective-permute-done | bytes 278560 | tf_op jit(solution)/shard_map/ppermute | solution.py:417
  26.7 1.8 %first_rows.1 = (f32[96,128]{1,0:T(8,128)S(1)}, f32[8,128,128]{2,1,0:T(8,128)S(1)}, f32[8,128,128]{2,1,0:T(8,128)S(1)}, f32[8,32,128]{2,1,0:T(8,128)S(1)}) custom-call(f32[16,72,256]{2,1,0:T(8,128)S(1)} %get-tuple-element.35.own_wide, f32[16,8,256]{2,1,0:T(8,128)S(1)} %get-tuple-element.36.own_coefs, f32[16,32,256]{2,1,0:T(8,128)S(1)} %get-tuple-element.37.refs_0_, ...), custom_call_target="tpu_custom_call" | custom-call | flops 40000000 | bytes 8000000 | tf_op jit(solution)/shard_map/first_rows/pallas_call | solution.py:472
  28.5 1.5 %collective-permute-done.3.refs_14_ = f32[544,128]{1,0:T(8,128)S(1)} collective-permute-done((f32[544,128]{1,0:T(8,128)S(1)}, f32[544,128]{1,0:T(8,128)S(1)}, u32[]{:S(2)}, u32[]{:S(2)}) %collective-permute-start.3) | collective-permute-done | bytes 278560 | tf_op jit(solution)/shard_map/ppermute | solution.py:417
  30.1 1.9 %last_rows.1 = (f32[32,128]{1,0:T(8,128)S(1)}, f32[8,128,128]{2,1,0:T(8,128)S(1)}, f32[8,128,128]{2,1,0:T(8,128)S(1)}, f32[8,32,128]{2,1,0:T(8,128)S(1)}) custom-call(f32[16,72,256]{2,1,0:T(8,128)S(1)} %get-tuple-element.35.own_wide, f32[16,8,256]{2,1,0:T(8,128)S(1)} %get-tuple-element.36.own_coefs, f32[16,32,256]{2,1,0:T(8,128)S(1)} %get-tuple-element.37.refs_0_, ...), custom_call_target="tpu_custom_call" | custom-call | flops 40000000 | bytes 8000000 | tf_op jit(solution)/shard_map/last_rows/pallas_call | solution.py:478
  32.0 13.8 %all_to_all.15 = f32[8,32,128]{2,1,0:T(8,128)S(1)} all-to-all(f32[8,32,128]{2,1,0:T(8,128)S(1)} %broadcast_in_dim.6), channel_id=1, replica_groups=mesh['zh'=2,'x'=4,'c'=2,'zl'=4,'y'=8] {'x','c'}, dimensions={0} | all-to-all | bytes 262144 | tf_op jit(solution)/shard_map/sum_moments/all_to_all | solution.py:423
  45.8 13.2 %all_to_all.16 = f32[8,32,128]{2,1,0:T(8,128)S(1)} all-to-all(f32[8,32,128]{2,1,0:T(8,128)S(1)} %broadcast_in_dim.7), channel_id=1, replica_groups=mesh['zh'=2,'x'=4,'c'=2,'zl'=4,'y'=8] {'zh','zl'}, dimensions={0} | all-to-all | bytes 262144 | tf_op jit(solution)/shard_map/sum_moments/all_to_all | solution.py:423
  59.1 11.8 %all_to_all.17 = f32[8,32,128]{2,1,0:T(8,128)S(1)} all-to-all(f32[8,32,128]{2,1,0:T(8,128)S(1)} %broadcast_in_dim.8), channel_id=1, replica_groups=mesh['zh'=2,'x'=4,'c'=2,'zl'=4,'y'=8] {'y'}, dimensions={0} | all-to-all | bytes 262144 | tf_op jit(solution)/shard_map/sum_moments/all_to_all | solution.py:423
  70.8 4.3 %solve_and_combine.1 = (f32[32,16,128]{2,1,0:T(8,128)}, f32[32,16,128]{2,1,0:T(8,128)}, f32[16,128]{1,0:T(8,128)}) custom-call(f32[32,128]{1,0:T(8,128)S(1)} %reduce_sum.29.sums, f32[16,72,128]{2,1,0:T(8,128)S(1)} %get-tuple-element.32.own, f32[8,128,128]{2,1,0:T(8,128)S(1)} %get-tuple-element.55.basis_first, ...), custom_call_target="tpu_custom_call" | custom-call | tf_op jit(solution)/shard_map/solve_and_combine/pallas_call | solution.py:487
  (6 shorter events, 0.1 us)
Async XLA Ops:
  2.4 5.4 %collective-permute-start = (f32[72,128]{1,0:T(8,128)S(1)}, f32[72,128]{1,0:T(8,128)S(1)}, u32[]{:S(2)}, u32[]{:S(2)}) collective-permute-start(f32[72,128]{1,0:T(8,128)S(1)} %get-tuple-element.33), channel_id=1, source_target_pairs={{32,64},{64,32},{96,128},{128,96},{160,192},{192,160},{224,256},{2... | collective-permute-start | bytes 110600 | tf_op jit(solution)/shard_map/ppermute | solution.py:417
  4.3 4.4 %collective-permute-start.1 = (f32[72,128]{1,0:T(8,128)S(1)}, f32[72,128]{1,0:T(8,128)S(1)}, u32[]{:S(2)}, u32[]{:S(2)}) collective-permute-start(f32[72,128]{1,0:T(8,128)S(1)} %get-tuple-element.34), channel_id=1, source_target_pairs={{0,32},{32,0},{64,96},{96,64},{128,160},{160,128},{192,224},{224,1... | collective-permute-start | bytes 110600 | tf_op jit(solution)/shard_map/ppermute | solution.py:417
  8.7 18.0 %collective-permute-start.2 = (f32[544,128]{1,0:T(8,128)S(1)}, f32[544,128]{1,0:T(8,128)S(1)}, u32[]{:S(2)}, u32[]{:S(2)}) collective-permute-start(f32[544,128]{1,0:T(8,128)S(1)} %get-tuple-element.51), channel_id=1, source_target_pairs={{0,31},{1,2},{2,1},{3,4},{4,3},{5,6},{6,5},{7,8},{8,7},{9,10},{10,... | collective-permute-start | bytes 835592 | tf_op jit(solution)/shard_map/ppermute | solution.py:417
  19.6 10.5 %collective-permute-start.3 = (f32[544,128]{1,0:T(8,128)S(1)}, f32[544,128]{1,0:T(8,128)S(1)}, u32[]{:S(2)}, u32[]{:S(2)}) collective-permute-start(f32[544,128]{1,0:T(8,128)S(1)} %get-tuple-element.53), channel_id=1, source_target_pairs={{0,1},{1,0},{2,3},{3,2},{4,5},{5,4},{6,7},{7,6},{8,9},{9,8},{10,11... | collective-permute-start | bytes 835592 | tf_op jit(solution)/shard_map/ppermute | solution.py:417

commit v9 on v8

--- a/solution.py
+++ b/solution.py
@@ -322,7 +322,7 @@
     axes,
     sums, own, basis_first, basis_last, images_first, images_last, probe_first, probe_last,
     solution_out, residual_out, grad_out,
-    coeffs, rows,
+    coeffs,
 ):
     _, odd_lon = parities(axes)
     packed = sums[...]
@@ -393,14 +393,10 @@
             values = both[0:PROBES, lanes] + own[i + n, 0:PROBES, :]
             terms = values * probe_image[j + n] + image[:, lanes] * own[i + n, PROBES : 2 * PROBES, :]
             wet = own[i + n, 64:65, :]
-            out = rows.at[jnp.where(odd_lon == 0, i + n, ROWS - 1 - i - n)]
-            out[0:PROBES, :] = values
-            out[PROBES : 2 * PROBES, :] = both[PROBES:, lanes]
-            out[2 * PROBES : 2 * PROBES + 1, :] = wet * (jnp.sum(terms, axis=0, keepdims=True) * (1.0 / PROBES))
-    for p in range(ROWS):
-        solution_out[:, p, :] = rows[p, 0:PROBES, :]
-        residual_out[:, p, :] = rows[p, PROBES : 2 * PROBES, :]
-        grad_out[p : p + 1, :] = rows[p, 2 * PROBES : 2 * PROBES + 1, :]
+            place = jnp.where(odd_lon == 0, i + n, ROWS - 1 - i - n)
+            solution_out[:, pl.ds(place, 1), :] = values.reshape(PROBES, 1, LANES)
+            residual_out[:, pl.ds(place, 1), :] = both[PROBES:, lanes].reshape(PROBES, 1, LANES)
+            grad_out[pl.ds(place, 1), :] = wet * (jnp.sum(terms, axis=0, keepdims=True) * (1.0 / PROBES))
 
 
 def f32(*shape):
@@ -493,7 +489,6 @@
             ),
             scratch_shapes=[
                 pltpu.VMEM((3 * PROBES, 4 * PROBES), jnp.float32),
-                pltpu.VMEM((ROWS, FIELDS, LANES), jnp.float32),
             ],
             compiler_params=PARAMS,
             name="solve_and_combine",

time: 75.4 us -> 75.4 us (level)
  no operation moved by 1% of the time
where the time goes in v9:
time: 75.4 us; the launch traced here: 75.1 us
  blocking collectives  38.8 us (51%)
  starting transfers between devices  18.1 us (24%)
  Pallas kernels  11.5 us (15%)
  waiting for transfers between devices  5.91 us (8%)
    all_to_all x3, blocking collectives, spread_sum(): return jnp.sum(lax.all_to_all(copies, axes, 0, 0), axis=0)  38.8 us
    ppermute x4, starting transfers between devices, exchanged(): return lax.ppermute(value, axes, pairs)  18.1 us
    ppermute x4, waiting for transfers between devices, exchanged(): return lax.ppermute(value, axes, pairs)  5.91 us
    pallas_call x1, Pallas kernels, local(): pl.pallas_call(functools.partial(finish_kernel, axes), out_shape=(f32(PRO...  4.24 us
    pallas_call x1, Pallas kernels, local(): pl.pallas_call(functools.partial(half_kernel, True), out_shape=(f32(PROBE...  1.89 us
    pallas_call x1, Pallas kernels, local(): pl.pallas_call(functools.partial(half_kernel, False), out_shape=(f32(3 *...  1.82 us
    pallas_call x1, Pallas kernels, local(): pl.pallas_call(functools.partial(pack_kernel, axes), out_shape=(f32(ROWS,...  1.71 us
    pallas_call x1, Pallas kernels, local(): pl.pallas_call(functools.partial(inside_kernel, axes), out_shape=(f32(ROW...  1.68 us
  transfers between devices with their start and end apart: 4, of which 3 were waited for; matrix products, arithmetic and copies ran while one was open for 0% of the time, Pallas kernels for 5%

profile of v9, /device:TPU:2, one launch (start us, length us, event | category | flops | bytes accessed | tf_op | source)
XLA Modules:
  0.0 75.1 jit_solution(15479784031979081729)
XLA Ops:
  0.6 1.7 %pack_edges.1 = (f32[16,72,128]{2,1,0:T(8,128)S(1)}, f32[3,16,128]{2,1,0:T(8,128)S(1)}, f32[72,128]{1,0:T(8,128)S(1)}, f32[72,128]{1,0:T(8,128)S(1)}) custom-call(f32[32,16,128]{2,1,0:T(8,128)} %warm_hbm.1, s32[32,16,128]{2,1,0:T(8,128)} %signs_hbm.1, s32[16,128]{1,0:T(8,128)} %mask_hbm.1, f32[16,128]{1,0:T(8,128)} %kappa_hbm.1, f32[16,128]{1,0:T(8,128)} %scale_hbm.1), custom_call_target="tpu_custom_call" | custom-call | tf_op jit(solution)/shard_map/pack_edges/pallas_call | solution.py:427
  2.4 1.9 %collective-permute-start = (f32[72,128]{1,0:T(8,128)S(1)}, f32[72,128]{1,0:T(8,128)S(1)}, u32[]{:S(2)}, u32[]{:S(2)}) collective-permute-start(f32[72,128]{1,0:T(8,128)S(1)} %get-tuple-element.33), channel_id=1, source_target_pairs={{32,64},{64,32},{96,128},{128,96},{160,192},{192,160},{224,256},{2... | collective-permute-start | bytes 110600 | tf_op jit(solution)/shard_map/ppermute | solution.py:413
  4.3 3.5 %collective-permute-start.1 = (f32[72,128]{1,0:T(8,128)S(1)}, f32[72,128]{1,0:T(8,128)S(1)}, u32[]{:S(2)}, u32[]{:S(2)}) collective-permute-start(f32[72,128]{1,0:T(8,128)S(1)} %get-tuple-element.34), channel_id=1, source_target_pairs={{0,32},{32,0},{64,96},{96,64},{128,160},{160,128},{192,224},{224,1... | collective-permute-start | bytes 110600 | tf_op jit(solution)/shard_map/ppermute | solution.py:413
  7.8 0.0 collective-permute-done.from_odd
  7.8 0.8 %collective-permute-done.1.from_even = f32[72,128]{1,0:T(8,128)S(1)} collective-permute-done((f32[72,128]{1,0:T(8,128)S(1)}, f32[72,128]{1,0:T(8,128)S(1)}, u32[]{:S(2)}, u32[]{:S(2)}) %collective-permute-start.1) | collective-permute-done | bytes 36896 | tf_op jit(solution)/shard_map/ppermute | solution.py:413
  8.6 0.1 pack_rows.1
  8.7 10.8 %collective-permute-start.2 = (f32[544,128]{1,0:T(8,128)S(1)}, f32[544,128]{1,0:T(8,128)S(1)}, u32[]{:S(2)}, u32[]{:S(2)}) collective-permute-start(f32[544,128]{1,0:T(8,128)S(1)} %get-tuple-element.51), channel_id=1, source_target_pairs={{0,31},{1,2},{2,1},{3,4},{4,3},{5,6},{6,5},{7,8},{8,7},{9,10},{10,... | collective-permute-start | bytes 835592 | tf_op jit(solution)/shard_map/ppermute | solution.py:413
  19.6 1.9 %collective-permute-start.3 = (f32[544,128]{1,0:T(8,128)S(1)}, f32[544,128]{1,0:T(8,128)S(1)}, u32[]{:S(2)}, u32[]{:S(2)}) collective-permute-start(f32[544,128]{1,0:T(8,128)S(1)} %get-tuple-element.53), channel_id=1, source_target_pairs={{0,1},{1,0},{2,3},{3,2},{4,5},{5,4},{6,7},{7,6},{8,9},{9,8},{10,11... | collective-permute-start | bytes 835592 | tf_op jit(solution)/shard_map/ppermute | solution.py:413
  21.5 1.7 %inside_rows.1 = (f32[16,72,256]{2,1,0:T(8,128)S(1)}, f32[16,8,256]{2,1,0:T(8,128)S(1)}, f32[16,32,256]{2,1,0:T(8,128)S(1)}, f32[16,32,256]{2,1,0:T(8,128)S(1)},...) custom-call(f32[16,72,128]{2,1,0:T(8,128)S(1)} %get-tuple-element.32, ...), custom_call_target="tpu_custom_call" | custom-call | flops 40000000 | bytes 8000000 | tf_op jit(solution)/shard_map/inside_rows/pallas_call | solution.py:450
  23.2 3.5 %collective-permute-done.2.refs_13_ = f32[544,128]{1,0:T(8,128)S(1)} collective-permute-done((f32[544,128]{1,0:T(8,128)S(1)}, f32[544,128]{1,0:T(8,128)S(1)}, u32[]{:S(2)}, u32[]{:S(2)}) %collective-permute-start.2) | collective-permute-done | bytes 278560 | tf_op jit(solution)/shard_map/ppermute | solution.py:413
  26.7 1.8 %first_rows.1 = (f32[96,128]{1,0:T(8,128)S(1)}, f32[8,128,128]{2,1,0:T(8,128)S(1)}, f32[8,128,128]{2,1,0:T(8,128)S(1)}, f32[8,32,128]{2,1,0:T(8,128)S(1)}) custom-call(f32[16,72,256]{2,1,0:T(8,128)S(1)} %get-tuple-element.35.own_wide, f32[16,8,256]{2,1,0:T(8,128)S(1)} %get-tuple-element.36.own_coefs, f32[16,32,256]{2,1,0:T(8,128)S(1)} %get-tuple-element.37.refs_0_, ...), custom_call_target="tpu_custom_call" | custom-call | flops 40000000 | bytes 8000000 | tf_op jit(solution)/shard_map/first_rows/pallas_call | solution.py:468
  28.5 1.5 %collective-permute-done.3.refs_14_ = f32[544,128]{1,0:T(8,128)S(1)} collective-permute-done((f32[544,128]{1,0:T(8,128)S(1)}, f32[544,128]{1,0:T(8,128)S(1)}, u32[]{:S(2)}, u32[]{:S(2)}) %collective-permute-start.3) | collective-permute-done | bytes 278560 | tf_op jit(solution)/shard_map/ppermute | solution.py:413
  30.1 1.9 %last_rows.1 = (f32[32,128]{1,0:T(8,128)S(1)}, f32[8,128,128]{2,1,0:T(8,128)S(1)}, f32[8,128,128]{2,1,0:T(8,128)S(1)}, f32[8,32,128]{2,1,0:T(8,128)S(1)}) custom-call(f32[16,72,256]{2,1,0:T(8,128)S(1)} %get-tuple-element.35.own_wide, f32[16,8,256]{2,1,0:T(8,128)S(1)} %get-tuple-element.36.own_coefs, f32[16,32,256]{2,1,0:T(8,128)S(1)} %get-tuple-element.37.refs_0_, ...), custom_call_target="tpu_custom_call" | custom-call | flops 40000000 | bytes 8000000 | tf_op jit(solution)/shard_map/last_rows/pallas_call | solution.py:474
  32.0 13.8 %all_to_all.15 = f32[8,32,128]{2,1,0:T(8,128)S(1)} all-to-all(f32[8,32,128]{2,1,0:T(8,128)S(1)} %broadcast_in_dim.6), channel_id=1, replica_groups=mesh['zh'=2,'x'=4,'c'=2,'zl'=4,'y'=8] {'x','c'}, dimensions={0} | all-to-all | bytes 262144 | tf_op jit(solution)/shard_map/sum_moments/all_to_all | solution.py:419
  45.8 13.2 %all_to_all.16 = f32[8,32,128]{2,1,0:T(8,128)S(1)} all-to-all(f32[8,32,128]{2,1,0:T(8,128)S(1)} %broadcast_in_dim.7), channel_id=1, replica_groups=mesh['zh'=2,'x'=4,'c'=2,'zl'=4,'y'=8] {'zh','zl'}, dimensions={0} | all-to-all | bytes 262144 | tf_op jit(solution)/shard_map/sum_moments/all_to_all | solution.py:419
  59.1 11.8 %all_to_all.17 = f32[8,32,128]{2,1,0:T(8,128)S(1)} all-to-all(f32[8,32,128]{2,1,0:T(8,128)S(1)} %broadcast_in_dim.8), channel_id=1, replica_groups=mesh['zh'=2,'x'=4,'c'=2,'zl'=4,'y'=8] {'y'}, dimensions={0} | all-to-all | bytes 262144 | tf_op jit(solution)/shard_map/sum_moments/all_to_all | solution.py:419
  70.8 4.2 %solve_and_combine.1 = (f32[32,16,128]{2,1,0:T(8,128)}, f32[32,16,128]{2,1,0:T(8,128)}, f32[16,128]{1,0:T(8,128)}) custom-call(f32[32,128]{1,0:T(8,128)S(1)} %reduce_sum.29.sums, f32[16,72,128]{2,1,0:T(8,128)S(1)} %get-tuple-element.32.own, f32[8,128,128]{2,1,0:T(8,128)S(1)} %get-tuple-element.55.basis_first, ...), custom_call_target="tpu_custom_call" | custom-call | tf_op jit(solution)/shard_map/solve_and_combine/pallas_call | solution.py:483
  (6 shorter events, 0.1 us)
Async XLA Ops:
  2.4 5.4 %collective-permute-start = (f32[72,128]{1,0:T(8,128)S(1)}, f32[72,128]{1,0:T(8,128)S(1)}, u32[]{:S(2)}, u32[]{:S(2)}) collective-permute-start(f32[72,128]{1,0:T(8,128)S(1)} %get-tuple-element.33), channel_id=1, source_target_pairs={{32,64},{64,32},{96,128},{128,96},{160,192},{192,160},{224,256},{2... | collective-permute-start | bytes 110600 | tf_op jit(solution)/shard_map/ppermute | solution.py:413
  4.3 4.4 %collective-permute-start.1 = (f32[72,128]{1,0:T(8,128)S(1)}, f32[72,128]{1,0:T(8,128)S(1)}, u32[]{:S(2)}, u32[]{:S(2)}) collective-permute-start(f32[72,128]{1,0:T(8,128)S(1)} %get-tuple-element.34), channel_id=1, source_target_pairs={{0,32},{32,0},{64,96},{96,64},{128,160},{160,128},{192,224},{224,1... | collective-permute-start | bytes 110600 | tf_op jit(solution)/shard_map/ppermute | solution.py:413
  8.7 18.0 %collective-permute-start.2 = (f32[544,128]{1,0:T(8,128)S(1)}, f32[544,128]{1,0:T(8,128)S(1)}, u32[]{:S(2)}, u32[]{:S(2)}) collective-permute-start(f32[544,128]{1,0:T(8,128)S(1)} %get-tuple-element.51), channel_id=1, source_target_pairs={{0,31},{1,2},{2,1},{3,4},{4,3},{5,6},{6,5},{7,8},{8,7},{9,10},{10,... | collective-permute-start | bytes 835592 | tf_op jit(solution)/shard_map/ppermute | solution.py:413
  19.6 10.5 %collective-permute-start.3 = (f32[544,128]{1,0:T(8,128)S(1)}, f32[544,128]{1,0:T(8,128)S(1)}, u32[]{:S(2)}, u32[]{:S(2)}) collective-permute-start(f32[544,128]{1,0:T(8,128)S(1)} %get-tuple-element.53), channel_id=1, source_target_pairs={{0,1},{1,0},{2,3},{3,2},{4,5},{5,4},{6,7},{7,6},{8,9},{9,8},{10,11... | collective-permute-start | bytes 835592 | tf_op jit(solution)/shard_map/ppermute | solution.py:413
